TPU v7x, 32 devices: a whole 2x2x4 slice. The times are simulated.
32 devices in a mesh: nodes: 8 (over z, x), heads: 4 (over y, core).
Axes of the slice: x: 2, y: 2, z: 4, core: 2. Of those that a mesh axis runs over, the one named last changes fastest.
Arguments:
- tokens: bfloat16 [8192, 512], P(('nodes', 'heads')), may hold values from -6 to 6
- w_qkv: bfloat16 [512, 1536], replicated, may hold values from -0.25 to 0.25
- w_out: bfloat16 [512, 512], replicated, may hold values from -0.5 to 0.5
- w_up: bfloat16 [512, 1024], replicated, may hold values from -0.25 to 0.25
- w_down: bfloat16 [1024, 512], replicated, may hold values from -0.1875 to 0.1875
- tile_cols: int32 [64, 8], P('nodes'), may hold values from 0 to 67, as said below
- tile_mask: int32 [64, 8, 128, 128], P('nodes'), may hold values from 0 to 1, as said below
- hub_blocks: int32 [4], replicated, may hold values from 0 to 63, as said below
Outputs:
- layer_out: bfloat16 [8192, 512], P(('nodes', 'heads'))
Inputs may be any that keep to these rules, and one draw needn't show every extreme that they name: `tile_cols`: row block b belongs to node group b // 8. Tile 0 of b is b itself; tile 1 lies in the group before (cyclically over 8 groups), tile 2 in the group after, tile 3 is a hub slot; every other entry lies in those three groups or is a hub slot. Padding tiles have column b. `tile_mask`: the diagonal of tile 0 is all ones; tiles 0 to 3 are never padding, and padding tiles are all zero. `hub_blocks`: distinct blocks; the first and the last block are always among them.
All inputs are finite; a program needn't handle non-finite values.
Results may differ from a plain program's by a relative error of at most 0.0055.
Values may be sent and summed in bfloat16 or wider, within the bound.
No kernel may reach another device: no remote copies, remote signals or barrier semaphores. Data moves between devices by JAX's collectives and lax.ppermute only.
A program may use at most 64 MiB of HBM per device.

v0:
```python
import jax
import jax.numpy as jnp
from jax import lax
from jax.sharding import PartitionSpec as P

TB = 128


def padded(block, sides, width):
    for axis, dim in sides:
        count = lax.axis_size(axis)
        forward = [(i, i + 1) for i in range(count - 1)]
        forward.append((count - 1, 0))
        backward = [(target, source) for source, target in forward]
        low = lax.ppermute(
            lax.slice_in_dim(block, block.shape[dim] - width, None, axis=dim), axis, forward
        )
        high = lax.ppermute(lax.slice_in_dim(block, 0, width, axis=dim), axis, backward)
        block = jnp.concatenate([low, block, high], axis=dim)
    return block


def broadcast(value, axis, source):
    kept = jnp.where(lax.axis_index(axis) == source, value, 0).astype(value.dtype)
    return lax.psum(kept, axis)


def layer_norm(value_rows):
    mean = jnp.mean(value_rows, axis=-1, keepdims=True)
    centered = value_rows - mean
    spread = jnp.mean(centered * centered, axis=-1, keepdims=True)
    return centered * lax.rsqrt(spread + 1e-05)


def body(tokens, w_qkv, w_out, w_up, w_down, tile_cols, tile_mask, hub_blocks):
    node_dev, width = tokens.shape
    head_count = lax.axis_size("heads")
    head_dim = width // head_count
    scale = 1.0 / head_dim**0.5
    per_group = tile_cols.shape[0]
    hub_count = hub_blocks.shape[0]
    features = tokens.astype(jnp.float32)
    normed = layer_norm(features).astype(jnp.bfloat16)
    head_here = lax.axis_index("heads")
    w_head = lax.dynamic_slice_in_dim(w_qkv, head_here * 3 * head_dim, 3 * head_dim, 1)
    mine = jnp.dot(
        lax.all_gather(normed, "heads", axis=0, tiled=True),
        w_head,
        preferred_element_type=jnp.float32,
    ).astype(jnp.bfloat16)
    queries = mine[:, :head_dim]
    keyval = mine[:, head_dim:]
    group_rows = keyval.shape[0]
    nearby = padded(keyval, (("nodes", 0),), group_rows)
    here = lax.axis_index("nodes")
    groups = lax.axis_size("nodes")
    blocks_all = per_group * groups
    pieces = []
    for slot in range(hub_count):
        block = hub_blocks[slot]
        local = lax.dynamic_slice_in_dim(keyval, block % per_group * TB, TB, 0)
        pieces.append(broadcast(local, "nodes", block // per_group))
    hub_rows = jnp.concatenate(pieces, axis=0)
    pool = jnp.concatenate([nearby, hub_rows], axis=0).reshape(-1, TB, 2 * head_dim)
    is_hub = tile_cols >= blocks_all
    hub_slot = jnp.clip(tile_cols - blocks_all, 0, hub_count - 1)
    col_group = tile_cols // per_group
    col_block = tile_cols % per_group
    offset = (col_group - here) % groups
    pool_index = jnp.where(
        is_hub,
        3 * per_group + hub_slot,
        jnp.where(
            offset == groups - 1,
            col_block,
            jnp.where(offset == 0, per_group + col_block, 2 * per_group + col_block),
        ),
    )
    tiles = pool[pool_index]
    key_rows = tiles[..., :head_dim]
    value_rows = tiles[..., head_dim:]
    query_block_rows = queries.reshape(per_group, TB, head_dim)
    score_matrix = jnp.einsum(
        "lou,lwgu->lwog", query_block_rows, key_rows, preferred_element_type=jnp.float32
    )
    weight = jnp.exp(score_matrix * scale) * tile_mask.astype(jnp.float32)
    total = jnp.sum(weight, axis=(1, 3))
    rounded_state = weight.astype(jnp.bfloat16)
    summed_state = jnp.einsum(
        "fzay,fzyo->fao", rounded_state, value_rows, preferred_element_type=jnp.float32
    )
    attended = (summed_state / total[:, :, None]).astype(jnp.bfloat16).reshape(group_rows, head_dim)
    attn = lax.all_to_all(attended, "heads", split_axis=0, concat_axis=1, tiled=True)
    mid = features + jnp.dot(attn, w_out, preferred_element_type=jnp.float32)
    second_normed_state = layer_norm(mid).astype(jnp.bfloat16)
    hidden = jax.nn.gelu(
        jnp.dot(second_normed_state, w_up, preferred_element_type=jnp.float32), approximate=False
    ).astype(jnp.bfloat16)
    return (mid + jnp.dot(hidden, w_down, preferred_element_type=jnp.float32)).astype(jnp.bfloat16)


def solution(mesh):
    placed = (
        P(("nodes", "heads"), None),
        P(),
        P(),
        P(),
        P(),
        P("nodes", None),
        P("nodes", None, None, None),
        P(),
    )
    return jax.shard_map(
        body, mesh=mesh, in_specs=placed, out_specs=P(("nodes", "heads"), None), check_vma=False
    )
```

profile of v0, /device:TPU:0, one launch (start us, length us, event | category | flops | bytes accessed | tf_op | source)
XLA Modules:
  0.0 157.7 jit_solution(17746857934866369299)
XLA Ops:
  6.5 0.0 copy-start
  6.5 0.0 all-gather.2.cloned.1.call-start
  6.5 1.2 convert_reduce_fusion
  7.7 1.2 fusion.33
  8.9 0.0 copy-start.6
  8.9 0.0 copy-start.5
  8.9 1.8 %fusion.34 = bf16[256,512]{1,0:T(8,128)(2,1)} fusion(bf16[256,512]{1,0:T(8,128)(2,1)} %param.8, f32[256]{0:T(256)S(1)} %add_rsqrt_fusion.1, f32[256]{0:T(256)S(1)} %broadcast_multiply_fusion.1), kind=kLoop, calls=%fused_computation.37 | loop fusion | flops 524288 | bytes 526336 | tf_op jit(solution)/shard_map/convert_element_type | solution.py:43
  10.7 0.0 all-gather.2.cloned.1.call-update
  10.8 0.0 all-reduce.3.cloned.1.call-start
  10.8 19.5 %all-gather.2.cloned.1.call-done = bf16[1024,512]{1,0:T(8,128)(2,1)} async-done(((bf16[256,512]{1,0:T(8,128)(2,1)}), bf16[1024,512]{1,0:T(8,128)(2,1)}) %all-gather.2.cloned.1.call-update) | async-done | bytes 1048592 | tf_op jit(solution)/shard_map/all_gather | solution.py:47
  30.3 0.0 copy-done
  30.3 1.9 %convolution_convert_fusion = bf16[1024,384]{1,0:T(8,128)(2,1)S(1)} fusion(bf16[1024,512]{1,0:T(8,128)(2,1)} %all-gather.2.cloned.1.call-done, bf16[512,1536]{1,0:T(8,128)(2,1)S(1)} %copy-done, s32[]{:T(128)S(6)} %select_n.100), kind=kOutput, calls=%fused_computation.7 | convolution fusion | flops 403046400 | bytes 2228228 | tf_op jit(solution)/shard_map/dot_general | solution.py:46
  32.3 0.0 copy-start.3
  32.3 0.9 slice.34
  33.2 1.5 collective-permute-start
  34.7 0.0 copy-done.6
  34.7 0.1 reshape.40
  34.8 0.0 copy-done.5
  34.8 0.6 fusion.106
  35.4 3.3 %collective-permute-start.1 = (bf16[1024,256]{1,0:T(8,128)(2,1)}, bf16[1024,256]{1,0:T(8,128)(2,1)}, u32[]{:S(2)}, u32[]{:S(2)}) collective-permute-start(bf16[1024,256]{1,0:T(8,128)(2,1)} %slice.34), channel_id=1, source_target_pairs={{4,0},{8,4},{12,8},{16,12},{20,16},{24,20},{28,24},{0,28},{5,1},{9... | collective-permute-start | bytes 1572872 | tf_op jit(solution)/shard_map/ppermute | solution.py:18
  48.5 5.4 %copy.11 = s32[8,8,128,128]{2,3,1,0:T(8,128)} copy(s32[8,8,128,128]{3,2,1,0:T(8,128)} %param.14) | data formatting | bytes 8388608 | tf_op args[6]
  53.9 0.0 copy-done.3
  53.9 0.7 slice.36
  54.6 1.7 %dynamic-slice_select_fusion = (bf16[128,256]{1,0:T(8,128)(2,1)}, bf16[128,256]{1,0:T(8,128)(2,1)}, bf16[128,256]{1,0:T(8,128)(2,1)}, bf16[128,256]{1,0:T(8,128)(2,1)}) fusion(bf16[1024,256]{1,0:T(8,128)(2,1)} %slice.34, s32[]{:T(128)S(6)} %select_n.119, pred[]{:T(512)S(6)} %eq.30, s32[]{:T(128)S(6)} %select_n.114, pred[]{:T(512)S(6)} %eq.29, ...), kind=kLoop, calls=%fused_computation.74 | loop fusion | flops 131072 | bytes 524308 | tf_op jit(solution)/shard_map/jit(_where)/select_n | solution.py:24
  56.2 0.0 all-reduce.3.cloned.1.call-update
  56.3 1.5 collective-permute-done
  57.8 1.1 constant_dynamic-update-slice_fusion.6
  58.9 1.1 constant_dynamic-update-slice_fusion.5
  60.0 0.8 collective-permute-done.1
  60.7 1.1 constant_dynamic-update-slice_fusion.4
  61.8 63.2 %all-reduce.3.cloned.1.call-done = (bf16[128,256]{1,0:T(8,128)(2,1)}, bf16[128,256]{1,0:T(8,128)(2,1)}, bf16[128,256]{1,0:T(8,128)(2,1)}, bf16[128,256]{1,0:T(8,128)(2,1)}) async-done(((bf16[128,256]{1,0:T(8,128)(2,1)}, bf16[128,256]{1,0:T(8,128)(2,1)}, bf16[128,256]{1,0:T(8,128)(2,1)}, bf16[128,256]{1,0:T(8,128)(2,1)}), (bf16[128,256]{1,0:T(8,128)(2,1)}, bf16[128,256]{1,0:T(8,128)(2,1)}, ...) | async-done | bytes 262160 | tf_op jit(solution)/shard_map/psum | solution.py:25
  125.0 0.8 constant_dynamic-update-slice_fusion.3
  125.9 0.8 constant_dynamic-update-slice_fusion.2
  126.7 0.8 constant_dynamic-update-slice_fusion.1
  127.6 0.8 constant_dynamic-update-slice_fusion
  128.4 2.8 %gather_fusion = bf16[64,128,256]{2,1,0:T(8,128)(2,1)} fusion(bf16[28,128,256]{2,1,0:T(8,128)(2,1)S(1)} %bitcast.31, s32[1024]{0:T(1024)S(1)} %pad_clamp_fusion), kind=kCustom, calls=%fused_computation | custom fusion | bytes 8388864 | tf_op jit(solution)/shard_map/gather | solution.py:79
  131.2 4.2 %fusion.107 = (f32[8,128]{1,0:T(8,128)S(1)}, bf16[8,8,128,128]{2,3,1,0:T(8,128)(2,1)S(1)}) fusion(s32[8,8,128,128]{2,3,1,0:T(8,128)} %copy.11, bf16[8,128,128,1]{2,1,3,0:T(8,128)(2,1)} %bitcast.34, bf16[8,8,128,256]{3,2,1,0:T(8,128)(2,1)} %bitcast.32), kind=kOutput, calls=%fused_computation.136 | convolution fusion | flops 273677312 | bytes 8654848 | tf_op jit(solution)/shard_map/lou,lwgu->lwog/dot_general | solution.py:83
  135.4 0.0 copy-done.1
  135.4 0.0 copy-start.2
  135.4 0.0 copy-start.4
  135.5 0.8 fusion.15
  136.3 0.1 copy.13
  136.4 8.6 %all_to_all.19 = bf16[4,256,128]{1,2,0:T(8,128)(2,1)S(1)} all-to-all(bf16[4,256,128]{1,2,0:T(8,128)(2,1)S(1)} %copy.13), channel_id=1, replica_groups=mesh['nodes'=8,'heads'=4] {'heads'}, dimensions={0} | all-to-all | bytes 524288 | tf_op jit(solution)/shard_map/all_to_all | solution.py:93
  145.0 0.0 copy-done.2
  145.0 0.0 copy-done.4
  145.0 0.4 fusion.108
  145.4 0.2 multiply_reduce_fusion
  145.6 5.2 %fusion.9 = bf16[256,512]{1,0:T(8,128)(2,1)} fusion(f32[256,512]{1,0:T(8,128)S(1)} %get-tuple-element.20, bf16[1024,512]{1,0:T(8,128)(2,1)} %param.12, bf16[512,1024]{1,0:T(8,128)(2,1)} %param.11, f32[256]{0:T(256)S(1)} %add_rsqrt_fusion, f32[256]{0:T(256)S(1)} %broadcast_multiply_fusion), kind=kOutput, calls=%fused_computation.11 | convolution fusion | flops 554565632 | bytes 2885632 | tf_op jit(solution)/shard_map/dot_general | solution.py:99
  (7 shorter events, 0.1 us)
Async XLA Ops:
  6.5 23.8 %copy-start = (bf16[512,1536]{1,0:T(8,128)(2,1)S(1)}, bf16[512,1536]{1,0:T(8,128)(2,1)}, u32[]{:S(2)}) copy-start(bf16[512,1536]{1,0:T(8,128)(2,1)} %param.9) | copy-start | bytes 4718596
  6.5 23.8 %all-gather.2.cloned.1.call-start = ((), (), s32[]{:S(2)}) async-start(), calls=%async_computation.1 | async-start | bytes 1310720 | tf_op jit(solution)/shard_map/all_gather | solution.py:47
  8.9 25.8 %copy-start.6 = (s32[8,8]{1,0:T(8,128)S(1)}, s32[8,8]{1,0:T(8,128)}, u32[]{:S(2)}) copy-start(s32[8,8]{1,0:T(8,128)} %param.13) | copy-start | bytes 772
  8.9 25.9 %copy-start.5 = (s32[4]{0:T(128)S(1)}, s32[4]{0:T(128)}, u32[]{:S(2)}) copy-start(s32[4]{0:T(128)} %param.15) | copy-start | bytes 52
  10.8 114.3 %all-reduce.3.cloned.1.call-start = ((), (), s32[]{:S(2)}) async-start(), calls=%async_computation.2 | async-start | bytes 524288 | tf_op jit(solution)/shard_map/psum | solution.py:25
  32.3 21.6 %copy-start.3 = (bf16[1024,384]{1,0:T(8,128)(2,1)}, bf16[1024,384]{1,0:T(8,128)(2,1)S(1)}, u32[]{:S(2)}) copy-start(bf16[1024,384]{1,0:T(8,128)(2,1)S(1)} %convolution_convert_fusion) | copy-start | bytes 2359300
  33.2 24.6 %collective-permute-start = (bf16[1024,256]{1,0:T(8,128)(2,1)}, bf16[1024,256]{1,0:T(8,128)(2,1)}, u32[]{:S(2)}, u32[]{:S(2)}) collective-permute-start(bf16[1024,256]{1,0:T(8,128)(2,1)} %slice.34), channel_id=1, source_target_pairs={{0,4},{4,8},{8,12},{12,16},{16,20},{20,24},{24,28},{28,0},{1,5},{5... | collective-permute-start | bytes 1572872 | tf_op jit(solution)/shard_map/ppermute | solution.py:15
  35.4 25.3 %collective-permute-start.1 = (bf16[1024,256]{1,0:T(8,128)(2,1)}, bf16[1024,256]{1,0:T(8,128)(2,1)}, u32[]{:S(2)}, u32[]{:S(2)}) collective-permute-start(bf16[1024,256]{1,0:T(8,128)(2,1)} %slice.34), channel_id=1, source_target_pairs={{4,0},{8,4},{12,8},{16,12},{20,16},{24,20},{28,24},{0,28},{5,1},{9... | collective-permute-start | bytes 1572872 | tf_op jit(solution)/shard_map/ppermute | solution.py:18
  131.2 4.2 %copy-start.1 = (bf16[64,128,256]{2,1,0:T(8,128)(2,1)S(1)}, bf16[64,128,256]{2,1,0:T(8,128)(2,1)}, u32[]{:S(2)}) copy-start(bf16[64,128,256]{2,1,0:T(8,128)(2,1)} %gather_fusion) | copy-start | bytes 12582916
  135.4 9.6 %copy-start.2 = (bf16[256,512]{1,0:T(8,128)(2,1)S(1)}, bf16[256,512]{1,0:T(8,128)(2,1)}, u32[]{:S(2)}) copy-start(bf16[256,512]{1,0:T(8,128)(2,1)} %param.8) | copy-start | bytes 786436
  135.4 9.6 %copy-start.4 = (bf16[512,512]{1,0:T(8,128)(2,1)S(1)}, bf16[512,512]{1,0:T(8,128)(2,1)}, u32[]{:S(2)}) copy-start(bf16[512,512]{1,0:T(8,128)(2,1)} %param.10) | copy-start | bytes 1572868
Sparse Core Ops, SparseCore 0:
  10.9 19.4 all-gather.1
  56.4 68.5 all-reduce.2
where the time goes:
time: 159 us; the launch traced here: 158 us
  waiting for transfers between devices  85.1 us (54%)
  between operations  23.4 us (15%)
  local copies, waits for them, and re-layouts  17.3 us (11%)
  matrix products  12.6 us (8%)
  blocking collectives  8.59 us (5%)
  other arithmetic  6.05 us (4%)
  starting transfers between devices  4.77 us (3%)
    psum x1, waiting for transfers between devices, broadcast(): return lax.psum(kept, axis)  63.2 us
    all_gather x1, waiting for transfers between devices, body(): lax.all_gather(normed, 'heads', axis=0, tiled=True)  19.5 us
    unnamed x21, local copies, waits for them, and re-layouts  11.2 us
    all_to_all x1, blocking collectives, body(): lax.all_to_all(attended, 'heads', split_axis=0, concat_axis=1, tiled=True)  8.59 us
    dot_general x1, matrix products, body(): jnp.dot(hidden, w_down, preferred_element_type=jnp.float32)  5.19 us
    dot_general x1, matrix products, body(): jnp.einsum('lou,lwgu->lwog', query_block_rows, key_rows, preferred_elemen...  4.23 us
    ppermute x1, starting transfers between devices, padded(): lax.ppermute(lax.slice_in_dim(block, 0, width, axis=dim), axis, backward)  3.26 us
  transfers between devices with their start and end apart: 4, of which 4 were waited for; matrix products, arithmetic and copies ran while one was open for 7% of the time, Pallas kernels for 0%

commit v1 on v0

v1 whole, which is shorter than its diff:
```python
import functools

import jax
import jax.numpy as jnp
from jax import lax
from jax.experimental import pallas as pl
from jax.experimental.pallas import tpu as pltpu
from jax.sharding import PartitionSpec as P

TB = 128
PIECES = 8
PIECE = TB // PIECES
AXES = ("nodes", "heads")
ANY = pl.BlockSpec(memory_space=pl.ANY)
VMEM = pl.BlockSpec(memory_space=pltpu.VMEM)


def send(value, nodes, heads, where):
    pairs = []
    for n in range(nodes):
        for h in range(heads):
            to_n, to_h = where(n, h)
            pairs.append((n * heads + h, to_n % nodes * heads + to_h))
    return lax.ppermute(value, AXES, pairs)


def layer_norm(value_rows):
    mean = jnp.mean(value_rows, axis=-1, keepdims=True)
    centered = value_rows - mean
    spread = jnp.mean(centered * centered, axis=-1, keepdims=True)
    return (centered * lax.rsqrt(spread + 1e-05)).astype(jnp.bfloat16)


def project(normed, w_ref, cols):
    return jnp.dot(normed, w_ref[:, cols], preferred_element_type=jnp.float32).astype(
        jnp.bfloat16
    )


def keyval_into(out_ref, rows, normed, w_ref, heads, head_dim):
    width = heads * head_dim
    if head_dim % 128 == 0:
        for h in range(heads):
            both = project(normed, w_ref, slice((3 * h + 1) * head_dim, (3 * h + 3) * head_dim))
            out_ref[rows, h * head_dim : (h + 1) * head_dim] = both[:, :head_dim]
            out_ref[rows, width + h * head_dim : width + (h + 1) * head_dim] = both[:, head_dim:]
    else:
        out_ref[rows, :] = project(normed, w_ref, slice(width, 3 * width))


def query_into(out_ref, normed, w_ref, heads, head_dim):
    if head_dim % 128 == 0:
        for h in range(heads):
            out_ref[:, h * head_dim : (h + 1) * head_dim] = project(
                normed, w_ref, slice(3 * h * head_dim, (3 * h + 1) * head_dim)
            )
    else:
        out_ref[...] = project(normed, w_ref, slice(0, heads * head_dim))


def keyval_kernel(heads, head_dim, first_ref, second_ref, w_ref, out_ref, *query_ref):
    node_dev = first_ref.shape[0]
    for at, ref in enumerate((first_ref, second_ref)):
        normed = layer_norm(ref[...].astype(jnp.float32))
        keyval_into(out_ref, slice(at * node_dev, (at + 1) * node_dev), normed, w_ref, heads, head_dim)
        if at == 0 and query_ref:
            query_into(query_ref[0], normed, w_ref, heads, head_dim)


def keyvals(first, second, w_qkv, heads, head_dim, with_query):
    node_dev, width = first.shape
    out_shape = [jax.ShapeDtypeStruct((2 * node_dev, 2 * width), jnp.bfloat16)]
    if with_query:
        out_shape.append(jax.ShapeDtypeStruct((node_dev, width), jnp.bfloat16))
    return pl.pallas_call(
        functools.partial(keyval_kernel, heads, head_dim),
        out_shape=out_shape,
        in_specs=[VMEM] * 3,
        out_specs=[VMEM] * len(out_shape),
        compiler_params=pltpu.CompilerParams(vmem_limit_bytes=16 << 20),
        cost_estimate=pl.CostEstimate(
            flops=8 * node_dev * width * width, bytes_accessed=6 * width * width, transcendentals=0
        ),
        name="keyvals",
    )(first, second, w_qkv)


def pick_kernel(hub_count, plan_ref, *refs):
    sources, out_ref, sem = refs[:8], refs[8], refs[9]
    for j in range(hub_count):
        code, slot = plan_ref[2 * j], plan_ref[2 * j + 1]
        place = out_ref.at[j * PIECE : (j + 1) * PIECE]
        for k, ref in enumerate(sources):
            @pl.when(code == k)
            def _():
                if k < 6:
                    row = slot * TB + plan_ref[2 * hub_count] * PIECE
                else:
                    row = slot * 2 * PIECE + plan_ref[2 * hub_count + 1] * PIECE
                rows = pl.ds(pl.multiple_of(row, PIECE), PIECE)
                pltpu.make_async_copy(ref.at[rows], place, sem.at[j]).start()

        @pl.when(code >= 8)
        def _():
            out_ref[j * PIECE : (j + 1) * PIECE] = jnp.zeros((PIECE, out_ref.shape[1]), out_ref.dtype)

    for j in range(hub_count):
        @pl.when(plan_ref[2 * j] < 8)
        def _():
            place = out_ref.at[j * PIECE : (j + 1) * PIECE]
            pltpu.make_async_copy(sources[0].at[0:PIECE], place, sem.at[j]).wait()


def pick_pieces(plan, sources, hub_count):
    width = sources[0].shape[1]
    return pl.pallas_call(
        functools.partial(pick_kernel, hub_count),
        out_shape=jax.ShapeDtypeStruct((hub_count * PIECE, width), jnp.bfloat16),
        in_specs=[pl.BlockSpec(memory_space=pltpu.SMEM)] + [ANY] * 8,
        out_specs=VMEM,
        scratch_shapes=[pltpu.SemaphoreType.DMA((hub_count,))],
        name="pick_pieces",
    )(plan, *sources)


def final_kernel(
    heads, head_dim, hub_count, tiles, count,
    plan_ref, tokens_ref, query_ref, hub_a_ref, hub_b_ref, mask_ref, w_qkv_ref, w_out_ref, w_up_ref, w_down_ref, *refs
):
    stores, out_ref = refs[:count], refs[count]
    tile_ref, hub_kv, hub_rows, mask, w_qkv, w_out, w_up, w_down, attn, tile_sem, sem = refs[count + 1 :]
    node_dev, width = tokens_ref.shape
    local = node_dev // TB
    slots = local * tiles
    in_store = stores[0].shape[0] // TB
    loads = [
        pltpu.make_async_copy(w_qkv_ref, w_qkv, sem.at[0]),
        pltpu.make_async_copy(
            mask_ref.at[pl.ds(plan_ref[slots] * local, local)], mask, sem.at[1]
        ),
        pltpu.make_async_copy(w_out_ref, w_out, sem.at[2]),
        pltpu.make_async_copy(w_up_ref, w_up, sem.at[3]),
        pltpu.make_async_copy(w_down_ref, w_down, sem.at[4]),
    ]
    loads[0].start()
    for i in range(slots):
        index = plan_ref[i]
        for a, store in enumerate(stores):
            @pl.when(index // in_store == a)
            def _():
                rows = pl.ds(pl.multiple_of(index % in_store * TB, TB), TB)
                pltpu.make_async_copy(store.at[rows], tile_ref.at[i], tile_sem.at[i]).start()

    for load in loads[1:]:
        load.start()
    half = PIECES // 2
    for k in range(PIECES):
        source = hub_b_ref if k & 1 else hub_a_ref
        piece = plan_ref[slots + 1 + k]
        for j in range(hub_count):
            row = (k >> 1) * hub_count * PIECE + j * PIECE
            place = pl.ds(pl.multiple_of(j * TB + piece * PIECE, PIECE), PIECE)
            hub_rows[place, :] = source[row : row + PIECE, :]
    hub_normed = layer_norm(hub_rows[...].astype(jnp.float32))
    loads[0].wait()
    keyval_into(hub_kv, slice(None), hub_normed, w_qkv, heads, head_dim)
    hub_base = count * in_store
    for i in range(slots):
        index = plan_ref[i]

        @pl.when(index >= hub_base)
        def _():
            rows = pl.ds(pl.multiple_of((index - hub_base) * TB, TB), TB)
            pltpu.make_async_copy(hub_kv.at[rows], tile_ref.at[i], tile_sem.at[i]).start()

    loads[1].wait()
    scale = 1.0 / head_dim**0.5
    group = max(head_dim, 128)
    per = group // head_dim
    lane = lax.broadcasted_iota(jnp.int32, (TB, group), 1)
    for r in range(local):
        for t in range(tiles):
            i = r * tiles + t
            pltpu.make_async_copy(hub_kv.at[0:TB], tile_ref.at[i], tile_sem.at[i]).wait()
        edges = jnp.concatenate([mask[r, t].astype(jnp.float32) for t in range(tiles)], axis=1)
        for g in range(heads // per):
            cols = slice(g * group, (g + 1) * group)
            keys = tile_ref[r * tiles : (r + 1) * tiles, :, cols].reshape(tiles * TB, group)
            values = tile_ref[
                r * tiles : (r + 1) * tiles, :, width + g * group : width + (g + 1) * group
            ].reshape(tiles * TB, group)
            query = query_ref[r * TB : (r + 1) * TB, cols]
            result = None
            for s in range(per):
                here = (lane >= s * head_dim) & (lane < (s + 1) * head_dim)
                own = query if per == 1 else jnp.where(here, query.astype(jnp.float32), 0.0).astype(jnp.bfloat16)
                score = lax.dot_general(
                    own, keys, (((1,), (1,)), ((), ())), preferred_element_type=jnp.float32
                )
                weight = jnp.exp(score * scale) * edges
                total = jnp.sum(weight, axis=1, keepdims=True)
                summed = jnp.dot(
                    weight.astype(jnp.bfloat16), values, preferred_element_type=jnp.float32
                )
                one = summed / total
                result = one if result is None else jnp.where(here, one, result)
            attn[r * TB : (r + 1) * TB, cols] = result.astype(jnp.bfloat16)
    loads[2].wait()
    mid = tokens_ref[...].astype(jnp.float32) + jnp.dot(
        attn[...], w_out[...], preferred_element_type=jnp.float32
    )
    normed = layer_norm(mid)
    loads[3].wait()
    up = jnp.dot(normed, w_up[...], preferred_element_type=jnp.float32)
    hidden = (0.5 * up * (1.0 + lax.erf(up * (0.5**0.5)))).astype(jnp.bfloat16)
    loads[4].wait()
    out_ref[...] = (
        mid + jnp.dot(hidden, w_down[...], preferred_element_type=jnp.float32)
    ).astype(jnp.bfloat16)


def finish(plan, tokens, query, hub_a, hub_b, mask, w_qkv, w_out, w_up, w_down, stores, heads, head_dim, hub_count):
    node_dev, width = tokens.shape
    local = node_dev // TB
    tiles = mask.shape[1]
    slots = local * tiles
    bf16 = jnp.bfloat16
    return pl.pallas_call(
        functools.partial(final_kernel, heads, head_dim, hub_count, tiles, len(stores)),
        out_shape=jax.ShapeDtypeStruct(tokens.shape, bf16),
        in_specs=[pl.BlockSpec(memory_space=pltpu.SMEM)] + [VMEM] * 4 + [ANY] * (5 + len(stores)),
        out_specs=VMEM,
        scratch_shapes=[
            pltpu.VMEM((slots, TB, 2 * width), bf16),
            pltpu.VMEM((hub_count * TB, 2 * width), bf16),
            pltpu.VMEM((hub_count * TB, width), bf16),
            pltpu.VMEM((local,) + mask.shape[1:], jnp.int32),
            pltpu.VMEM(w_qkv.shape, bf16),
            pltpu.VMEM(w_out.shape, bf16),
            pltpu.VMEM(w_up.shape, bf16),
            pltpu.VMEM(w_down.shape, bf16),
            pltpu.VMEM((node_dev, width), bf16),
            pltpu.SemaphoreType.DMA((slots,)),
            pltpu.SemaphoreType.DMA((5,)),
        ],
        compiler_params=pltpu.CompilerParams(vmem_limit_bytes=40 << 20),
        name="finish",
    )(plan, tokens, query, hub_a, hub_b, mask, w_qkv, w_out, w_up, w_down, *stores)


def body(tokens, w_qkv, w_out, w_up, w_down, tile_cols, tile_mask, hub_blocks):
    node_dev, width = tokens.shape
    nodes = lax.axis_size("nodes")
    heads = lax.axis_size("heads")
    head_dim = width // heads
    per_group, tiles = tile_cols.shape
    hub_count = hub_blocks.shape[0]
    local = node_dev // TB
    here = lax.axis_index("nodes")
    head_here = lax.axis_index("heads")
    go = functools.partial(send, nodes=nodes, heads=heads)

    def core(value):
        return go(value, where=lambda n, h: (n, h ^ 1))

    def pair(value):
        return go(value, where=lambda n, h: (n ^ 1, h))

    def along(value):
        return go(value, where=lambda n, h: (n + 2 - 4 * (n & 1), h))

    strip_at = ((1 - here % 2) * 4 + ((head_here % 4) ^ 2) // 2 * 2) * PIECE
    strip = lax.dynamic_slice_in_dim(tokens.reshape(local, TB, width), strip_at, 2 * PIECE, 1)
    strip = strip.reshape(local * 2 * PIECE, width)
    paired = pair(tokens)
    sides = [go(tokens, where=lambda n, h, o=o: (n, h ^ o)) for o in range(2, heads, 2)]
    across = go(strip, where=lambda n, h: (n ^ 1, h ^ 2))
    token_core = core(tokens)
    paired, *sides, across = lax.optimization_barrier((paired, *sides, across))
    paired_core = core(paired)
    sides_core = [core(v) for v in sides]
    across_core = core(across)

    owner_n = hub_blocks // per_group
    owner_h = hub_blocks % per_group // local
    whole_bits = nodes // 2 * (heads // 4)
    owner_area = owner_n // 2 * (heads // 4) + owner_h // 4
    area = here // 2 * (heads // 4) + head_here // 4
    offset = ((owner_n ^ here) & 1) * 4 + ((owner_h ^ head_here) & 3)
    code = jnp.where(owner_area == area, offset, 8)
    my_piece = here % 2 * 4 + head_here % 4
    pick_plan = jnp.concatenate(
        [
            jnp.stack([code, hub_blocks % local], axis=1).reshape(-1),
            jnp.stack([my_piece, head_here % 2]),
        ]
    ).astype(jnp.int32)
    sources = [tokens, token_core, sides[0], sides_core[0], paired, paired_core, across, across_core]
    piece = pick_pieces(pick_plan, sources, hub_count)

    far = along(paired)
    paired_sides = [pair(v) for v in sides]

    def to_area(n, h, shift):
        at = (n // 2 * (heads // 4) + h // 4) ^ shift
        return at // (heads // 4) * 2 + n % 2, at % (heads // 4) * 4 + h % 4

    step = 1
    apart = owner_area ^ area
    while step < whole_bits:
        reach = [s * step for s in (1, 2, 3) if s * step < whole_bits]
        got = [go(piece, where=lambda n, h, s=s: to_area(n, h, s)) for s in reach]
        digit = jnp.repeat(apart // step % 4, PIECE)[:, None]
        for s, value in zip(reach, got):
            piece = jnp.where(digit == s // step, value, piece)
        step *= 4

    far_sides = [along(v) for v in paired_sides]
    around = [
        piece,
        go(piece, where=lambda n, h: (n, h ^ 2)),
        pair(piece),
        go(piece, where=lambda n, h: (n ^ 1, h ^ 2)),
    ]
    hub_a = jnp.concatenate(around, axis=0)
    hub_b = core(hub_a)

    far_core = core(far)
    paired_sides_core = [core(v) for v in paired_sides]
    far_sides_core = [core(v) for v in far_sides]

    weights = w_qkv
    if head_dim % 128:
        weights = w_qkv.reshape(width, heads, 3, head_dim).swapaxes(1, 2).reshape(width, 3 * width)
    keyval = functools.partial(keyvals, w_qkv=weights, heads=heads, head_dim=head_dim)
    first, query = keyval(tokens, token_core, with_query=True)
    stores = [first]
    for value, other in zip(sides, sides_core):
        stores += keyval(value, other, with_query=False)
    stores += keyval(paired, paired_core, with_query=False)
    for value, other in zip(paired_sides, paired_sides_core):
        stores += keyval(value, other, with_query=False)
    stores += keyval(far, far_core, with_query=False)
    for value, other in zip(far_sides, far_sides_core):
        stores += keyval(value, other, with_query=False)

    mine = lax.dynamic_slice_in_dim(tile_cols, head_here * local, local, 0)
    blocks_all = per_group * nodes
    col_group = mine // per_group
    col_block = mine % per_group
    region = jnp.where(col_group == here, 0, jnp.where(col_group == (here ^ 1), 1, 2))
    index = region * per_group + ((col_block // local) ^ head_here) * local + col_block % local
    hub_slot = jnp.clip(mine - blocks_all, 0, hub_count - 1)
    index = jnp.where(mine >= blocks_all, 3 * per_group + hub_slot, index).reshape(-1)
    offsets = jnp.array([0, 1, 2, 3, 4, 5, 6, 7], jnp.int32)
    plan = jnp.concatenate([index, head_here[None], offsets ^ my_piece]).astype(jnp.int32)
    return finish(
        plan, tokens, query, hub_a, hub_b, tile_mask, weights, w_out, w_up, w_down, stores, heads, head_dim, hub_count
    )


def solution(mesh):
    placed = (
        P(("nodes", "heads"), None),
        P(),
        P(),
        P(),
        P(),
        P("nodes", None),
        P("nodes", None, None, None),
        P(),
    )
    return jax.shard_map(
        body, mesh=mesh, in_specs=placed, out_specs=P(("nodes", "heads"), None), check_vma=False
    )
```

time: 159 us -> 69.4 us (0.44)
  the two profiles are of different devices: /device:TPU:0 before, /device:TPU:9 now
where the time goes in v1:
time: 69.4 us; the launch traced here: 68.5 us
  starting transfers between devices  23 us (33%)
  waiting for transfers between devices  18.1 us (26%)
  Pallas kernels  15 us (22%)
  local copies, waits for them, and re-layouts  8.23 us (12%)
  other arithmetic  3.76 us (5%)
    ppermute x20, starting transfers between devices, send(): return lax.ppermute(value, AXES, pairs)  23 us
    ppermute x20, waiting for transfers between devices, send(): return lax.ppermute(value, AXES, pairs)  18.1 us
    pallas_call x1, Pallas kernels, finish(): pl.pallas_call(functools.partial(final_kernel, heads, head_dim, hub_count...  7.71 us
    unnamed x38, local copies, waits for them, and re-layouts  6.65 us
    pallas_call x6, Pallas kernels, keyvals(): pl.pallas_call(functools.partial(keyval_kernel, heads, head_dim), out_sha...  5.86 us
    pallas_call x1, Pallas kernels, pick_pieces(): pl.pallas_call(functools.partial(pick_kernel, hub_count), out_shape=jax.S...  1.4 us
  transfers between devices with their start and end apart: 20, of which 4 were waited for; matrix products, arithmetic and copies ran while one was open for 8% of the time, Pallas kernels for 11%

profile of v1, /device:TPU:9, one launch (start us, length us, event | category | flops | bytes accessed | tf_op | source)
XLA Modules:
  0.0 68.5 jit_solution(11667647723294671674)
XLA Ops:
  0.0 1.2 %collective-permute-start.2 = (bf16[256,512]{1,0:T(8,128)(2,1)}, bf16[256,512]{1,0:T(8,128)(2,1)S(1)}, u32[]{:S(2)}, u32[]{:S(2)}) collective-permute-start(bf16[256,512]{1,0:T(8,128)(2,1)} %tokens_ref.1), channel_id=1, source_target_pairs={{0,2},{1,3},{2,0},{3,1},{4,6},{5,7},{6,4},{7,5},{8,10},{9,11},{10,... | collective-permute-start | bytes 786440 | tf_op jit(solution)/shard_map/ppermute | solution.py:24
  1.2 1.2 %collective-permute-start.1 = (bf16[256,512]{1,0:T(8,128)(2,1)}, bf16[256,512]{1,0:T(8,128)(2,1)S(1)}, u32[]{:S(2)}, u32[]{:S(2)}) collective-permute-start(bf16[256,512]{1,0:T(8,128)(2,1)} %tokens_ref.1), channel_id=1, source_target_pairs={{0,4},{1,5},{2,6},{3,7},{4,0},{5,1},{6,2},{7,3},{8,12},{9,13},{10,... | collective-permute-start | bytes 786440 | tf_op jit(solution)/shard_map/ppermute | solution.py:24
  2.5 1.2 %collective-permute-start = (bf16[256,512]{1,0:T(8,128)(2,1)}, bf16[256,512]{1,0:T(8,128)(2,1)S(1)}, u32[]{:S(2)}, u32[]{:S(2)}) collective-permute-start(bf16[256,512]{1,0:T(8,128)(2,1)} %tokens_ref.1), channel_id=1, source_target_pairs={{0,1},{1,0},{2,3},{3,2},{4,5},{5,4},{6,7},{7,6},{8,9},{9,8},{10,11... | collective-permute-start | bytes 786440 | tf_op jit(solution)/shard_map/ppermute | solution.py:24
  3.7 0.8 %constant_dynamic-slice_fusion = bf16[2,32,512]{2,1,0:T(8,128)(2,1)S(1)} fusion(bf16[2,128,512]{2,1,0:T(8,128)(2,1)} %bitcast.9, s32[]{:T(128)S(6)} %select_n.129), kind=kLoop, calls=%fused_computation.47 | loop fusion | bytes 131076 | tf_op jit(solution)/shard_map/dynamic_slice | solution.py:273
  4.5 0.2 collective-permute-start.3
  4.7 0.7 %broadcast_compare_fusion.1 = (pred[4]{0:T(512)(128)(4,1)S(1)}, s32[4]{0:T(128)S(1)}, s32[4]{0:T(128)S(1)}, s32[4]{0:T(128)S(1)}, s32[4]{0:T(128)S(1)}) fusion(s32[]{:T(128)S(6)} %add.88, s32[4]{0:T(128)} %param.16), kind=kLoop, calls=%fused_computation.51 | loop fusion | flops 312 | bytes 88 | tf_op jit(solution)/shard_map/eq | solution.py:315
  5.4 0.7 fusion.3
  6.1 3.3 %collective-permute-done.3.refs_6_ = bf16[64,512]{1,0:T(8,128)(2,1)S(1)} collective-permute-done((bf16[64,512]{1,0:T(8,128)(2,1)S(1)}, bf16[64,512]{1,0:T(8,128)(2,1)S(1)}, u32[]{:S(2)}, u32[]{:S(2)}) %collective-permute-start.3) | collective-permute-done | bytes 65568 | tf_op jit(solution)/shard_map/ppermute | solution.py:24
  9.4 2.2 %collective-permute-start.4 = (bf16[256,512]{1,0:T(8,128)(2,1)S(1)}, bf16[256,512]{1,0:T(8,128)(2,1)S(1)}, u32[]{:S(2)}, u32[]{:S(2)}) collective-permute-start(bf16[256,512]{1,0:T(8,128)(2,1)S(1)} %collective-permute-done.2.refs_2_.first_ref), channel_id=1, source_target_pairs={{0,1},{1,0},{2,3},{3,2},{4,5},{5,4},{6,7},{7,6},{8,9},{9,8},{10,11... | collective-permute-start | bytes 786440 | tf_op jit(solution)/shard_map/ppermute | solution.py:24
  11.7 1.3 %collective-permute-start.14 = (bf16[256,512]{1,0:T(8,128)(2,1)S(1)}, bf16[256,512]{1,0:T(8,128)(2,1)S(1)}, u32[]{:S(2)}, u32[]{:S(2)}) collective-permute-start(bf16[256,512]{1,0:T(8,128)(2,1)S(1)} %collective-permute-done.2.refs_2_.first_ref), channel_id=1, source_target_pairs={{0,4},{1,5},{2,6},{3,7},{4,0},{5,1},{6,2},{7,3},{8,12},{9,13},{10,... | collective-permute-start | bytes 786440 | tf_op jit(solution)/shard_map/ppermute | solution.py:24
  13.0 0.7 %compare_select_fusion.5 = s32[2,8]{1,0:T(2,128)S(1)} fusion(s32[8,8]{1,0:T(8,128)} %param.14, s32[]{:T(128)S(6)} %select_n.107, s32[]{:T(128)} %axis_index.22, s32[]{:T(128)S(6)} %xor.36, s32[]{:T(128)S(6)} %axis_index.25), kind=kLoop, calls=%fused_computation.18 | loop fusion | flops 832 | bytes 144 | tf_op jit(solution)/shard_map/jit(_where)/select_n | solution.py:354
  13.8 0.1 eq.73
  13.9 0.1 copy.11
  14.2 0.1 eq.76
  14.3 0.1 eq.78
  14.4 0.7 collective-permute-start.6
  15.1 0.7 pad_add_fusion.2.plan_ref
  15.8 0.2 collective-permute-done.6.refs_7_
  16.0 0.4 copy-done.14
  16.5 0.2 copy-done.18
  16.6 0.1 copy-done.10
  16.7 0.7 %copy-done.12 = bf16[256,512]{1,0:T(8,128)(2,1)} copy-done((bf16[256,512]{1,0:T(8,128)(2,1)}, bf16[256,512]{1,0:T(8,128)(2,1)S(1)}, u32[]{:S(2)}) %copy-start.12) | copy-done | bytes 262168
  17.4 1.4 %pick_pieces.1 = bf16[64,512]{1,0:T(8,128)(2,1)} custom-call(s32[10]{0:T(128)} %pad_add_fusion.2.plan_ref, bf16[256,512]{1,0:T(8,128)(2,1)} %tokens_ref.1, bf16[256,512]{1,0:T(8,128)(2,1)} %copy-done.14, bf16[256,512]{1,0:T(8,128)(2,1)} %copy-done.6, bf16[256,512]{1,0:T(8,128)(2,1)} %copy-done.10, bf16[256,512]{1,0:T(8,128)(2,1)} %copy-done.8, ...), custom_call_target="tpu_custom_call" | custom-call | tf_op jit(solution)/shard_map/pick_pieces/pallas_call | solution.py:116
  18.9 0.9 %collective-permute-start.9 = (bf16[64,512]{1,0:T(8,128)(2,1)}, bf16[64,512]{1,0:T(8,128)(2,1)S(1)}, u32[]{:S(2)}, u32[]{:S(2)}) collective-permute-start(bf16[64,512]{1,0:T(8,128)(2,1)} %pick_pieces.1), channel_id=1, source_target_pairs={{0,8},{1,9},{2,10},{3,11},{4,12},{5,13},{6,14},{7,15},{8,0},{9,1},... | collective-permute-start | bytes 196616 | tf_op jit(solution)/shard_map/ppermute | solution.py:24
  19.8 2.2 %collective-permute-start.8 = (bf16[64,512]{1,0:T(8,128)(2,1)}, bf16[64,512]{1,0:T(8,128)(2,1)S(1)}, u32[]{:S(2)}, u32[]{:S(2)}) collective-permute-start(bf16[64,512]{1,0:T(8,128)(2,1)} %pick_pieces.1), channel_id=1, source_target_pairs={{0,16},{1,17},{2,18},{3,19},{4,20},{5,21},{6,22},{7,23},{8,24},{9,... | collective-permute-start | bytes 196616 | tf_op jit(solution)/shard_map/ppermute | solution.py:24
  22.0 0.2 collective-permute-start.7
  22.2 1.3 %collective-permute-start.16 = (bf16[256,512]{1,0:T(8,128)(2,1)}, bf16[256,512]{1,0:T(8,128)(2,1)S(1)}, u32[]{:S(2)}, u32[]{:S(2)}) collective-permute-start(bf16[256,512]{1,0:T(8,128)(2,1)} %copy-done.8), channel_id=1, source_target_pairs={{0,8},{1,9},{2,10},{3,11},{4,28},{5,29},{6,30},{7,31},{8,16},{9,17... | collective-permute-start | bytes 786440 | tf_op jit(solution)/shard_map/ppermute | solution.py:24
  23.5 2.3 %collective-permute-start.18 = (bf16[256,512]{1,0:T(8,128)(2,1)S(1)}, bf16[256,512]{1,0:T(8,128)(2,1)S(1)}, u32[]{:S(2)}, u32[]{:S(2)}) collective-permute-start(bf16[256,512]{1,0:T(8,128)(2,1)S(1)} %collective-permute-done.14.first_ref), channel_id=1, source_target_pairs={{0,8},{1,9},{2,10},{3,11},{4,28},{5,29},{6,30},{7,31},{8,16},{9,17... | collective-permute-start | bytes 786440 | tf_op jit(solution)/shard_map/ppermute | solution.py:24
  25.8 14.3 %collective-permute-done.7 = bf16[64,512]{1,0:T(8,128)(2,1)S(1)} collective-permute-done((bf16[64,512]{1,0:T(8,128)(2,1)}, bf16[64,512]{1,0:T(8,128)(2,1)S(1)}, u32[]{:S(2)}, u32[]{:S(2)}) %collective-permute-start.7) | collective-permute-done | bytes 65568 | tf_op jit(solution)/shard_map/ppermute | solution.py:24
  40.1 0.9 %select_select_fusion = bf16[64,512]{1,0:T(8,128)(2,1)S(1)} fusion(bf16[64,512]{1,0:T(8,128)(2,1)S(1)} %collective-permute-done.7, bf16[64,512]{1,0:T(8,128)(2,1)S(1)} %collective-permute-done.8, bf16[64,512]{1,0:T(8,128)(2,1)S(1)} %collective-permute-done.9, bf16[64,512]{1,0:T(8,128)(2,1)} %pick_pieces.1, pred[64]{0:T(512)(128)(4,1)S(1)} %eq.78, ...), kind=kLoop, calls=%fused_computation.1 | loop fusion | flops 98304 | bytes 327872 | tf_op jit(solution)/shard_map/jit(_where)/select_n | solution.py:315
  41.1 2.4 %collective-permute-start.11 = (bf16[64,512]{1,0:T(8,128)(2,1)S(1)}, bf16[64,512]{1,0:T(8,128)(2,1)S(1)}, u32[]{:S(2)}, u32[]{:S(2)}) collective-permute-start(bf16[64,512]{1,0:T(8,128)(2,1)S(1)} %select_select_fusion), channel_id=1, source_target_pairs={{0,4},{1,5},{2,6},{3,7},{4,0},{5,1},{6,2},{7,3},{8,12},{9,13},{10,... | collective-permute-start | bytes 196616 | tf_op jit(solution)/shard_map/ppermute | solution.py:24
  43.5 0.2 collective-permute-start.10
  43.8 1.7 %collective-permute-start.15 = (bf16[256,512]{1,0:T(8,128)(2,1)S(1)}, bf16[256,512]{1,0:T(8,128)(2,1)S(1)}, u32[]{:S(2)}, u32[]{:S(2)}) collective-permute-start(bf16[256,512]{1,0:T(8,128)(2,1)S(1)} %collective-permute-done.14.first_ref), channel_id=1, source_target_pairs={{0,1},{1,0},{2,3},{3,2},{4,5},{5,4},{6,7},{7,6},{8,9},{9,8},{10,11... | collective-permute-start | bytes 786440 | tf_op jit(solution)/shard_map/ppermute | solution.py:24
  45.6 1.7 %collective-permute-start.17 = (bf16[256,512]{1,0:T(8,128)(2,1)S(1)}, bf16[256,512]{1,0:T(8,128)(2,1)S(1)}, u32[]{:S(2)}, u32[]{:S(2)}) collective-permute-start(bf16[256,512]{1,0:T(8,128)(2,1)S(1)} %collective-permute-done.16.first_ref), channel_id=1, source_target_pairs={{0,1},{1,0},{2,3},{3,2},{4,5},{5,4},{6,7},{7,6},{8,9},{9,8},{10,11... | collective-permute-start | bytes 786440 | tf_op jit(solution)/shard_map/ppermute | solution.py:24
  47.3 0.2 collective-permute-done.10
  47.5 1.8 %collective-permute-start.13 = (bf16[256,512]{1,0:T(8,128)(2,1)S(1)}, bf16[256,512]{1,0:T(8,128)(2,1)S(1)}, u32[]{:S(2)}, u32[]{:S(2)}) collective-permute-start(bf16[256,512]{1,0:T(8,128)(2,1)S(1)} %pad_maximum_fusion.hub_a_ref), channel_id=1, source_target_pairs={{0,1},{1,0},{2,3},{3,2},{4,5},{5,4},{6,7},{7,6},{8,9},{9,8},{10,11... | collective-permute-start | bytes 786440 | tf_op jit(solution)/shard_map/ppermute | solution.py:24
  49.3 1.4 %copy-done = bf16[512,1536]{1,0:T(8,128)(2,1)S(1)} copy-done((bf16[512,1536]{1,0:T(8,128)(2,1)S(1)}, bf16[512,1536]{1,0:T(8,128)(2,1)}, u32[]{:S(2)}) %copy-start) | copy-done | bytes 1572888
  50.7 0.9 %copy-done.2 = bf16[256,512]{1,0:T(8,128)(2,1)S(1)} copy-done((bf16[256,512]{1,0:T(8,128)(2,1)S(1)}, bf16[256,512]{1,0:T(8,128)(2,1)}, u32[]{:S(2)}) %copy-start.2) | copy-done | bytes 262168
  51.7 0.9 %copy-done.15 = bf16[256,512]{1,0:T(8,128)(2,1)S(1)} copy-done((bf16[256,512]{1,0:T(8,128)(2,1)S(1)}, bf16[256,512]{1,0:T(8,128)(2,1)}, u32[]{:S(2)}) %copy-start.15) | copy-done | bytes 262168
  52.6 1.2 %keyvals.6 = (bf16[512,1024]{1,0:T(8,128)(2,1)S(1)}, bf16[256,512]{1,0:T(8,128)(2,1)S(1)}) custom-call(bf16[256,512]{1,0:T(8,128)(2,1)S(1)} %copy-done.2, bf16[256,512]{1,0:T(8,128)(2,1)S(1)} %copy-done.15, bf16[512,1536]{1,0:T(8,128)(2,1)S(1)} %copy-done), custom_call_target="tpu_custom_call" | custom-call | flops 536870912 | bytes 1572864 | tf_op jit(solution)/shard_map/keyvals/pallas_call | solution.py:75
  53.9 0.9 %copy-done.9 = bf16[256,512]{1,0:T(8,128)(2,1)S(1)} copy-done((bf16[256,512]{1,0:T(8,128)(2,1)S(1)}, bf16[256,512]{1,0:T(8,128)(2,1)}, u32[]{:S(2)}) %copy-start.9) | copy-done | bytes 262168
  54.8 0.9 %copy-done.13 = bf16[256,512]{1,0:T(8,128)(2,1)S(1)} copy-done((bf16[256,512]{1,0:T(8,128)(2,1)S(1)}, bf16[256,512]{1,0:T(8,128)(2,1)}, u32[]{:S(2)}) %copy-start.13) | copy-done | bytes 262168
  55.8 0.9 %keyvals.8.refs_2_ = bf16[512,1024]{1,0:T(8,128)(2,1)S(1)} custom-call(bf16[256,512]{1,0:T(8,128)(2,1)S(1)} %copy-done.9, bf16[256,512]{1,0:T(8,128)(2,1)S(1)} %copy-done.13, bf16[512,1536]{1,0:T(8,128)(2,1)S(1)} %copy-done.1), custom_call_target="tpu_custom_call" | custom-call | flops 536870912 | bytes 1572864 | tf_op jit(solution)/shard_map/keyvals/pallas_call | solution.py:75
  56.7 0.9 %keyvals.7.refs_1_ = bf16[512,1024]{1,0:T(8,128)(2,1)S(1)} custom-call(bf16[256,512]{1,0:T(8,128)(2,1)S(1)} %copy-done.7, bf16[256,512]{1,0:T(8,128)(2,1)S(1)} %copy-done.11, bf16[512,1536]{1,0:T(8,128)(2,1)S(1)} %copy-done.1), custom_call_target="tpu_custom_call" | custom-call | flops 536870912 | bytes 1572864 | tf_op jit(solution)/shard_map/keyvals/pallas_call | solution.py:75
  57.7 0.9 %keyvals.10.refs_4_ = bf16[512,1024]{1,0:T(8,128)(2,1)S(1)} custom-call(bf16[256,512]{1,0:T(8,128)(2,1)S(1)} %collective-permute-done.16.first_ref, bf16[256,512]{1,0:T(8,128)(2,1)S(1)} %collective-permute-done.17.second_ref, bf16[512,1536]{1,0:T(8,128)(2,1)S(1)} %copy-done.1), custom_call_target="tpu_custom_call" | custom-call | flops 536870912 | bytes 1572864 | tf_op jit(solution)/shard_map/keyvals/pallas_call | solution.py:75
  58.7 0.9 %keyvals.9.refs_3_ = bf16[512,1024]{1,0:T(8,128)(2,1)S(1)} custom-call(bf16[256,512]{1,0:T(8,128)(2,1)S(1)} %collective-permute-done.14.first_ref, bf16[256,512]{1,0:T(8,128)(2,1)S(1)} %collective-permute-done.15.second_ref, bf16[512,1536]{1,0:T(8,128)(2,1)S(1)} %copy-done.1), custom_call_target="tpu_custom_call" | custom-call | flops 536870912 | bytes 1572864 | tf_op jit(solution)/shard_map/keyvals/pallas_call | solution.py:75
  59.6 0.9 %keyvals.11.refs_5_ = bf16[512,1024]{1,0:T(8,128)(2,1)S(1)} custom-call(bf16[256,512]{1,0:T(8,128)(2,1)S(1)} %collective-permute-done.18.first_ref, bf16[256,512]{1,0:T(8,128)(2,1)S(1)} %collective-permute-done.19.second_ref, bf16[512,1536]{1,0:T(8,128)(2,1)S(1)} %copy-done.1), custom_call_target="tpu_custom_call" | custom-call | flops 536870912 | bytes 1572864 | tf_op jit(solution)/shard_map/keyvals/pallas_call | solution.py:75
  60.6 7.7 %finish.1 = bf16[256,512]{1,0:T(8,128)(2,1)} custom-call(s32[25]{0:T(128)S(1)} %pad_add_fusion.1.plan_ref, bf16[256,512]{1,0:T(8,128)(2,1)S(1)} %copy-done.3, bf16[256,512]{1,0:T(8,128)(2,1)S(1)} %get-tuple-element.10.query_ref, bf16[256,512]{1,0:T(8,128)(2,1)S(1)} %pad_maximum_fusion.hub_a_ref, bf16[256,512]{1,0:T(8,128)(2,1)S(1)} %collective-permute-done.13.hub_b_ref, ...), custom_call_target="tpu_custom_call" | custom-call | tf_op jit(solution)/shard_map/finish/pallas_call | solution.py:228
  (58 shorter events, 0.8 us)
Async XLA Ops:
  0.0 53.9 %copy-start.1 = (bf16[512,1536]{1,0:T(8,128)(2,1)S(1)}, bf16[512,1536]{1,0:T(8,128)(2,1)}, u32[]{:S(2)}) copy-start(bf16[512,1536]{1,0:T(8,128)(2,1)} %w_qkv_ref.1) | copy-start | bytes 4718596
  0.0 9.4 %collective-permute-start.2 = (bf16[256,512]{1,0:T(8,128)(2,1)}, bf16[256,512]{1,0:T(8,128)(2,1)S(1)}, u32[]{:S(2)}, u32[]{:S(2)}) collective-permute-start(bf16[256,512]{1,0:T(8,128)(2,1)} %tokens_ref.1), channel_id=1, source_target_pairs={{0,2},{1,3},{2,0},{3,1},{4,6},{5,7},{6,4},{7,5},{8,10},{9,11},{10,... | collective-permute-start | bytes 786440 | tf_op jit(solution)/shard_map/ppermute | solution.py:24
  1.2 8.1 %collective-permute-start.1 = (bf16[256,512]{1,0:T(8,128)(2,1)}, bf16[256,512]{1,0:T(8,128)(2,1)S(1)}, u32[]{:S(2)}, u32[]{:S(2)}) collective-permute-start(bf16[256,512]{1,0:T(8,128)(2,1)} %tokens_ref.1), channel_id=1, source_target_pairs={{0,4},{1,5},{2,6},{3,7},{4,0},{5,1},{6,2},{7,3},{8,12},{9,13},{10,... | collective-permute-start | bytes 786440 | tf_op jit(solution)/shard_map/ppermute | solution.py:24
  2.5 13.3 %collective-permute-start = (bf16[256,512]{1,0:T(8,128)(2,1)}, bf16[256,512]{1,0:T(8,128)(2,1)S(1)}, u32[]{:S(2)}, u32[]{:S(2)}) collective-permute-start(bf16[256,512]{1,0:T(8,128)(2,1)} %tokens_ref.1), channel_id=1, source_target_pairs={{0,1},{1,0},{2,3},{3,2},{4,5},{5,4},{6,7},{7,6},{8,9},{9,8},{10,11... | collective-permute-start | bytes 786440 | tf_op jit(solution)/shard_map/ppermute | solution.py:24
  4.5 4.8 %collective-permute-start.3 = (bf16[64,512]{1,0:T(8,128)(2,1)S(1)}, bf16[64,512]{1,0:T(8,128)(2,1)S(1)}, u32[]{:S(2)}, u32[]{:S(2)}) collective-permute-start(bf16[64,512]{1,0:T(8,128)(2,1)S(1)} %bitcast.10), channel_id=1, source_target_pairs={{0,6},{1,7},{2,4},{3,5},{4,2},{5,3},{6,0},{7,1},{8,14},{9,15},{10,... | collective-permute-start | bytes 196616 | tf_op jit(solution)/shard_map/ppermute | solution.py:24
  9.4 6.7 %copy-start.17 = (bf16[64,512]{1,0:T(8,128)(2,1)}, bf16[64,512]{1,0:T(8,128)(2,1)S(1)}, u32[]{:S(2)}) copy-start(bf16[64,512]{1,0:T(8,128)(2,1)S(1)} %collective-permute-done.3.refs_6_) | copy-start | bytes 196612
  9.4 6.7 %copy-start.6 = (bf16[256,512]{1,0:T(8,128)(2,1)}, bf16[256,512]{1,0:T(8,128)(2,1)S(1)}, u32[]{:S(2)}) copy-start(bf16[256,512]{1,0:T(8,128)(2,1)S(1)} %collective-permute-done.2.refs_2_.first_ref) | copy-start | bytes 786436
  9.4 6.7 %copy-start.8 = (bf16[256,512]{1,0:T(8,128)(2,1)}, bf16[256,512]{1,0:T(8,128)(2,1)S(1)}, u32[]{:S(2)}) copy-start(bf16[256,512]{1,0:T(8,128)(2,1)S(1)} %collective-permute-done.1.refs_4_.first_ref) | copy-start | bytes 786436
  9.4 6.6 %collective-permute-start.4 = (bf16[256,512]{1,0:T(8,128)(2,1)S(1)}, bf16[256,512]{1,0:T(8,128)(2,1)S(1)}, u32[]{:S(2)}, u32[]{:S(2)}) collective-permute-start(bf16[256,512]{1,0:T(8,128)(2,1)S(1)} %collective-permute-done.2.refs_2_.first_ref), channel_id=1, source_target_pairs={{0,1},{1,0},{2,3},{3,2},{4,5},{5,4},{6,7},{7,6},{8,9},{9,8},{10,11... | collective-permute-start | bytes 786440 | tf_op jit(solution)/shard_map/ppermute | solution.py:24
  11.6 4.4 %collective-permute-start.5 = (bf16[256,512]{1,0:T(8,128)(2,1)S(1)}, bf16[256,512]{1,0:T(8,128)(2,1)S(1)}, u32[]{:S(2)}, u32[]{:S(2)}) collective-permute-start(bf16[256,512]{1,0:T(8,128)(2,1)S(1)} %collective-permute-done.1.refs_4_.first_ref), channel_id=1, source_target_pairs={{0,1},{1,0},{2,3},{3,2},{4,5},{5,4},{6,7},{7,6},{8,9},{9,8},{10,11... | collective-permute-start | bytes 786440 | tf_op jit(solution)/shard_map/ppermute | solution.py:24
  11.7 11.8 %collective-permute-start.14 = (bf16[256,512]{1,0:T(8,128)(2,1)S(1)}, bf16[256,512]{1,0:T(8,128)(2,1)S(1)}, u32[]{:S(2)}, u32[]{:S(2)}) collective-permute-start(bf16[256,512]{1,0:T(8,128)(2,1)S(1)} %collective-permute-done.2.refs_2_.first_ref), channel_id=1, source_target_pairs={{0,4},{1,5},{2,6},{3,7},{4,0},{5,1},{6,2},{7,3},{8,12},{9,13},{10,... | collective-permute-start | bytes 786440 | tf_op jit(solution)/shard_map/ppermute | solution.py:24
  14.4 1.6 %collective-permute-start.6 = (bf16[64,512]{1,0:T(8,128)(2,1)S(1)}, bf16[64,512]{1,0:T(8,128)(2,1)S(1)}, u32[]{:S(2)}, u32[]{:S(2)}) collective-permute-start(bf16[64,512]{1,0:T(8,128)(2,1)S(1)} %collective-permute-done.3.refs_6_), channel_id=1, source_target_pairs={{0,1},{1,0},{2,3},{3,2},{4,5},{5,4},{6,7},{7,6},{8,9},{9,8},{10,11... | collective-permute-start | bytes 196616 | tf_op jit(solution)/shard_map/ppermute | solution.py:24
  15.8 0.7 %copy-start.14 = (bf16[256,512]{1,0:T(8,128)(2,1)}, bf16[256,512]{1,0:T(8,128)(2,1)S(1)}, u32[]{:S(2)}) copy-start(bf16[256,512]{1,0:T(8,128)(2,1)S(1)} %collective-permute-done.second_ref.refs_1_) | copy-start | bytes 786436
  16.0 0.6 copy-start.18
  16.0 0.7 %copy-start.10 = (bf16[256,512]{1,0:T(8,128)(2,1)}, bf16[256,512]{1,0:T(8,128)(2,1)S(1)}, u32[]{:S(2)}) copy-start(bf16[256,512]{1,0:T(8,128)(2,1)S(1)} %collective-permute-done.4.refs_3_.second_ref) | copy-start | bytes 786436
  16.7 0.7 %copy-start.12 = (bf16[256,512]{1,0:T(8,128)(2,1)}, bf16[256,512]{1,0:T(8,128)(2,1)S(1)}, u32[]{:S(2)}) copy-start(bf16[256,512]{1,0:T(8,128)(2,1)S(1)} %collective-permute-done.5.refs_5_.second_ref) | copy-start | bytes 786436
  18.9 37.8 %copy-start.7 = (bf16[256,512]{1,0:T(8,128)(2,1)S(1)}, bf16[256,512]{1,0:T(8,128)(2,1)}, u32[]{:S(2)}) copy-start(bf16[256,512]{1,0:T(8,128)(2,1)} %copy-done.6) | copy-start | bytes 786436
  18.9 37.8 %copy-start.11 = (bf16[256,512]{1,0:T(8,128)(2,1)S(1)}, bf16[256,512]{1,0:T(8,128)(2,1)}, u32[]{:S(2)}) copy-start(bf16[256,512]{1,0:T(8,128)(2,1)} %copy-done.10) | copy-start | bytes 786436
  18.9 6.9 %collective-permute-start.9 = (bf16[64,512]{1,0:T(8,128)(2,1)}, bf16[64,512]{1,0:T(8,128)(2,1)S(1)}, u32[]{:S(2)}, u32[]{:S(2)}) collective-permute-start(bf16[64,512]{1,0:T(8,128)(2,1)} %pick_pieces.1), channel_id=1, source_target_pairs={{0,8},{1,9},{2,10},{3,11},{4,12},{5,13},{6,14},{7,15},{8,0},{9,1},... | collective-permute-start | bytes 196616 | tf_op jit(solution)/shard_map/ppermute | solution.py:24
  19.8 6.0 %collective-permute-start.8 = (bf16[64,512]{1,0:T(8,128)(2,1)}, bf16[64,512]{1,0:T(8,128)(2,1)S(1)}, u32[]{:S(2)}, u32[]{:S(2)}) collective-permute-start(bf16[64,512]{1,0:T(8,128)(2,1)} %pick_pieces.1), channel_id=1, source_target_pairs={{0,16},{1,17},{2,18},{3,19},{4,20},{5,21},{6,22},{7,23},{8,24},{9,... | collective-permute-start | bytes 196616 | tf_op jit(solution)/shard_map/ppermute | solution.py:24
  22.0 18.1 %collective-permute-start.7 = (bf16[64,512]{1,0:T(8,128)(2,1)}, bf16[64,512]{1,0:T(8,128)(2,1)S(1)}, u32[]{:S(2)}, u32[]{:S(2)}) collective-permute-start(bf16[64,512]{1,0:T(8,128)(2,1)} %pick_pieces.1), channel_id=1, source_target_pairs={{0,24},{1,25},{2,26},{3,27},{4,28},{5,29},{6,30},{7,31},{8,16},{9,... | collective-permute-start | bytes 196616 | tf_op jit(solution)/shard_map/ppermute | solution.py:24
  22.2 21.6 %collective-permute-start.16 = (bf16[256,512]{1,0:T(8,128)(2,1)}, bf16[256,512]{1,0:T(8,128)(2,1)S(1)}, u32[]{:S(2)}, u32[]{:S(2)}) collective-permute-start(bf16[256,512]{1,0:T(8,128)(2,1)} %copy-done.8), channel_id=1, source_target_pairs={{0,8},{1,9},{2,10},{3,11},{4,28},{5,29},{6,30},{7,31},{8,16},{9,17... | collective-permute-start | bytes 786440 | tf_op jit(solution)/shard_map/ppermute | solution.py:24
  23.5 23.8 %collective-permute-start.18 = (bf16[256,512]{1,0:T(8,128)(2,1)S(1)}, bf16[256,512]{1,0:T(8,128)(2,1)S(1)}, u32[]{:S(2)}, u32[]{:S(2)}) collective-permute-start(bf16[256,512]{1,0:T(8,128)(2,1)S(1)} %collective-permute-done.14.first_ref), channel_id=1, source_target_pairs={{0,8},{1,9},{2,10},{3,11},{4,28},{5,29},{6,30},{7,31},{8,16},{9,17... | collective-permute-start | bytes 786440 | tf_op jit(solution)/shard_map/ppermute | solution.py:24
  41.0 4.5 %collective-permute-start.12 = (bf16[64,512]{1,0:T(8,128)(2,1)S(1)}, bf16[64,512]{1,0:T(8,128)(2,1)S(1)}, u32[]{:S(2)}, u32[]{:S(2)}) collective-permute-start(bf16[64,512]{1,0:T(8,128)(2,1)S(1)} %select_select_fusion), channel_id=1, source_target_pairs={{0,6},{1,7},{2,4},{3,5},{4,2},{5,3},{6,0},{7,1},{8,14},{9,15},{10,... | collective-permute-start | bytes 196616 | tf_op jit(solution)/shard_map/ppermute | solution.py:24
  41.1 6.2 %collective-permute-start.11 = (bf16[64,512]{1,0:T(8,128)(2,1)S(1)}, bf16[64,512]{1,0:T(8,128)(2,1)S(1)}, u32[]{:S(2)}, u32[]{:S(2)}) collective-permute-start(bf16[64,512]{1,0:T(8,128)(2,1)S(1)} %select_select_fusion), channel_id=1, source_target_pairs={{0,4},{1,5},{2,6},{3,7},{4,0},{5,1},{6,2},{7,3},{8,12},{9,13},{10,... | collective-permute-start | bytes 196616 | tf_op jit(solution)/shard_map/ppermute | solution.py:24
  43.5 4.0 %collective-permute-start.10 = (bf16[64,512]{1,0:T(8,128)(2,1)S(1)}, bf16[64,512]{1,0:T(8,128)(2,1)S(1)}, u32[]{:S(2)}, u32[]{:S(2)}) collective-permute-start(bf16[64,512]{1,0:T(8,128)(2,1)S(1)} %select_select_fusion), channel_id=1, source_target_pairs={{0,2},{1,3},{2,0},{3,1},{4,6},{5,7},{6,4},{7,5},{8,10},{9,11},{10,... | collective-permute-start | bytes 196616 | tf_op jit(solution)/shard_map/ppermute | solution.py:24
  43.8 14.8 %collective-permute-start.15 = (bf16[256,512]{1,0:T(8,128)(2,1)S(1)}, bf16[256,512]{1,0:T(8,128)(2,1)S(1)}, u32[]{:S(2)}, u32[]{:S(2)}) collective-permute-start(bf16[256,512]{1,0:T(8,128)(2,1)S(1)} %collective-permute-done.14.first_ref), channel_id=1, source_target_pairs={{0,1},{1,0},{2,3},{3,2},{4,5},{5,4},{6,7},{7,6},{8,9},{9,8},{10,11... | collective-permute-start | bytes 786440 | tf_op jit(solution)/shard_map/ppermute | solution.py:24
  45.6 12.1 %collective-permute-start.17 = (bf16[256,512]{1,0:T(8,128)(2,1)S(1)}, bf16[256,512]{1,0:T(8,128)(2,1)S(1)}, u32[]{:S(2)}, u32[]{:S(2)}) collective-permute-start(bf16[256,512]{1,0:T(8,128)(2,1)S(1)} %collective-permute-done.16.first_ref), channel_id=1, source_target_pairs={{0,1},{1,0},{2,3},{3,2},{4,5},{5,4},{6,7},{7,6},{8,9},{9,8},{10,11... | collective-permute-start | bytes 786440 | tf_op jit(solution)/shard_map/ppermute | solution.py:24
  47.3 12.3 %collective-permute-start.19 = (bf16[256,512]{1,0:T(8,128)(2,1)S(1)}, bf16[256,512]{1,0:T(8,128)(2,1)S(1)}, u32[]{:S(2)}, u32[]{:S(2)}) collective-permute-start(bf16[256,512]{1,0:T(8,128)(2,1)S(1)} %collective-permute-done.18.first_ref), channel_id=1, source_target_pairs={{0,1},{1,0},{2,3},{3,2},{4,5},{5,4},{6,7},{7,6},{8,9},{9,8},{10,11... | collective-permute-start | bytes 786440 | tf_op jit(solution)/shard_map/ppermute | solution.py:24
  47.5 13.0 %collective-permute-start.13 = (bf16[256,512]{1,0:T(8,128)(2,1)S(1)}, bf16[256,512]{1,0:T(8,128)(2,1)S(1)}, u32[]{:S(2)}, u32[]{:S(2)}) collective-permute-start(bf16[256,512]{1,0:T(8,128)(2,1)S(1)} %pad_maximum_fusion.hub_a_ref), channel_id=1, source_target_pairs={{0,1},{1,0},{2,3},{3,2},{4,5},{5,4},{6,7},{7,6},{8,9},{9,8},{10,11... | collective-permute-start | bytes 786440 | tf_op jit(solution)/shard_map/ppermute | solution.py:24
  49.3 1.4 %copy-start = (bf16[512,1536]{1,0:T(8,128)(2,1)S(1)}, bf16[512,1536]{1,0:T(8,128)(2,1)}, u32[]{:S(2)}) copy-start(bf16[512,1536]{1,0:T(8,128)(2,1)} %w_qkv_ref.1) | copy-start | bytes 4718596
  50.7 0.9 %copy-start.2 = (bf16[256,512]{1,0:T(8,128)(2,1)S(1)}, bf16[256,512]{1,0:T(8,128)(2,1)}, u32[]{:S(2)}) copy-start(bf16[256,512]{1,0:T(8,128)(2,1)} %tokens_ref.1) | copy-start | bytes 786436
  51.7 0.9 %copy-start.15 = (bf16[256,512]{1,0:T(8,128)(2,1)S(1)}, bf16[256,512]{1,0:T(8,128)(2,1)}, u32[]{:S(2)}) copy-start(bf16[256,512]{1,0:T(8,128)(2,1)} %copy-done.14) | copy-start | bytes 786436
  53.9 1.0 %copy-start.9 = (bf16[256,512]{1,0:T(8,128)(2,1)S(1)}, bf16[256,512]{1,0:T(8,128)(2,1)}, u32[]{:S(2)}) copy-start(bf16[256,512]{1,0:T(8,128)(2,1)} %copy-done.8) | copy-start | bytes 786436
  54.8 0.9 %copy-start.13 = (bf16[256,512]{1,0:T(8,128)(2,1)S(1)}, bf16[256,512]{1,0:T(8,128)(2,1)}, u32[]{:S(2)}) copy-start(bf16[256,512]{1,0:T(8,128)(2,1)} %copy-done.12) | copy-start | bytes 786436
  57.6 2.9 %copy-start.3 = (bf16[256,512]{1,0:T(8,128)(2,1)S(1)}, bf16[256,512]{1,0:T(8,128)(2,1)}, u32[]{:S(2)}) copy-start(bf16[256,512]{1,0:T(8,128)(2,1)} %tokens_ref.1) | copy-start | bytes 786436
  57.7 2.9 %copy-start.4 = (bf16[512,1024]{1,0:T(8,128)(2,1)S(1)}, bf16[512,1024]{1,0:T(8,128)(2,1)}, u32[]{:S(2)}) copy-start(bf16[512,1024]{1,0:T(8,128)(2,1)} %w_up_ref.1) | copy-start | bytes 3145732
  57.7 2.9 %copy-start.5 = (bf16[1024,512]{1,0:T(8,128)(2,1)S(1)}, bf16[1024,512]{1,0:T(8,128)(2,1)}, u32[]{:S(2)}) copy-start(bf16[1024,512]{1,0:T(8,128)(2,1)} %w_down_ref.1) | copy-start | bytes 3145732
  57.7 2.9 %copy-start.16 = (bf16[512,512]{1,0:T(8,128)(2,1)S(1)}, bf16[512,512]{1,0:T(8,128)(2,1)}, u32[]{:S(2)}) copy-start(bf16[512,512]{1,0:T(8,128)(2,1)} %w_out_ref.1) | copy-start | bytes 1572868

commit v2 on v1

v2 whole, which is shorter than its diff:
```python
import functools

import jax
import jax.numpy as jnp
from jax import lax
from jax.experimental import pallas as pl
from jax.experimental.pallas import tpu as pltpu
from jax.sharding import PartitionSpec as P

TB = 128
PIECES = 8
PIECE = TB // PIECES
AXES = ("nodes", "heads")
ANY = pl.BlockSpec(memory_space=pl.ANY)
VMEM = pl.BlockSpec(memory_space=pltpu.VMEM)


def send(value, nodes, heads, where):
    pairs = []
    for n in range(nodes):
        for h in range(heads):
            to_n, to_h = where(n, h)
            pairs.append((n * heads + h, to_n % nodes * heads + to_h))
    return lax.ppermute(value, AXES, pairs)


def layer_norm(value_rows):
    mean = jnp.mean(value_rows, axis=-1, keepdims=True)
    centered = value_rows - mean
    spread = jnp.mean(centered * centered, axis=-1, keepdims=True)
    return (centered * lax.rsqrt(spread + 1e-05)).astype(jnp.bfloat16)


def project(normed, w_ref, cols):
    return jnp.dot(normed, w_ref[:, cols], preferred_element_type=jnp.float32).astype(
        jnp.bfloat16
    )


def keyval_into(out_ref, rows, normed, w_ref, heads, head_dim):
    width = heads * head_dim
    if head_dim % 128 == 0:
        for h in range(heads):
            both = project(normed, w_ref, slice((3 * h + 1) * head_dim, (3 * h + 3) * head_dim))
            out_ref[rows, h * head_dim : (h + 1) * head_dim] = both[:, :head_dim]
            out_ref[rows, width + h * head_dim : width + (h + 1) * head_dim] = both[:, head_dim:]
    else:
        out_ref[rows, :] = project(normed, w_ref, slice(width, 3 * width))


def query_into(out_ref, normed, w_ref, heads, head_dim):
    if head_dim % 128 == 0:
        for h in range(heads):
            out_ref[:, h * head_dim : (h + 1) * head_dim] = project(
                normed, w_ref, slice(3 * h * head_dim, (3 * h + 1) * head_dim)
            )
    else:
        out_ref[...] = project(normed, w_ref, slice(0, heads * head_dim))


def keyval_kernel(heads, head_dim, node_dev, first_ref, second_ref, w_ref, out_ref, *query_ref):
    for at, ref in enumerate((first_ref, second_ref)):
        normed = layer_norm(ref[:node_dev, :].astype(jnp.float32))
        keyval_into(out_ref, slice(at * node_dev, (at + 1) * node_dev), normed, w_ref, heads, head_dim)
        if at == 0 and query_ref:
            query_into(query_ref[0], normed, w_ref, heads, head_dim)


def keyvals(first, second, w_qkv, heads, head_dim, node_dev, with_query=False):
    width = first.shape[1]
    out_shape = [jax.ShapeDtypeStruct((2 * node_dev, 2 * width), jnp.bfloat16)]
    if with_query:
        out_shape.append(jax.ShapeDtypeStruct((node_dev, width), jnp.bfloat16))
    return pl.pallas_call(
        functools.partial(keyval_kernel, heads, head_dim, node_dev),
        out_shape=out_shape,
        in_specs=[VMEM] * 3,
        out_specs=[VMEM] * len(out_shape),
        compiler_params=pltpu.CompilerParams(vmem_limit_bytes=8 << 20),
        cost_estimate=pl.CostEstimate(
            flops=64 * node_dev * width * width, bytes_accessed=6 * width * width, transcendentals=0
        ),
        name="keyvals",
    )(first, second, w_qkv)


def place():
    return lax.axis_index("nodes"), lax.axis_index("heads")


def copy_chosen(code, sources, out_ref, out_rows):
    for k, (ref, row) in enumerate(sources):
        @pl.when(code == k)
        def _():
            rows = pl.ds(pl.multiple_of(row, PIECE), PIECE)
            out_ref[out_rows, :] = ref[rows, :]


def pick_kernel(hub_count, per_group, local, heads, hubs_ref, *refs):
    *sources, piece_ref = refs
    here, head_here = place()
    piece = here % 2 * 4 + head_here % 4
    for j in range(hub_count):
        owner_n = hubs_ref[j] // per_group
        owner_h = hubs_ref[j] % per_group // local
        slot = hubs_ref[j] % local
        far = (owner_n // 2 != here // 2) | (owner_h // 4 != head_here // 4)
        offset = (owner_n + here) % 2 * 4 + ((owner_h % 4) ^ (head_here % 4))
        code = jnp.where(far, -1, offset)
        whole = slot * TB + piece * PIECE
        strip = slot * 2 * PIECE + head_here % 2 * PIECE
        rows = slice(j * PIECE, (j + 1) * PIECE)
        copy_chosen(code, [(ref, whole if k < 6 else strip) for k, ref in enumerate(sources)], piece_ref, rows)

        @pl.when(far)
        def _():
            piece_ref[rows, :] = jnp.zeros((PIECE, piece_ref.shape[1]), piece_ref.dtype)


def pick_pieces(hub_blocks, sources, per_group, heads):
    node_dev, width = sources[0].shape
    hub_count = hub_blocks.shape[0]
    return pl.pallas_call(
        functools.partial(pick_kernel, hub_count, per_group, node_dev // TB, heads),
        out_shape=jax.ShapeDtypeStruct((hub_count * PIECE, width), jnp.bfloat16),
        in_specs=[pl.BlockSpec(memory_space=pltpu.SMEM)] + [VMEM] * 8,
        out_specs=VMEM,
        compiler_params=pltpu.CompilerParams(vmem_limit_bytes=4 << 20),
        name="pick_pieces",
    )(hub_blocks, *sources)


def choose_kernel(hub_count, from_where, hubs_ref, *refs):
    *sources, piece_ref = refs
    here, head_here = place()
    for j in range(hub_count):
        code = from_where(hubs_ref[j], here, head_here)
        rows = slice(j * PIECE, (j + 1) * PIECE)
        copy_chosen(code, [(ref, j * PIECE) for ref in sources], piece_ref, rows)


def choose_pieces(hub_blocks, sources, from_where):
    return pl.pallas_call(
        functools.partial(choose_kernel, hub_blocks.shape[0], from_where),
        out_shape=jax.ShapeDtypeStruct(sources[0].shape, jnp.bfloat16),
        in_specs=[pl.BlockSpec(memory_space=pltpu.SMEM)] + [VMEM] * len(sources),
        out_specs=VMEM,
        compiler_params=pltpu.CompilerParams(vmem_limit_bytes=4 << 20),
        name="choose_pieces",
    )(hub_blocks, *sources)


def final_kernel(
    heads, head_dim, hub_count, per_group, nodes, count,
    cols_ref, tokens_ref, query_ref, mask_ref, w_qkv_ref, w_out_ref, w_up_ref, w_down_ref, *refs
):
    around, refs = refs[:PIECES], refs[PIECES:]
    stores, out_ref = refs[:count], refs[count]
    tile_ref, hub_kv, hub_rows, mask, w_qkv, w_out, w_up, w_down, attn, tile_sem, sem = refs[count + 1 :]
    node_dev, width = tokens_ref.shape
    local = node_dev // TB
    tiles = mask_ref.shape[1]
    slots = local * tiles
    in_store = stores[0].shape[0] // TB
    here, head_here = place()
    hub_base = count * in_store
    indices = []
    for i in range(slots):
        col = cols_ref[head_here * local + i // tiles, i % tiles]
        group, block = col // per_group, col % per_group
        region = jnp.where(group == here, 0, jnp.where(group // 2 == here // 2, 1, 2))
        index = region * per_group + ((block // local) ^ head_here) * local + block % local
        indices.append(jnp.where(col >= nodes * per_group, hub_base + col - nodes * per_group, index))
    loads = [
        pltpu.make_async_copy(w_qkv_ref, w_qkv, sem.at[0]),
        pltpu.make_async_copy(
            mask_ref.at[pl.ds(head_here * local, local)], mask, sem.at[1]
        ),
        pltpu.make_async_copy(w_out_ref, w_out, sem.at[2]),
        pltpu.make_async_copy(w_up_ref, w_up, sem.at[3]),
        pltpu.make_async_copy(w_down_ref, w_down, sem.at[4]),
    ]
    loads[0].start()
    for i in range(slots):
        index = indices[i]
        for a, store in enumerate(stores):
            @pl.when(index // in_store == a)
            def _():
                rows = pl.ds(pl.multiple_of(index % in_store * TB, TB), TB)
                pltpu.make_async_copy(store.at[rows], tile_ref.at[i], tile_sem.at[i]).start()

    for load in loads[1:]:
        load.start()
    mine = here % 2 * 4 + head_here % 4
    for k, ref in enumerate(around):
        for j in range(hub_count):
            row = ref.shape[0] - (hub_count - j) * PIECE
            rows = pl.ds(pl.multiple_of(j * TB + (mine ^ k) * PIECE, PIECE), PIECE)
            hub_rows[rows, :] = ref[row : row + PIECE, :]
    hub_normed = layer_norm(hub_rows[...].astype(jnp.float32))
    loads[0].wait()
    keyval_into(hub_kv, slice(None), hub_normed, w_qkv, heads, head_dim)
    for i in range(slots):
        index = indices[i]

        @pl.when(index >= hub_base)
        def _():
            rows = pl.ds(pl.multiple_of((index - hub_base) * TB, TB), TB)
            pltpu.make_async_copy(hub_kv.at[rows], tile_ref.at[i], tile_sem.at[i]).start()

    loads[1].wait()
    scale = 1.0 / head_dim**0.5
    group = max(head_dim, 128)
    per = group // head_dim
    lane = lax.broadcasted_iota(jnp.int32, (TB, group), 1)
    for r in range(local):
        for t in range(tiles):
            i = r * tiles + t
            pltpu.make_async_copy(hub_kv.at[0:TB], tile_ref.at[i], tile_sem.at[i]).wait()
        edges = jnp.concatenate([mask[r, t].astype(jnp.float32) for t in range(tiles)], axis=1)
        for g in range(heads // per):
            cols = slice(g * group, (g + 1) * group)
            keys = tile_ref[r * tiles : (r + 1) * tiles, :, cols].reshape(tiles * TB, group)
            values = tile_ref[
                r * tiles : (r + 1) * tiles, :, width + g * group : width + (g + 1) * group
            ].reshape(tiles * TB, group)
            query = query_ref[r * TB : (r + 1) * TB, cols]
            result = None
            for s in range(per):
                here = (lane >= s * head_dim) & (lane < (s + 1) * head_dim)
                own = query if per == 1 else jnp.where(here, query.astype(jnp.float32), 0.0).astype(jnp.bfloat16)
                score = lax.dot_general(
                    own, keys, (((1,), (1,)), ((), ())), preferred_element_type=jnp.float32
                )
                weight = jnp.exp(score * scale) * edges
                total = jnp.sum(weight, axis=1, keepdims=True)
                summed = jnp.dot(
                    weight.astype(jnp.bfloat16), values, preferred_element_type=jnp.float32
                )
                one = summed / total
                result = one if result is None else jnp.where(here, one, result)
            attn[r * TB : (r + 1) * TB, cols] = result.astype(jnp.bfloat16)
    loads[2].wait()
    mid = tokens_ref[...].astype(jnp.float32) + jnp.dot(
        attn[...], w_out[...], preferred_element_type=jnp.float32
    )
    normed = layer_norm(mid)
    loads[3].wait()
    up = jnp.dot(normed, w_up[...], preferred_element_type=jnp.float32)
    hidden = (0.5 * up * (1.0 + lax.erf(up * (0.5**0.5)))).astype(jnp.bfloat16)
    loads[4].wait()
    out_ref[...] = (
        mid + jnp.dot(hidden, w_down[...], preferred_element_type=jnp.float32)
    ).astype(jnp.bfloat16)


def finish(cols, tokens, query, mask, w_qkv, w_out, w_up, w_down, around, stores, heads, head_dim, hub_count, nodes):
    node_dev, width = tokens.shape
    local = node_dev // TB
    tiles = mask.shape[1]
    slots = local * tiles
    bf16 = jnp.bfloat16
    return pl.pallas_call(
        functools.partial(final_kernel, heads, head_dim, hub_count, cols.shape[0], nodes, len(stores)),
        out_shape=jax.ShapeDtypeStruct(tokens.shape, bf16),
        in_specs=[pl.BlockSpec(memory_space=pltpu.SMEM)] + [VMEM] * 2 + [ANY] * 5 + [VMEM] * PIECES + [ANY] * len(stores),
        out_specs=VMEM,
        scratch_shapes=[
            pltpu.VMEM((slots, TB, 2 * width), bf16),
            pltpu.VMEM((hub_count * TB, 2 * width), bf16),
            pltpu.VMEM((hub_count * TB, width), bf16),
            pltpu.VMEM((local,) + mask.shape[1:], jnp.int32),
            pltpu.VMEM(w_qkv.shape, bf16),
            pltpu.VMEM(w_out.shape, bf16),
            pltpu.VMEM(w_up.shape, bf16),
            pltpu.VMEM(w_down.shape, bf16),
            pltpu.VMEM((node_dev, width), bf16),
            pltpu.SemaphoreType.DMA((slots,)),
            pltpu.SemaphoreType.DMA((5,)),
        ],
        compiler_params=pltpu.CompilerParams(vmem_limit_bytes=28 << 20),
        name="finish",
    )(cols, tokens, query, mask, w_qkv, w_out, w_up, w_down, *around, *stores)


def body(tokens, w_qkv, w_out, w_up, w_down, tile_cols, tile_mask, hub_blocks):
    node_dev, width = tokens.shape
    nodes = lax.axis_size("nodes")
    heads = lax.axis_size("heads")
    head_dim = width // heads
    per_group = tile_cols.shape[0]
    hub_count = hub_blocks.shape[0]
    local = node_dev // TB
    in_row = heads // 4
    areas = nodes // 2 * in_row
    go = functools.partial(send, nodes=nodes, heads=heads)

    def core(value):
        return go(value, where=lambda n, h: (n, h ^ 1))

    def pair(value):
        return go(value, where=lambda n, h: (n ^ 1, h))

    def across(value):
        return go(value, where=lambda n, h: (n ^ 1, h ^ 2))

    def side(value, offset=2):
        return go(value, where=lambda n, h: (n, h ^ offset))

    def along(value, by=1):
        return go(value, where=lambda n, h: (n + (2 - 4 * (n & 1)) * by, h))

    weights = w_qkv
    if head_dim % 128:
        weights = w_qkv.reshape(width, heads, 3, head_dim).swapaxes(1, 2).reshape(width, 3 * width)
    keyval = functools.partial(keyvals, w_qkv=weights, heads=heads, head_dim=head_dim, node_dev=node_dev)

    other = range(2, heads, 2)
    sides = [side(tokens, o) for o in other]
    paired = pair(tokens)
    here, head_here = place()
    strip_at = ((1 - here % 2) * 4 + ((head_here % 4) ^ 2) // 2 * 2) * PIECE
    strip = lax.dynamic_slice_in_dim(tokens.reshape(local, TB, width), strip_at, 2 * PIECE, 1)
    strip = across(strip.reshape(local * 2 * PIECE, width))
    token_core = core(tokens)
    first, query = keyval(tokens, token_core, with_query=True)
    paired, strip, first, query, *sides = lax.optimization_barrier((paired, strip, first, query, *sides))

    paired_core, strip_core = core(paired), core(strip)
    sides_core = [core(v) for v in sides]
    sources = [tokens, token_core, sides[0], sides_core[0], paired, paired_core, strip, strip_core]
    far = along(paired)
    piece = pick_pieces(hub_blocks, sources, per_group, heads)

    piece, *onward = lax.optimization_barrier((piece, *sides))
    paired_sides = [pair(v) for v in onward]
    stores = [first]
    stores += [keyval(v, c)[0] for v, c in zip(sides, sides_core)]
    stores += list(keyval(paired, paired_core))

    def owner_area(block):
        return block // per_group // 2 * in_row + block % per_group // local // 4

    def area_of(here, head_here):
        return here // 2 * in_row + head_here // 4

    if areas == 4 and in_row == 1:
        got = [piece, along(piece), along(piece, 2), along(piece, -1)]
        got, stores, far = lax.optimization_barrier((got, stores, far))

        def from_where(block, here, head_here):
            ahead = area_of(here, head_here) + 4 - owner_area(block)
            return jnp.where(here % 2 == 0, ahead, 8 - ahead) % 4

        piece = choose_pieces(hub_blocks, got, from_where)
    else:

        def to_area(n, h, shift):
            at = (n // 2 * in_row + h // 4) ^ shift
            return at // in_row * 2 + n % 2, at % in_row * 4 + h % 4

        step = 1
        while step < areas:
            reach = [s * step for s in (1, 2, 3) if s * step < areas]
            got = [go(piece, where=lambda n, h, s=s: to_area(n, h, s)) for s in reach]

            def from_where(block, here, head_here, step=step):
                return (owner_area(block) ^ area_of(here, head_here)) // step % 4

            piece = choose_pieces(hub_blocks, [piece, *got], from_where)
            step *= 4

    far_sides = [side(far, o) for o in other]
    around = [piece, side(piece), pair(piece), across(piece)]
    far_core = core(far)
    paired_sides_core = [core(v) for v in paired_sides]
    stores += [keyval(v, c)[0] for v, c in zip(paired_sides, paired_sides_core)]
    stores += list(keyval(far, far_core))
    around, stores, far_sides = lax.optimization_barrier((around, stores, far_sides))
    far_sides_core = [core(v) for v in far_sides]
    stores += [keyval(v, c)[0] for v, c in zip(far_sides, far_sides_core)]

    around = [v for value in around for v in (value, core(value))]
    return finish(
        tile_cols, tokens, query, tile_mask, weights, w_out, w_up, w_down, around, stores, heads, head_dim, hub_count, nodes
    )


def solution(mesh):
    placed = (
        P(("nodes", "heads"), None),
        P(),
        P(),
        P(),
        P(),
        P("nodes", None),
        P("nodes", None, None, None),
        P(),
    )
    return jax.shard_map(
        body, mesh=mesh, in_specs=placed, out_specs=P(("nodes", "heads"), None), check_vma=False
    )
```

time: 69.4 us -> 51.1 us (0.74)
  the two profiles are of different devices: /device:TPU:9 before, /device:TPU:0 now
where the time goes in v2:
time: 51.1 us; the launch traced here: 50.9 us
  starting transfers between devices  18.6 us (36%)
  Pallas kernels  15.6 us (31%)
  waiting for transfers between devices  13 us (25%)
  local copies, waits for them, and re-layouts  3.28 us (6%)
    ppermute x23, starting transfers between devices, send(): return lax.ppermute(value, AXES, pairs)  18.6 us
    ppermute x23, waiting for transfers between devices, send(): return lax.ppermute(value, AXES, pairs)  13 us
    pallas_call x1, Pallas kernels, finish(): pl.pallas_call(functools.partial(final_kernel, heads, head_dim, hub_count...  8.13 us
    pallas_call x6, Pallas kernels, keyvals(): pl.pallas_call(functools.partial(keyval_kernel, heads, head_dim, node_dev...  5.88 us
    unnamed x20, local copies, waits for them, and re-layouts  2.4 us
  transfers between devices with their start and end apart: 23, of which 8 were waited for; matrix products, arithmetic and copies ran while one was open for 2% of the time, Pallas kernels for 15%

profile of v2, /device:TPU:0, one launch (start us, length us, event | category | flops | bytes accessed | tf_op | source)
XLA Modules:
  0.0 50.9 jit_solution(488514098455055539)
XLA Ops:
  0.0 0.5 collective-permute-start.2
  0.5 2.5 %collective-permute-start = (bf16[256,512]{1,0:T(8,128)(2,1)}, bf16[256,512]{1,0:T(8,128)(2,1)S(1)}, u32[]{:S(2)}, u32[]{:S(2)}) collective-permute-start(bf16[256,512]{1,0:T(8,128)(2,1)} %tokens_ref.1), channel_id=1, source_target_pairs={{0,4},{1,5},{2,6},{3,7},{4,0},{5,1},{6,2},{7,3},{8,12},{9,13},{10,... | collective-permute-start | bytes 786440 | tf_op jit(solution)/shard_map/ppermute | solution.py:24
  2.9 1.5 %collective-permute-start.3 = (bf16[256,512]{1,0:T(8,128)(2,1)}, bf16[256,512]{1,0:T(8,128)(2,1)S(1)}, u32[]{:S(2)}, u32[]{:S(2)}) collective-permute-start(bf16[256,512]{1,0:T(8,128)(2,1)} %tokens_ref.1), channel_id=1, source_target_pairs={{0,2},{1,3},{2,0},{3,1},{4,6},{5,7},{6,4},{7,5},{8,10},{9,11},{10,... | collective-permute-start | bytes 786440 | tf_op jit(solution)/shard_map/ppermute | solution.py:24
  4.5 0.9 %constant_dynamic-slice_fusion = bf16[2,32,512]{2,1,0:T(8,128)(2,1)S(1)} fusion(bf16[2,128,512]{2,1,0:T(8,128)(2,1)} %bitcast.2, s32[]{:T(128)S(6)} %select_n.21), kind=kLoop, calls=%fused_computation | loop fusion | bytes 131076 | tf_op jit(solution)/shard_map/dynamic_slice | solution.py:323
  5.3 0.0 collective-permute-start.1
  5.4 0.0 collective-permute-done.2.second_ref.refs_1_
  5.4 1.4 %copy-done.1 = bf16[512,1536]{1,0:T(8,128)(2,1)S(1)} copy-done((bf16[512,1536]{1,0:T(8,128)(2,1)S(1)}, bf16[512,1536]{1,0:T(8,128)(2,1)}, u32[]{:S(2)}) %copy-start.1) | copy-done | bytes 1572888
  6.8 0.9 %copy-done.3 = bf16[256,512]{1,0:T(8,128)(2,1)S(1)} copy-done((bf16[256,512]{1,0:T(8,128)(2,1)S(1)}, bf16[256,512]{1,0:T(8,128)(2,1)}, u32[]{:S(2)}) %copy-start.3) | copy-done | bytes 262168
  7.8 1.2 %keyvals.6 = (bf16[512,1024]{1,0:T(8,128)(2,1)S(1)}, bf16[256,512]{1,0:T(8,128)(2,1)S(1)}) custom-call(bf16[256,512]{1,0:T(8,128)(2,1)S(1)} %copy-done.3, bf16[256,512]{1,0:T(8,128)(2,1)S(1)} %collective-permute-done.2.second_ref.refs_1_, bf16[512,1536]{1,0:T(8,128)(2,1)S(1)} %copy-done.1), custom_call_target="tpu_custom_call" | custom-call | flops 4294967296 | bytes 1572864 | tf_op jit(solution)/shard_map/keyvals/pallas_call | solution.py:74
  8.9 3.9 %collective-permute-done.1.refs_6_ = bf16[64,512]{1,0:T(8,128)(2,1)S(1)} collective-permute-done((bf16[64,512]{1,0:T(8,128)(2,1)S(1)}, bf16[64,512]{1,0:T(8,128)(2,1)S(1)}, u32[]{:S(2)}, u32[]{:S(2)}) %collective-permute-start.1) | collective-permute-done | bytes 65568 | tf_op jit(solution)/shard_map/ppermute | solution.py:24
  12.8 0.0 collective-permute-done.refs_4_.first_ref
  12.9 0.1 collective-permute-done.3.refs_2_.first_ref
  13.0 0.5 collective-permute-start.4
  13.5 0.0 collective-permute-start.6
  13.5 1.6 %collective-permute-start.10 = (bf16[256,512]{1,0:T(8,128)(2,1)S(1)}, bf16[256,512]{1,0:T(8,128)(2,1)S(1)}, u32[]{:S(2)}, u32[]{:S(2)}) collective-permute-start(bf16[256,512]{1,0:T(8,128)(2,1)S(1)} %collective-permute-done.refs_4_.first_ref), channel_id=1, source_target_pairs={{0,8},{1,9},{2,10},{3,11},{4,28},{5,29},{6,30},{7,31},{8,16},{9,17... | collective-permute-start | bytes 786440 | tf_op jit(solution)/shard_map/ppermute | solution.py:24
  15.1 0.9 %pick_pieces.1.refs_0_ = bf16[64,512]{1,0:T(8,128)(2,1)S(1)} custom-call(s32[4]{0:T(128)S(1)} %copy-done.9, bf16[256,512]{1,0:T(8,128)(2,1)S(1)} %copy-done.3, bf16[256,512]{1,0:T(8,128)(2,1)S(1)} %collective-permute-done.2.second_ref.refs_1_, bf16[256,512]{1,0:T(8,128)(2,1)S(1)} %collective-permute-done.3.refs_2_.first_ref, ...), custom_call_target="tpu_custom_call" | custom-call | tf_op jit(solution)/shard_map/pick_pieces/pallas_call | solution.py:123
  16.0 1.6 %collective-permute-start.7 = (bf16[64,512]{1,0:T(8,128)(2,1)S(1)}, bf16[64,512]{1,0:T(8,128)(2,1)S(1)}, u32[]{:S(2)}, u32[]{:S(2)}) collective-permute-start(bf16[64,512]{1,0:T(8,128)(2,1)S(1)} %pick_pieces.1.refs_0_), channel_id=1, source_target_pairs={{0,8},{1,9},{2,10},{3,11},{4,28},{5,29},{6,30},{7,31},{8,16},{9,17... | collective-permute-start | bytes 196616 | tf_op jit(solution)/shard_map/ppermute | solution.py:24
  17.6 2.5 %collective-permute-start.8 = (bf16[64,512]{1,0:T(8,128)(2,1)S(1)}, bf16[64,512]{1,0:T(8,128)(2,1)S(1)}, u32[]{:S(2)}, u32[]{:S(2)}) collective-permute-start(bf16[64,512]{1,0:T(8,128)(2,1)S(1)} %pick_pieces.1.refs_0_), channel_id=1, source_target_pairs={{0,16},{1,17},{2,18},{3,19},{4,20},{5,21},{6,22},{7,23},{8,24},{9,... | collective-permute-start | bytes 196616 | tf_op jit(solution)/shard_map/ppermute | solution.py:24
  20.1 1.4 %collective-permute-start.9 = (bf16[64,512]{1,0:T(8,128)(2,1)S(1)}, bf16[64,512]{1,0:T(8,128)(2,1)S(1)}, u32[]{:S(2)}, u32[]{:S(2)}) collective-permute-start(bf16[64,512]{1,0:T(8,128)(2,1)S(1)} %pick_pieces.1.refs_0_), channel_id=1, source_target_pairs={{0,24},{1,25},{2,26},{3,27},{4,12},{5,13},{6,14},{7,15},{8,0},{9,1... | collective-permute-start | bytes 196616 | tf_op jit(solution)/shard_map/ppermute | solution.py:24
  21.5 0.2 collective-permute-start.14
  21.8 0.9 %keyvals.8.refs_10_ = bf16[512,1024]{1,0:T(8,128)(2,1)S(1)} custom-call(bf16[256,512]{1,0:T(8,128)(2,1)S(1)} %collective-permute-done.refs_4_.first_ref, bf16[256,512]{1,0:T(8,128)(2,1)S(1)} %collective-permute-done.5.refs_5_.second_ref, bf16[512,1536]{1,0:T(8,128)(2,1)S(1)} %copy-done.2), custom_call_target="tpu_custom_call" | custom-call | flops 4294967296 | bytes 1572864 | tf_op jit(solution)/shard_map/keyvals/pallas_call | solution.py:74
  22.7 0.9 %keyvals.7.refs_9_ = bf16[512,1024]{1,0:T(8,128)(2,1)S(1)} custom-call(bf16[256,512]{1,0:T(8,128)(2,1)S(1)} %collective-permute-done.3.refs_2_.first_ref, bf16[256,512]{1,0:T(8,128)(2,1)S(1)} %collective-permute-done.4.refs_3_.second_ref, bf16[512,1536]{1,0:T(8,128)(2,1)S(1)} %copy-done.2), custom_call_target="tpu_custom_call" | custom-call | flops 4294967296 | bytes 1572864 | tf_op jit(solution)/shard_map/keyvals/pallas_call | solution.py:74
  23.7 0.9 %collective-permute-done.10.first_ref = bf16[256,512]{1,0:T(8,128)(2,1)S(1)} collective-permute-done((bf16[256,512]{1,0:T(8,128)(2,1)S(1)}, bf16[256,512]{1,0:T(8,128)(2,1)S(1)}, u32[]{:S(2)}, u32[]{:S(2)}) %collective-permute-start.10) | collective-permute-done | bytes 262176 | tf_op jit(solution)/shard_map/ppermute | solution.py:24
  24.6 1.3 %collective-permute-done.7.refs_1_ = bf16[64,512]{1,0:T(8,128)(2,1)S(1)} collective-permute-done((bf16[64,512]{1,0:T(8,128)(2,1)S(1)}, bf16[64,512]{1,0:T(8,128)(2,1)S(1)}, u32[]{:S(2)}, u32[]{:S(2)}) %collective-permute-start.7) | collective-permute-done | bytes 65568 | tf_op jit(solution)/shard_map/ppermute | solution.py:24
  25.9 2.5 %collective-permute-done.8.refs_2_ = bf16[64,512]{1,0:T(8,128)(2,1)S(1)} collective-permute-done((bf16[64,512]{1,0:T(8,128)(2,1)S(1)}, bf16[64,512]{1,0:T(8,128)(2,1)S(1)}, u32[]{:S(2)}, u32[]{:S(2)}) %collective-permute-start.8) | collective-permute-done | bytes 65568 | tf_op jit(solution)/shard_map/ppermute | solution.py:24
  28.4 1.5 %collective-permute-start.17 = (bf16[256,512]{1,0:T(8,128)(2,1)S(1)}, bf16[256,512]{1,0:T(8,128)(2,1)S(1)}, u32[]{:S(2)}, u32[]{:S(2)}) collective-permute-start(bf16[256,512]{1,0:T(8,128)(2,1)S(1)} %collective-permute-done.10.first_ref), channel_id=1, source_target_pairs={{0,2},{1,3},{2,0},{3,1},{4,6},{5,7},{6,4},{7,5},{8,10},{9,11},{10,... | collective-permute-start | bytes 786440 | tf_op jit(solution)/shard_map/ppermute | solution.py:24
  30.0 0.7 %choose_pieces.1.refs_0_ = bf16[64,512]{1,0:T(8,128)(2,1)S(1)} custom-call(s32[4]{0:T(128)S(1)} %copy-done.9, bf16[64,512]{1,0:T(8,128)(2,1)S(1)} %pick_pieces.1.refs_0_, bf16[64,512]{1,0:T(8,128)(2,1)S(1)} %collective-permute-done.7.refs_1_, bf16[64,512]{1,0:T(8,128)(2,1)S(1)} %collective-permute-done.8.refs_2_, ...), custom_call_target="tpu_custom_call" | custom-call | tf_op jit(solution)/shard_map/choose_pieces/pallas_call | solution.py:143
  30.7 0.6 %collective-permute-start.11 = (bf16[64,512]{1,0:T(8,128)(2,1)S(1)}, bf16[64,512]{1,0:T(8,128)(2,1)S(1)}, u32[]{:S(2)}, u32[]{:S(2)}) collective-permute-start(bf16[64,512]{1,0:T(8,128)(2,1)S(1)} %choose_pieces.1.refs_0_), channel_id=1, source_target_pairs={{0,2},{1,3},{2,0},{3,1},{4,6},{5,7},{6,4},{7,5},{8,10},{9,11},{10,... | collective-permute-start | bytes 196616 | tf_op jit(solution)/shard_map/ppermute | solution.py:24
  31.3 1.7 %collective-permute-start.12 = (bf16[64,512]{1,0:T(8,128)(2,1)S(1)}, bf16[64,512]{1,0:T(8,128)(2,1)S(1)}, u32[]{:S(2)}, u32[]{:S(2)}) collective-permute-start(bf16[64,512]{1,0:T(8,128)(2,1)S(1)} %choose_pieces.1.refs_0_), channel_id=1, source_target_pairs={{0,4},{1,5},{2,6},{3,7},{4,0},{5,1},{6,2},{7,3},{8,12},{9,13},{10,... | collective-permute-start | bytes 196616 | tf_op jit(solution)/shard_map/ppermute | solution.py:24
  33.0 1.3 %collective-permute-start.13 = (bf16[64,512]{1,0:T(8,128)(2,1)S(1)}, bf16[64,512]{1,0:T(8,128)(2,1)S(1)}, u32[]{:S(2)}, u32[]{:S(2)}) collective-permute-start(bf16[64,512]{1,0:T(8,128)(2,1)S(1)} %choose_pieces.1.refs_0_), channel_id=1, source_target_pairs={{0,6},{1,7},{2,4},{3,5},{4,2},{5,3},{6,0},{7,1},{8,14},{9,15},{10,... | collective-permute-start | bytes 196616 | tf_op jit(solution)/shard_map/ppermute | solution.py:24
  34.3 0.9 %keyvals.10.refs_12_ = bf16[512,1024]{1,0:T(8,128)(2,1)S(1)} custom-call(bf16[256,512]{1,0:T(8,128)(2,1)S(1)} %collective-permute-done.10.first_ref, bf16[256,512]{1,0:T(8,128)(2,1)S(1)} %collective-permute-done.16.second_ref, bf16[512,1536]{1,0:T(8,128)(2,1)S(1)} %copy-done.2), custom_call_target="tpu_custom_call" | custom-call | flops 4294967296 | bytes 1572864 | tf_op jit(solution)/shard_map/keyvals/pallas_call | solution.py:74
  35.2 0.6 %collective-permute-done.15.second_ref = bf16[256,512]{1,0:T(8,128)(2,1)S(1)} collective-permute-done((bf16[256,512]{1,0:T(8,128)(2,1)S(1)}, bf16[256,512]{1,0:T(8,128)(2,1)S(1)}, u32[]{:S(2)}, u32[]{:S(2)}) %collective-permute-start.15) | collective-permute-done | bytes 262176 | tf_op jit(solution)/shard_map/ppermute | solution.py:24
  35.8 0.9 %keyvals.9.refs_11_ = bf16[512,1024]{1,0:T(8,128)(2,1)S(1)} custom-call(bf16[256,512]{1,0:T(8,128)(2,1)S(1)} %collective-permute-done.14.first_ref, bf16[256,512]{1,0:T(8,128)(2,1)S(1)} %collective-permute-done.15.second_ref, bf16[512,1536]{1,0:T(8,128)(2,1)S(1)} %copy-done.2), custom_call_target="tpu_custom_call" | custom-call | flops 4294967296 | bytes 1572864 | tf_op jit(solution)/shard_map/keyvals/pallas_call | solution.py:74
  36.8 0.0 copy-start
  36.8 0.0 copy-start.4
  36.8 0.0 copy-start.5
  36.8 0.0 copy-start.6
  36.8 0.0 copy-start.7
  36.8 0.0 copy-start.8
  36.8 3.1 %collective-permute-done.11.refs_2_ = bf16[64,512]{1,0:T(8,128)(2,1)S(1)} collective-permute-done((bf16[64,512]{1,0:T(8,128)(2,1)S(1)}, bf16[64,512]{1,0:T(8,128)(2,1)S(1)}, u32[]{:S(2)}, u32[]{:S(2)}) %collective-permute-start.11) | collective-permute-done | bytes 65568 | tf_op jit(solution)/shard_map/ppermute | solution.py:24
  40.0 0.1 collective-permute-start.22
  40.1 0.5 collective-permute-start.18
  40.6 0.1 collective-permute-start.19
  40.6 0.4 collective-permute-start.20
  41.1 0.1 collective-permute-start.21
  41.2 0.4 collective-permute-done.22.second_ref
  41.6 0.9 %keyvals.11.refs_13_ = bf16[512,1024]{1,0:T(8,128)(2,1)S(1)} custom-call(bf16[256,512]{1,0:T(8,128)(2,1)S(1)} %collective-permute-done.17.first_ref, bf16[256,512]{1,0:T(8,128)(2,1)S(1)} %collective-permute-done.22.second_ref, bf16[512,1536]{1,0:T(8,128)(2,1)S(1)} %copy-done.2), custom_call_target="tpu_custom_call" | custom-call | flops 4294967296 | bytes 1572864 | tf_op jit(solution)/shard_map/keyvals/pallas_call | solution.py:74
  42.6 8.1 %finish.1 = bf16[256,512]{1,0:T(8,128)(2,1)} custom-call(s32[8,8]{1,0:T(8,128)S(1)} %copy-done.8, bf16[256,512]{1,0:T(8,128)(2,1)S(1)} %copy-done.4, bf16[256,512]{1,0:T(8,128)(2,1)S(1)} %get-tuple-element.34.query_ref, s32[8,8,128,128]{3,2,1,0:T(8,128)S(1)} %copy-done, bf16[512,1536]{1,0:T(8,128)(2,1)S(1)} %copy-done.2, bf16[512,512]{1,0:T(8,128)(2,1)S(1)} %copy-done.7, ...), custom_call_target="tpu_custom_call" | custom-call | tf_op jit(solution)/shard_map/finish/pallas_call | solution.py:263
  (28 shorter events, 0.1 us)
Async XLA Ops:
  0.0 5.4 %collective-permute-start.2 = (bf16[256,512]{1,0:T(8,128)(2,1)}, bf16[256,512]{1,0:T(8,128)(2,1)S(1)}, u32[]{:S(2)}, u32[]{:S(2)}) collective-permute-start(bf16[256,512]{1,0:T(8,128)(2,1)} %tokens_ref.1), channel_id=1, source_target_pairs={{0,1},{1,0},{2,3},{3,2},{4,5},{5,4},{6,7},{7,6},{8,9},{9,8},{10,11... | collective-permute-start | bytes 786440 | tf_op jit(solution)/shard_map/ppermute | solution.py:24
  0.5 12.4 %collective-permute-start = (bf16[256,512]{1,0:T(8,128)(2,1)}, bf16[256,512]{1,0:T(8,128)(2,1)S(1)}, u32[]{:S(2)}, u32[]{:S(2)}) collective-permute-start(bf16[256,512]{1,0:T(8,128)(2,1)} %tokens_ref.1), channel_id=1, source_target_pairs={{0,4},{1,5},{2,6},{3,7},{4,0},{5,1},{6,2},{7,3},{8,12},{9,13},{10,... | collective-permute-start | bytes 786440 | tf_op jit(solution)/shard_map/ppermute | solution.py:24
  2.9 10.1 %collective-permute-start.3 = (bf16[256,512]{1,0:T(8,128)(2,1)}, bf16[256,512]{1,0:T(8,128)(2,1)S(1)}, u32[]{:S(2)}, u32[]{:S(2)}) collective-permute-start(bf16[256,512]{1,0:T(8,128)(2,1)} %tokens_ref.1), channel_id=1, source_target_pairs={{0,2},{1,3},{2,0},{3,1},{4,6},{5,7},{6,4},{7,5},{8,10},{9,11},{10,... | collective-permute-start | bytes 786440 | tf_op jit(solution)/shard_map/ppermute | solution.py:24
  5.3 9.8 %copy-start.9 = (s32[4]{0:T(128)S(1)}, s32[4]{0:T(128)}, u32[]{:S(2)}) copy-start(s32[4]{0:T(128)} %hubs_ref.3) | copy-start | bytes 52
  5.3 7.5 %collective-permute-start.1 = (bf16[64,512]{1,0:T(8,128)(2,1)S(1)}, bf16[64,512]{1,0:T(8,128)(2,1)S(1)}, u32[]{:S(2)}, u32[]{:S(2)}) collective-permute-start(bf16[64,512]{1,0:T(8,128)(2,1)S(1)} %bitcast.3), channel_id=1, source_target_pairs={{0,6},{1,7},{2,4},{3,5},{4,2},{5,3},{6,0},{7,1},{8,14},{9,15},{10,... | collective-permute-start | bytes 196616 | tf_op jit(solution)/shard_map/ppermute | solution.py:24
  5.4 1.4 %copy-start.1 = (bf16[512,1536]{1,0:T(8,128)(2,1)S(1)}, bf16[512,1536]{1,0:T(8,128)(2,1)}, u32[]{:S(2)}) copy-start(bf16[512,1536]{1,0:T(8,128)(2,1)} %w_qkv_ref.1) | copy-start | bytes 4718596
  6.8 0.9 %copy-start.3 = (bf16[256,512]{1,0:T(8,128)(2,1)S(1)}, bf16[256,512]{1,0:T(8,128)(2,1)}, u32[]{:S(2)}) copy-start(bf16[256,512]{1,0:T(8,128)(2,1)} %tokens_ref.1) | copy-start | bytes 786436
  7.8 14.0 %copy-start.2 = (bf16[512,1536]{1,0:T(8,128)(2,1)S(1)}, bf16[512,1536]{1,0:T(8,128)(2,1)}, u32[]{:S(2)}) copy-start(bf16[512,1536]{1,0:T(8,128)(2,1)} %w_qkv_ref.1) | copy-start | bytes 4718596
  13.0 2.1 %collective-permute-start.5 = (bf16[256,512]{1,0:T(8,128)(2,1)S(1)}, bf16[256,512]{1,0:T(8,128)(2,1)S(1)}, u32[]{:S(2)}, u32[]{:S(2)}) collective-permute-start(bf16[256,512]{1,0:T(8,128)(2,1)S(1)} %collective-permute-done.refs_4_.first_ref), channel_id=1, source_target_pairs={{0,1},{1,0},{2,3},{3,2},{4,5},{5,4},{6,7},{7,6},{8,9},{9,8},{10,11... | collective-permute-start | bytes 786440 | tf_op jit(solution)/shard_map/ppermute | solution.py:24
  13.0 2.1 %collective-permute-start.4 = (bf16[256,512]{1,0:T(8,128)(2,1)S(1)}, bf16[256,512]{1,0:T(8,128)(2,1)S(1)}, u32[]{:S(2)}, u32[]{:S(2)}) collective-permute-start(bf16[256,512]{1,0:T(8,128)(2,1)S(1)} %collective-permute-done.3.refs_2_.first_ref), channel_id=1, source_target_pairs={{0,1},{1,0},{2,3},{3,2},{4,5},{5,4},{6,7},{7,6},{8,9},{9,8},{10,11... | collective-permute-start | bytes 786440 | tf_op jit(solution)/shard_map/ppermute | solution.py:24
  13.5 1.6 %collective-permute-start.6 = (bf16[64,512]{1,0:T(8,128)(2,1)S(1)}, bf16[64,512]{1,0:T(8,128)(2,1)S(1)}, u32[]{:S(2)}, u32[]{:S(2)}) collective-permute-start(bf16[64,512]{1,0:T(8,128)(2,1)S(1)} %collective-permute-done.1.refs_6_), channel_id=1, source_target_pairs={{0,1},{1,0},{2,3},{3,2},{4,5},{5,4},{6,7},{7,6},{8,9},{9,8},{10,11... | collective-permute-start | bytes 196616 | tf_op jit(solution)/shard_map/ppermute | solution.py:24
  13.5 11.1 %collective-permute-start.10 = (bf16[256,512]{1,0:T(8,128)(2,1)S(1)}, bf16[256,512]{1,0:T(8,128)(2,1)S(1)}, u32[]{:S(2)}, u32[]{:S(2)}) collective-permute-start(bf16[256,512]{1,0:T(8,128)(2,1)S(1)} %collective-permute-done.refs_4_.first_ref), channel_id=1, source_target_pairs={{0,8},{1,9},{2,10},{3,11},{4,28},{5,29},{6,30},{7,31},{8,16},{9,17... | collective-permute-start | bytes 786440 | tf_op jit(solution)/shard_map/ppermute | solution.py:24
  16.0 10.0 %collective-permute-start.7 = (bf16[64,512]{1,0:T(8,128)(2,1)S(1)}, bf16[64,512]{1,0:T(8,128)(2,1)S(1)}, u32[]{:S(2)}, u32[]{:S(2)}) collective-permute-start(bf16[64,512]{1,0:T(8,128)(2,1)S(1)} %pick_pieces.1.refs_0_), channel_id=1, source_target_pairs={{0,8},{1,9},{2,10},{3,11},{4,28},{5,29},{6,30},{7,31},{8,16},{9,17... | collective-permute-start | bytes 196616 | tf_op jit(solution)/shard_map/ppermute | solution.py:24
  17.6 10.8 %collective-permute-start.8 = (bf16[64,512]{1,0:T(8,128)(2,1)S(1)}, bf16[64,512]{1,0:T(8,128)(2,1)S(1)}, u32[]{:S(2)}, u32[]{:S(2)}) collective-permute-start(bf16[64,512]{1,0:T(8,128)(2,1)S(1)} %pick_pieces.1.refs_0_), channel_id=1, source_target_pairs={{0,16},{1,17},{2,18},{3,19},{4,20},{5,21},{6,22},{7,23},{8,24},{9,... | collective-permute-start | bytes 196616 | tf_op jit(solution)/shard_map/ppermute | solution.py:24
  20.1 8.3 %collective-permute-start.9 = (bf16[64,512]{1,0:T(8,128)(2,1)S(1)}, bf16[64,512]{1,0:T(8,128)(2,1)S(1)}, u32[]{:S(2)}, u32[]{:S(2)}) collective-permute-start(bf16[64,512]{1,0:T(8,128)(2,1)S(1)} %pick_pieces.1.refs_0_), channel_id=1, source_target_pairs={{0,24},{1,25},{2,26},{3,27},{4,12},{5,13},{6,14},{7,15},{8,0},{9,1... | collective-permute-start | bytes 196616 | tf_op jit(solution)/shard_map/ppermute | solution.py:24
  21.5 11.4 %collective-permute-start.14 = (bf16[256,512]{1,0:T(8,128)(2,1)S(1)}, bf16[256,512]{1,0:T(8,128)(2,1)S(1)}, u32[]{:S(2)}, u32[]{:S(2)}) collective-permute-start(bf16[256,512]{1,0:T(8,128)(2,1)S(1)} %collective-permute-done.3.refs_2_.first_ref), channel_id=1, source_target_pairs={{0,4},{1,5},{2,6},{3,7},{4,0},{5,1},{6,2},{7,3},{8,12},{9,13},{10,... | collective-permute-start | bytes 786440 | tf_op jit(solution)/shard_map/ppermute | solution.py:24
  28.4 5.8 %collective-permute-start.16 = (bf16[256,512]{1,0:T(8,128)(2,1)S(1)}, bf16[256,512]{1,0:T(8,128)(2,1)S(1)}, u32[]{:S(2)}, u32[]{:S(2)}) collective-permute-start(bf16[256,512]{1,0:T(8,128)(2,1)S(1)} %collective-permute-done.10.first_ref), channel_id=1, source_target_pairs={{0,1},{1,0},{2,3},{3,2},{4,5},{5,4},{6,7},{7,6},{8,9},{9,8},{10,11... | collective-permute-start | bytes 786440 | tf_op jit(solution)/shard_map/ppermute | solution.py:24
  28.4 11.5 %collective-permute-start.17 = (bf16[256,512]{1,0:T(8,128)(2,1)S(1)}, bf16[256,512]{1,0:T(8,128)(2,1)S(1)}, u32[]{:S(2)}, u32[]{:S(2)}) collective-permute-start(bf16[256,512]{1,0:T(8,128)(2,1)S(1)} %collective-permute-done.10.first_ref), channel_id=1, source_target_pairs={{0,2},{1,3},{2,0},{3,1},{4,6},{5,7},{6,4},{7,5},{8,10},{9,11},{10,... | collective-permute-start | bytes 786440 | tf_op jit(solution)/shard_map/ppermute | solution.py:24
  30.7 9.3 %collective-permute-start.11 = (bf16[64,512]{1,0:T(8,128)(2,1)S(1)}, bf16[64,512]{1,0:T(8,128)(2,1)S(1)}, u32[]{:S(2)}, u32[]{:S(2)}) collective-permute-start(bf16[64,512]{1,0:T(8,128)(2,1)S(1)} %choose_pieces.1.refs_0_), channel_id=1, source_target_pairs={{0,2},{1,3},{2,0},{3,1},{4,6},{5,7},{6,4},{7,5},{8,10},{9,11},{10,... | collective-permute-start | bytes 196616 | tf_op jit(solution)/shard_map/ppermute | solution.py:24
  31.3 8.7 %collective-permute-start.12 = (bf16[64,512]{1,0:T(8,128)(2,1)S(1)}, bf16[64,512]{1,0:T(8,128)(2,1)S(1)}, u32[]{:S(2)}, u32[]{:S(2)}) collective-permute-start(bf16[64,512]{1,0:T(8,128)(2,1)S(1)} %choose_pieces.1.refs_0_), channel_id=1, source_target_pairs={{0,4},{1,5},{2,6},{3,7},{4,0},{5,1},{6,2},{7,3},{8,12},{9,13},{10,... | collective-permute-start | bytes 196616 | tf_op jit(solution)/shard_map/ppermute | solution.py:24
  33.0 7.0 %collective-permute-start.13 = (bf16[64,512]{1,0:T(8,128)(2,1)S(1)}, bf16[64,512]{1,0:T(8,128)(2,1)S(1)}, u32[]{:S(2)}, u32[]{:S(2)}) collective-permute-start(bf16[64,512]{1,0:T(8,128)(2,1)S(1)} %choose_pieces.1.refs_0_), channel_id=1, source_target_pairs={{0,6},{1,7},{2,4},{3,5},{4,2},{5,3},{6,0},{7,1},{8,14},{9,15},{10,... | collective-permute-start | bytes 196616 | tf_op jit(solution)/shard_map/ppermute | solution.py:24
  34.3 1.5 %collective-permute-start.15 = (bf16[256,512]{1,0:T(8,128)(2,1)S(1)}, bf16[256,512]{1,0:T(8,128)(2,1)S(1)}, u32[]{:S(2)}, u32[]{:S(2)}) collective-permute-start(bf16[256,512]{1,0:T(8,128)(2,1)S(1)} %collective-permute-done.14.first_ref), channel_id=1, source_target_pairs={{0,1},{1,0},{2,3},{3,2},{4,5},{5,4},{6,7},{7,6},{8,9},{9,8},{10,11... | collective-permute-start | bytes 786440 | tf_op jit(solution)/shard_map/ppermute | solution.py:24
  36.8 5.8 %copy-start = (s32[8,8,128,128]{3,2,1,0:T(8,128)S(1)}, s32[8,8,128,128]{3,2,1,0:T(8,128)}, u32[]{:S(2)}) copy-start(s32[8,8,128,128]{3,2,1,0:T(8,128)} %mask_ref.1) | copy-start | bytes 12582916
  36.8 5.8 %copy-start.4 = (bf16[256,512]{1,0:T(8,128)(2,1)S(1)}, bf16[256,512]{1,0:T(8,128)(2,1)}, u32[]{:S(2)}) copy-start(bf16[256,512]{1,0:T(8,128)(2,1)} %tokens_ref.1) | copy-start | bytes 786436
  36.8 5.8 %copy-start.5 = (bf16[512,1024]{1,0:T(8,128)(2,1)S(1)}, bf16[512,1024]{1,0:T(8,128)(2,1)}, u32[]{:S(2)}) copy-start(bf16[512,1024]{1,0:T(8,128)(2,1)} %w_up_ref.1) | copy-start | bytes 3145732
  36.8 5.8 %copy-start.6 = (bf16[1024,512]{1,0:T(8,128)(2,1)S(1)}, bf16[1024,512]{1,0:T(8,128)(2,1)}, u32[]{:S(2)}) copy-start(bf16[1024,512]{1,0:T(8,128)(2,1)} %w_down_ref.1) | copy-start | bytes 3145732
  36.8 5.8 %copy-start.7 = (bf16[512,512]{1,0:T(8,128)(2,1)S(1)}, bf16[512,512]{1,0:T(8,128)(2,1)}, u32[]{:S(2)}) copy-start(bf16[512,512]{1,0:T(8,128)(2,1)} %w_out_ref.1) | copy-start | bytes 1572868
  36.8 5.8 %copy-start.8 = (s32[8,8]{1,0:T(8,128)S(1)}, s32[8,8]{1,0:T(8,128)}, u32[]{:S(2)}) copy-start(s32[8,8]{1,0:T(8,128)} %cols_ref.1) | copy-start | bytes 772
  40.0 1.6 %collective-permute-start.22 = (bf16[256,512]{1,0:T(8,128)(2,1)S(1)}, bf16[256,512]{1,0:T(8,128)(2,1)S(1)}, u32[]{:S(2)}, u32[]{:S(2)}) collective-permute-start(bf16[256,512]{1,0:T(8,128)(2,1)S(1)} %collective-permute-done.17.first_ref), channel_id=1, source_target_pairs={{0,1},{1,0},{2,3},{3,2},{4,5},{5,4},{6,7},{7,6},{8,9},{9,8},{10,11... | collective-permute-start | bytes 786440 | tf_op jit(solution)/shard_map/ppermute | solution.py:24
  40.1 2.5 %collective-permute-start.18 = (bf16[64,512]{1,0:T(8,128)(2,1)S(1)}, bf16[64,512]{1,0:T(8,128)(2,1)S(1)}, u32[]{:S(2)}, u32[]{:S(2)}) collective-permute-start(bf16[64,512]{1,0:T(8,128)(2,1)S(1)} %choose_pieces.1.refs_0_), channel_id=1, source_target_pairs={{0,1},{1,0},{2,3},{3,2},{4,5},{5,4},{6,7},{7,6},{8,9},{9,8},{10,11... | collective-permute-start | bytes 196616 | tf_op jit(solution)/shard_map/ppermute | solution.py:24
  40.6 2.0 %collective-permute-start.19 = (bf16[64,512]{1,0:T(8,128)(2,1)S(1)}, bf16[64,512]{1,0:T(8,128)(2,1)S(1)}, u32[]{:S(2)}, u32[]{:S(2)}) collective-permute-start(bf16[64,512]{1,0:T(8,128)(2,1)S(1)} %collective-permute-done.11.refs_2_), channel_id=1, source_target_pairs={{0,1},{1,0},{2,3},{3,2},{4,5},{5,4},{6,7},{7,6},{8,9},{9,8},{10,11... | collective-permute-start | bytes 196616 | tf_op jit(solution)/shard_map/ppermute | solution.py:24
  40.6 1.9 %collective-permute-start.20 = (bf16[64,512]{1,0:T(8,128)(2,1)S(1)}, bf16[64,512]{1,0:T(8,128)(2,1)S(1)}, u32[]{:S(2)}, u32[]{:S(2)}) collective-permute-start(bf16[64,512]{1,0:T(8,128)(2,1)S(1)} %collective-permute-done.12.refs_4_), channel_id=1, source_target_pairs={{0,1},{1,0},{2,3},{3,2},{4,5},{5,4},{6,7},{7,6},{8,9},{9,8},{10,11... | collective-permute-start | bytes 196616 | tf_op jit(solution)/shard_map/ppermute | solution.py:24
  41.1 1.5 %collective-permute-start.21 = (bf16[64,512]{1,0:T(8,128)(2,1)S(1)}, bf16[64,512]{1,0:T(8,128)(2,1)S(1)}, u32[]{:S(2)}, u32[]{:S(2)}) collective-permute-start(bf16[64,512]{1,0:T(8,128)(2,1)S(1)} %collective-permute-done.13.refs_6_), channel_id=1, source_target_pairs={{0,1},{1,0},{2,3},{3,2},{4,5},{5,4},{6,7},{7,6},{8,9},{9,8},{10,11... | collective-permute-start | bytes 196616 | tf_op jit(solution)/shard_map/ppermute | solution.py:24

commit v3 on v2

v3 whole, which is shorter than its diff:
```python
import functools

import jax
import jax.numpy as jnp
from jax import lax
from jax.experimental import pallas as pl
from jax.experimental.pallas import tpu as pltpu
from jax.sharding import PartitionSpec as P

TB = 128
PIECES = 8
PIECE = TB // PIECES
AXES = ("nodes", "heads")
ANY = pl.BlockSpec(memory_space=pl.ANY)
VMEM = pl.BlockSpec(memory_space=pltpu.VMEM)


def send(value, nodes, heads, where):
    pairs = []
    for n in range(nodes):
        for h in range(heads):
            to_n, to_h = where(n, h)
            pairs.append((n * heads + h, to_n % nodes * heads + to_h))
    return lax.ppermute(value, AXES, pairs)


def layer_norm(value_rows):
    mean = jnp.mean(value_rows, axis=-1, keepdims=True)
    centered = value_rows - mean
    spread = jnp.mean(centered * centered, axis=-1, keepdims=True)
    return (centered * lax.rsqrt(spread + 1e-05)).astype(jnp.bfloat16)


def project(normed, w_ref, cols):
    return jnp.dot(normed, w_ref[:, cols], preferred_element_type=jnp.float32).astype(
        jnp.bfloat16
    )


def keyval_into(out_ref, rows, normed, w_ref, heads, head_dim):
    width = heads * head_dim
    if head_dim % 128 == 0:
        for h in range(heads):
            both = project(normed, w_ref, slice((3 * h + 1) * head_dim, (3 * h + 3) * head_dim))
            out_ref[rows, h * head_dim : (h + 1) * head_dim] = both[:, :head_dim]
            out_ref[rows, width + h * head_dim : width + (h + 1) * head_dim] = both[:, head_dim:]
    else:
        out_ref[rows, :] = project(normed, w_ref, slice(width, 3 * width))


def query_into(out_ref, normed, w_ref, heads, head_dim):
    if head_dim % 128 == 0:
        for h in range(heads):
            out_ref[:, h * head_dim : (h + 1) * head_dim] = project(
                normed, w_ref, slice(3 * h * head_dim, (3 * h + 1) * head_dim)
            )
    else:
        out_ref[...] = project(normed, w_ref, slice(0, heads * head_dim))


def keyval_kernel(heads, head_dim, at, first_ref, second_ref, w_ref, *refs):
    node_dev = first_ref.shape[0]
    pool_ref = refs[-1] if at else refs[-3]
    for k, ref in enumerate((first_ref, second_ref)):
        normed = layer_norm(ref[...].astype(jnp.float32))
        rows = slice((at + k) * node_dev, (at + k + 1) * node_dev)
        keyval_into(pool_ref, rows, normed, w_ref, heads, head_dim)
        if not at and not k:
            query_into(refs[-2], normed, w_ref, heads, head_dim)
            refs[-1][...] = ref[...]


def keyvals(pool, at, first, second, w_qkv, heads, head_dim, blocks, after=()):
    node_dev, width = first.shape
    out_shape = [jax.ShapeDtypeStruct((blocks * TB, 2 * width), jnp.bfloat16)]
    if not at:
        out_shape += [jax.ShapeDtypeStruct((node_dev, width), jnp.bfloat16)] * 2
    operands = [first, second, w_qkv, *after] + ([pool] if at else [])
    result = pl.pallas_call(
        functools.partial(keyval_kernel, heads, head_dim, at),
        out_shape=out_shape,
        in_specs=[VMEM] * 3 + [ANY] * len(after) + [VMEM] * bool(at),
        out_specs=[VMEM] * len(out_shape),
        input_output_aliases={len(operands) - 1: 0} if at else {},
        compiler_params=pltpu.CompilerParams(vmem_limit_bytes=8 << 20),
        cost_estimate=pl.CostEstimate(
            flops=64 * node_dev * width * width, bytes_accessed=6 * width * width, transcendentals=0
        ),
        name="keyvals",
    )(*operands)
    return result if not at else result[0]


def place():
    return lax.axis_index("nodes"), lax.axis_index("heads")


def copy_chosen(code, sources, out_ref, out_rows):
    for k, (ref, row) in enumerate(sources):
        @pl.when(code == k)
        def _():
            rows = pl.ds(pl.multiple_of(row, PIECE), PIECE)
            out_ref[out_rows, :] = ref[rows, :]


def pick_kernel(hub_count, per_group, local, heads, hubs_ref, *refs):
    *sources, piece_ref = refs
    here, head_here = place()
    piece = here % 2 * 4 + head_here % 4
    for j in range(hub_count):
        owner_n = hubs_ref[j] // per_group
        owner_h = hubs_ref[j] % per_group // local
        slot = hubs_ref[j] % local
        far = (owner_n // 2 != here // 2) | (owner_h // 4 != head_here // 4)
        offset = (owner_n + here) % 2 * 4 + ((owner_h % 4) ^ (head_here % 4))
        code = jnp.where(far, -1, offset)
        whole = slot * TB + piece * PIECE
        strip = slot * 2 * PIECE + head_here % 2 * PIECE
        rows = slice(j * PIECE, (j + 1) * PIECE)
        copy_chosen(code, [(ref, whole if k < 6 else strip) for k, ref in enumerate(sources)], piece_ref, rows)

        @pl.when(far)
        def _():
            piece_ref[rows, :] = jnp.zeros((PIECE, piece_ref.shape[1]), piece_ref.dtype)


def pick_pieces(hub_blocks, sources, per_group, heads):
    node_dev, width = sources[0].shape
    hub_count = hub_blocks.shape[0]
    return pl.pallas_call(
        functools.partial(pick_kernel, hub_count, per_group, node_dev // TB, heads),
        out_shape=jax.ShapeDtypeStruct((hub_count * PIECE, width), jnp.bfloat16),
        in_specs=[pl.BlockSpec(memory_space=pltpu.SMEM)] + [VMEM] * 8,
        out_specs=VMEM,
        compiler_params=pltpu.CompilerParams(vmem_limit_bytes=4 << 20),
        name="pick_pieces",
    )(hub_blocks, *sources)


def choose_kernel(hub_count, from_where, hubs_ref, *refs):
    *sources, piece_ref = refs
    here, head_here = place()
    for j in range(hub_count):
        code = from_where(hubs_ref[j], here, head_here)
        rows = slice(j * PIECE, (j + 1) * PIECE)
        copy_chosen(code, [(ref, j * PIECE) for ref in sources], piece_ref, rows)


def choose_pieces(hub_blocks, sources, from_where):
    return pl.pallas_call(
        functools.partial(choose_kernel, hub_blocks.shape[0], from_where),
        out_shape=jax.ShapeDtypeStruct(sources[0].shape, jnp.bfloat16),
        in_specs=[pl.BlockSpec(memory_space=pltpu.SMEM)] + [VMEM] * len(sources),
        out_specs=VMEM,
        compiler_params=pltpu.CompilerParams(vmem_limit_bytes=4 << 20),
        name="choose_pieces",
    )(hub_blocks, *sources)


def finish_kernel(
    heads, head_dim, hub_count, hub_base, cols_ref,
    tokens_ref, query_ref, mask_ref, w_qkv_ref, w_out_ref, w_up_ref, w_down_ref, *refs
):
    around, (_, out_ref, pool_ref, hub_rows, mask, attn, sem) = refs[:PIECES], refs[PIECES:]
    node_dev, width = tokens_ref.shape
    local = node_dev // TB
    per_group, tiles = cols_ref.shape
    here, head_here = place()
    load = pltpu.make_async_copy(mask_ref.at[pl.ds(head_here * local, local)], mask, sem)
    load.start()
    mine = here % 2 * 4 + head_here % 4
    for k, ref in enumerate(around):
        for j in range(hub_count):
            row = ref.shape[0] - (hub_count - j) * PIECE
            rows = pl.ds(pl.multiple_of(j * TB + (mine ^ k) * PIECE, PIECE), PIECE)
            hub_rows[rows, :] = ref[row : row + PIECE, :]
    hub_normed = layer_norm(hub_rows[...].astype(jnp.float32))
    hub_place = pool_ref.shape[0] // TB - hub_count
    keyval_into(pool_ref, slice(hub_place * TB, None), hub_normed, w_qkv_ref, heads, head_dim)
    load.wait()
    group = max(head_dim, 128)
    for r in range(local):
        rows = slice(r * TB, (r + 1) * TB)
        places = []
        for t in range(tiles):
            col = cols_ref[head_here * local + r, t]
            near, block = col // per_group, col % per_group
            region = jnp.where(near == here, 0, jnp.where(near // 2 == here // 2, 1, 2))
            index = region * per_group + ((block // local) ^ head_here) * local + block % local
            index = jnp.where(col < hub_base, index, hub_place + col - hub_base)
            places.append(pl.ds(pl.multiple_of(index * TB, TB), TB))
        edges = jnp.concatenate([mask[r, t].astype(jnp.float32) for t in range(tiles)], axis=1)
        for g in range(width // group):
            cols = slice(g * group, (g + 1) * group)
            beyond = slice(width + g * group, width + (g + 1) * group)
            keys = jnp.concatenate([pool_ref[at, cols] for at in places], axis=0)
            values = jnp.concatenate([pool_ref[at, beyond] for at in places], axis=0)
            attn[rows, cols] = attention(query_ref[rows, cols], keys, values, edges, head_dim)
    mid = tokens_ref[...].astype(jnp.float32) + jnp.dot(
        attn[...], w_out_ref[...], preferred_element_type=jnp.float32
    )
    normed = layer_norm(mid)
    up = jnp.dot(normed, w_up_ref[...], preferred_element_type=jnp.float32)
    hidden = (0.5 * up * (1.0 + lax.erf(up * (0.5**0.5)))).astype(jnp.bfloat16)
    out_ref[...] = (
        mid + jnp.dot(hidden, w_down_ref[...], preferred_element_type=jnp.float32)
    ).astype(jnp.bfloat16)


def attention(query, keys, values, edges, head_dim):
    per = query.shape[1] // head_dim
    scale = 1.0 / head_dim**0.5
    lane = lax.broadcasted_iota(jnp.int32, query.shape, 1)
    result = None
    for s in range(per):
        here = (lane >= s * head_dim) & (lane < (s + 1) * head_dim)
        own = query if per == 1 else jnp.where(here, query.astype(jnp.float32), 0.0).astype(jnp.bfloat16)
        score = lax.dot_general(own, keys, (((1,), (1,)), ((), ())), preferred_element_type=jnp.float32)
        weight = jnp.exp(score * scale) * edges
        total = jnp.sum(weight, axis=1, keepdims=True)
        summed = jnp.dot(weight.astype(jnp.bfloat16), values, preferred_element_type=jnp.float32)
        one = summed / total
        result = one if result is None else jnp.where(here, one, result)
    return result.astype(jnp.bfloat16)


def finish(cols, tokens, query, mask, w_qkv, w_out, w_up, w_down, around, pool, heads, head_dim, hub_count, hub_base):
    node_dev, width = tokens.shape
    bf16 = jnp.bfloat16
    return pl.pallas_call(
        functools.partial(finish_kernel, heads, head_dim, hub_count, hub_base),
        out_shape=[jax.ShapeDtypeStruct(tokens.shape, bf16), jax.ShapeDtypeStruct(pool.shape, bf16)],
        in_specs=[pl.BlockSpec(memory_space=pltpu.SMEM)]
        + [VMEM] * 2
        + [pl.BlockSpec(memory_space=pltpu.HBM)]
        + [VMEM] * (5 + PIECES),
        out_specs=[VMEM, VMEM],
        input_output_aliases={8 + PIECES: 1},
        scratch_shapes=[
            pltpu.VMEM((hub_count * TB, width), bf16),
            pltpu.VMEM((node_dev // TB,) + mask.shape[1:], jnp.int32),
            pltpu.VMEM((node_dev, width), bf16),
            pltpu.SemaphoreType.DMA,
        ],
        compiler_params=pltpu.CompilerParams(vmem_limit_bytes=20 << 20),
        name="finish",
    )(cols, tokens, query, mask, w_qkv, w_out, w_up, w_down, *around, pool)[0]


def body(tokens, w_qkv, w_out, w_up, w_down, tile_cols, tile_mask, hub_blocks):
    node_dev, width = tokens.shape
    nodes = lax.axis_size("nodes")
    heads = lax.axis_size("heads")
    head_dim = width // heads
    per_group = tile_cols.shape[0]
    hub_count = hub_blocks.shape[0]
    local = node_dev // TB
    in_row = heads // 4
    areas = nodes // 2 * in_row
    go = functools.partial(send, nodes=nodes, heads=heads)

    def core(value):
        return go(value, where=lambda n, h: (n, h ^ 1))

    def pair(value):
        return go(value, where=lambda n, h: (n ^ 1, h))

    def across(value):
        return go(value, where=lambda n, h: (n ^ 1, h ^ 2))

    def side(value, offset=2):
        return go(value, where=lambda n, h: (n, h ^ offset))

    def along(value, by=1):
        return go(value, where=lambda n, h: (n + (2 - 4 * (n & 1)) * by, h))

    weights = w_qkv
    if head_dim % 128:
        weights = w_qkv.reshape(width, heads, 3, head_dim).swapaxes(1, 2).reshape(width, 3 * width)
    keyval = functools.partial(
        keyvals, w_qkv=weights, heads=heads, head_dim=head_dim, blocks=3 * per_group + hub_count
    )

    other = range(2, heads, 2)
    sides = [side(tokens, o) for o in other]
    paired = pair(tokens)
    here, head_here = place()
    strip_at = ((1 - here % 2) * 4 + ((head_here % 4) ^ 2) // 2 * 2) * PIECE
    strip = lax.dynamic_slice_in_dim(tokens.reshape(local, TB, width), strip_at, 2 * PIECE, 1)
    strip = across(strip.reshape(local * 2 * PIECE, width))
    token_core = core(tokens)
    pool, query, again = keyval(None, 0, tokens, token_core)
    far = go(again, where=lambda n, h: (n - 1 + 2 * (n & 1), h))
    paired, strip, pool, query, *sides = lax.optimization_barrier((paired, strip, pool, query, *sides))

    paired_core, strip_core = core(paired), core(strip)
    sides_core = [core(v) for v in sides]
    paired_sides = [pair(v) for v in sides]
    sources = [tokens, token_core, sides[0], sides_core[0], paired, paired_core, strip, strip_core]
    piece = pick_pieces(hub_blocks, sources, per_group, heads)

    for k, (value, other_value) in enumerate(zip(sides, sides_core)):
        pool = keyval(pool, 2 + 2 * k, value, other_value, after=(piece,))
    far, pool = lax.optimization_barrier((far, pool))
    far_sides = [side(far, o) for o in other]
    far_core = core(far)
    pool = keyval(pool, heads, paired, paired_core)

    def owner_area(block):
        return block // per_group // 2 * in_row + block % per_group // local // 4

    def area_of(here, head_here):
        return here // 2 * in_row + head_here // 4

    if areas == 4 and in_row == 1:
        got = [piece, along(piece), along(piece, 2), along(piece, -1)]
        got, pool, paired_sides = lax.optimization_barrier((got, pool, paired_sides))

        def from_where(block, here, head_here):
            ahead = area_of(here, head_here) + 4 - owner_area(block)
            return jnp.where(here % 2 == 0, ahead, 8 - ahead) % 4

        piece = choose_pieces(hub_blocks, got, from_where)
    else:

        def to_area(n, h, shift):
            at = (n // 2 * in_row + h // 4) ^ shift
            return at // in_row * 2 + n % 2, at % in_row * 4 + h % 4

        step = 1
        while step < areas:
            reach = [s * step for s in (1, 2, 3) if s * step < areas]
            got = [go(piece, where=lambda n, h, s=s: to_area(n, h, s)) for s in reach]

            def from_where(block, here, head_here, step=step):
                return (owner_area(block) ^ area_of(here, head_here)) // step % 4

            piece = choose_pieces(hub_blocks, [piece, *got], from_where)
            step *= 4

    around = [piece, side(piece), pair(piece), across(piece)]
    paired_sides_core = [core(v) for v in paired_sides]
    far_sides_core = [core(v) for v in far_sides]
    for k, (value, other_value) in enumerate(zip(paired_sides, paired_sides_core)):
        pool = keyval(pool, heads + 2 + 2 * k, value, other_value)
    for k, (value, other_value) in enumerate(zip([far, *far_sides], [far_core, *far_sides_core])):
        pool = keyval(pool, 2 * heads + 2 * k, value, other_value)
    around, pool = lax.optimization_barrier((around, pool))

    around = [v for value in around for v in (value, core(value))]
    return finish(
        tile_cols, tokens, query, tile_mask, weights, w_out, w_up, w_down, around, pool, heads, head_dim, hub_count, per_group * nodes
    )


def solution(mesh):
    placed = (
        P(("nodes", "heads"), None),
        P(),
        P(),
        P(),
        P(),
        P("nodes", None),
        P("nodes", None, None, None),
        P(),
    )
    return jax.shard_map(
        body, mesh=mesh, in_specs=placed, out_specs=P(("nodes", "heads"), None), check_vma=False
    )
```

time: 51.1 us -> 47.4 us (0.928)
  waiting for transfers between devices: 13 us -> 10.1 us
  Pallas kernels: 15.6 us -> 13.1 us
  starting transfers between devices: 18.6 us -> 20.4 us
    ppermute x23, waiting for transfers between devices: 13 us -> 10.1 us  [send(): return lax.ppermute(value, AXES, pairs)]
    pallas_call x7, Pallas kernels: 14 us -> 11.5 us  [the longest x6 5.78 us: keyvals(): pl.pallas_call(functools.partial(keyval_kernel, heads, head_dim, at), out...]
    ppermute x23, starting transfers between devices: 18.6 us -> 20.4 us  [send(): return lax.ppermute(value, AXES, pairs)]
  transfers between devices with their start and end apart: 23 -> 23, of which waited for: 8 -> 9; matrix products, arithmetic and copies ran while one was open for 2% -> 2% of each run, Pallas kernels for 15% -> 16%
where the time goes in v3:
time: 47.4 us; the launch traced here: 47.1 us
  starting transfers between devices  20.4 us (43%)
  Pallas kernels  13.1 us (28%)
  waiting for transfers between devices  10.1 us (21%)
  local copies, waits for them, and re-layouts  3.28 us (7%)
    ppermute x23, starting transfers between devices, send(): return lax.ppermute(value, AXES, pairs)  20.4 us
    ppermute x23, waiting for transfers between devices, send(): return lax.ppermute(value, AXES, pairs)  10.1 us
    pallas_call x6, Pallas kernels, keyvals(): pl.pallas_call(functools.partial(keyval_kernel, heads, head_dim, at), out...  5.78 us
    pallas_call x1, Pallas kernels, finish(): pl.pallas_call(functools.partial(finish_kernel, heads, head_dim, hub_coun...  5.71 us
    unnamed x20, local copies, waits for them, and re-layouts  2.41 us
  transfers between devices with their start and end apart: 23, of which 9 were waited for; matrix products, arithmetic and copies ran while one was open for 2% of the time, Pallas kernels for 16%

profile of v3, /device:TPU:0, one launch (start us, length us, event | category | flops | bytes accessed | tf_op | source)
XLA Modules:
  0.0 47.1 jit_solution(15193998513086266199)
XLA Ops:
  0.0 0.5 collective-permute-start.2
  0.5 2.5 %collective-permute-start = (bf16[256,512]{1,0:T(8,128)(2,1)}, bf16[256,512]{1,0:T(8,128)(2,1)S(1)}, u32[]{:S(2)}, u32[]{:S(2)}) collective-permute-start(bf16[256,512]{1,0:T(8,128)(2,1)} %tokens_ref.1), channel_id=1, source_target_pairs={{0,4},{1,5},{2,6},{3,7},{4,0},{5,1},{6,2},{7,3},{8,12},{9,13},{10,... | collective-permute-start | bytes 786440 | tf_op jit(solution)/shard_map/ppermute | solution.py:24
  2.9 1.5 %collective-permute-start.3 = (bf16[256,512]{1,0:T(8,128)(2,1)}, bf16[256,512]{1,0:T(8,128)(2,1)S(1)}, u32[]{:S(2)}, u32[]{:S(2)}) collective-permute-start(bf16[256,512]{1,0:T(8,128)(2,1)} %tokens_ref.1), channel_id=1, source_target_pairs={{0,2},{1,3},{2,0},{3,1},{4,6},{5,7},{6,4},{7,5},{8,10},{9,11},{10,... | collective-permute-start | bytes 786440 | tf_op jit(solution)/shard_map/ppermute | solution.py:24
  4.5 0.9 %constant_dynamic-slice_fusion = bf16[2,32,512]{2,1,0:T(8,128)(2,1)S(1)} fusion(bf16[2,128,512]{2,1,0:T(8,128)(2,1)} %bitcast.2, s32[]{:T(128)S(6)} %select_n.21), kind=kLoop, calls=%fused_computation | loop fusion | bytes 131076 | tf_op jit(solution)/shard_map/dynamic_slice | solution.py:289
  5.3 0.0 collective-permute-start.1
  5.4 1.4 %copy-done = bf16[512,1536]{1,0:T(8,128)(2,1)S(1)} copy-done((bf16[512,1536]{1,0:T(8,128)(2,1)S(1)}, bf16[512,1536]{1,0:T(8,128)(2,1)}, u32[]{:S(2)}) %copy-start) | copy-done | bytes 1572888
  6.8 0.9 %copy-done.3 = bf16[256,512]{1,0:T(8,128)(2,1)S(1)} copy-done((bf16[256,512]{1,0:T(8,128)(2,1)S(1)}, bf16[256,512]{1,0:T(8,128)(2,1)}, u32[]{:S(2)}) %copy-start.3) | copy-done | bytes 262168
  7.8 1.2 %keyvals.6 = (bf16[3584,1024]{1,0:T(8,128)(2,1)S(1)}, bf16[256,512]{1,0:T(8,128)(2,1)S(1)}, bf16[256,512]{1,0:T(8,128)(2,1)S(1)}) custom-call(bf16[256,512]{1,0:T(8,128)(2,1)S(1)} %copy-done.3, bf16[256,512]{1,0:T(8,128)(2,1)S(1)} %collective-permute-done.2.second_ref.refs_1_, bf16[512,1536]{1,0:T(8,128)(2,1)S(1)} %copy-done), custom_call_target="tpu_custom_call" | custom-call | flops 4294967296 | bytes 1572864 | tf_op jit(solution)/shard_map/keyvals/pallas_call | solution.py:79
  8.9 3.9 %collective-permute-done.1.refs_6_ = bf16[64,512]{1,0:T(8,128)(2,1)S(1)} collective-permute-done((bf16[64,512]{1,0:T(8,128)(2,1)S(1)}, bf16[64,512]{1,0:T(8,128)(2,1)S(1)}, u32[]{:S(2)}, u32[]{:S(2)}) %collective-permute-start.1) | collective-permute-done | bytes 65568 | tf_op jit(solution)/shard_map/ppermute | solution.py:24
  12.9 0.1 collective-permute-done.3.refs_2_.first_ref
  13.0 0.5 %collective-permute-start.5 = (bf16[256,512]{1,0:T(8,128)(2,1)S(1)}, bf16[256,512]{1,0:T(8,128)(2,1)S(1)}, u32[]{:S(2)}, u32[]{:S(2)}) collective-permute-start(bf16[256,512]{1,0:T(8,128)(2,1)S(1)} %collective-permute-done.refs_4_.first_ref), channel_id=1, source_target_pairs={{0,1},{1,0},{2,3},{3,2},{4,5},{5,4},{6,7},{7,6},{8,9},{9,8},{10,11... | collective-permute-start | bytes 786440 | tf_op jit(solution)/shard_map/ppermute | solution.py:24
  13.5 0.0 collective-permute-start.6
  13.5 1.3 %collective-permute-start.11 = (bf16[256,512]{1,0:T(8,128)(2,1)S(1)}, bf16[256,512]{1,0:T(8,128)(2,1)S(1)}, u32[]{:S(2)}, u32[]{:S(2)}) collective-permute-start(bf16[256,512]{1,0:T(8,128)(2,1)S(1)} %collective-permute-done.3.refs_2_.first_ref), channel_id=1, source_target_pairs={{0,4},{1,5},{2,6},{3,7},{4,0},{5,1},{6,2},{7,3},{8,12},{9,13},{10,... | collective-permute-start | bytes 786440 | tf_op jit(solution)/shard_map/ppermute | solution.py:24
  14.8 3.8 %collective-permute-start.10 = (bf16[256,512]{1,0:T(8,128)(2,1)S(1)}, bf16[256,512]{1,0:T(8,128)(2,1)S(1)}, u32[]{:S(2)}, u32[]{:S(2)}) collective-permute-start(bf16[256,512]{1,0:T(8,128)(2,1)S(1)} %get-tuple-element.33), channel_id=1, source_target_pairs={{0,28},{1,29},{2,30},{3,31},{4,8},{5,9},{6,10},{7,11},{8,4},{9,5},... | collective-permute-start | bytes 786440 | tf_op jit(solution)/shard_map/ppermute | solution.py:24
  18.6 0.0 collective-permute-done.6.refs_7_
  18.6 0.9 %pick_pieces.1.refs_0_ = bf16[64,512]{1,0:T(8,128)(2,1)S(1)} custom-call(s32[4]{0:T(128)S(1)} %copy-done.9, bf16[256,512]{1,0:T(8,128)(2,1)S(1)} %copy-done.3, bf16[256,512]{1,0:T(8,128)(2,1)S(1)} %collective-permute-done.2.second_ref.refs_1_, bf16[256,512]{1,0:T(8,128)(2,1)S(1)} %collective-permute-done.3.refs_2_.first_ref, ...), custom_call_target="tpu_custom_call" | custom-call | tf_op jit(solution)/shard_map/pick_pieces/pallas_call | solution.py:130
  19.5 0.1 collective-permute-start.7
  19.5 1.0 %collective-permute-start.8 = (bf16[64,512]{1,0:T(8,128)(2,1)S(1)}, bf16[64,512]{1,0:T(8,128)(2,1)S(1)}, u32[]{:S(2)}, u32[]{:S(2)}) collective-permute-start(bf16[64,512]{1,0:T(8,128)(2,1)S(1)} %pick_pieces.1.refs_0_), channel_id=1, source_target_pairs={{0,16},{1,17},{2,18},{3,19},{4,20},{5,21},{6,22},{7,23},{8,24},{9,... | collective-permute-start | bytes 196616 | tf_op jit(solution)/shard_map/ppermute | solution.py:24
  20.5 2.8 %collective-permute-start.9 = (bf16[64,512]{1,0:T(8,128)(2,1)S(1)}, bf16[64,512]{1,0:T(8,128)(2,1)S(1)}, u32[]{:S(2)}, u32[]{:S(2)}) collective-permute-start(bf16[64,512]{1,0:T(8,128)(2,1)S(1)} %pick_pieces.1.refs_0_), channel_id=1, source_target_pairs={{0,24},{1,25},{2,26},{3,27},{4,12},{5,13},{6,14},{7,15},{8,0},{9,1... | collective-permute-start | bytes 196616 | tf_op jit(solution)/shard_map/ppermute | solution.py:24
  23.3 0.9 %keyvals.7.refs_0_ = bf16[3584,1024]{1,0:T(8,128)(2,1)S(1)} custom-call(bf16[256,512]{1,0:T(8,128)(2,1)S(1)} %collective-permute-done.3.refs_2_.first_ref, bf16[256,512]{1,0:T(8,128)(2,1)S(1)} %collective-permute-done.4.refs_3_.second_ref, bf16[512,1536]{1,0:T(8,128)(2,1)S(1)} %copy-done, ...), custom_call_target="tpu_custom_call", output_to_operand_aliasing={{}: (4, {})} | custom-call | flops 4294967296 | bytes 1572864 | tf_op jit(solution)/shard_map/keyvals/pallas_call | solution.py:79
  24.3 2.5 %collective-permute-done.10.first_ref = bf16[256,512]{1,0:T(8,128)(2,1)S(1)} collective-permute-done((bf16[256,512]{1,0:T(8,128)(2,1)S(1)}, bf16[256,512]{1,0:T(8,128)(2,1)S(1)}, u32[]{:S(2)}, u32[]{:S(2)}) %collective-permute-start.10) | collective-permute-done | bytes 262176 | tf_op jit(solution)/shard_map/ppermute | solution.py:24
  26.7 0.7 %collective-permute-start.15 = (bf16[256,512]{1,0:T(8,128)(2,1)S(1)}, bf16[256,512]{1,0:T(8,128)(2,1)S(1)}, u32[]{:S(2)}, u32[]{:S(2)}) collective-permute-start(bf16[256,512]{1,0:T(8,128)(2,1)S(1)} %collective-permute-done.10.first_ref), channel_id=1, source_target_pairs={{0,2},{1,3},{2,0},{3,1},{4,6},{5,7},{6,4},{7,5},{8,10},{9,11},{10,... | collective-permute-start | bytes 786440 | tf_op jit(solution)/shard_map/ppermute | solution.py:24
  27.4 0.9 %keyvals.8.refs_0_ = bf16[3584,1024]{1,0:T(8,128)(2,1)S(1)} custom-call(bf16[256,512]{1,0:T(8,128)(2,1)S(1)} %collective-permute-done.refs_4_.first_ref, bf16[256,512]{1,0:T(8,128)(2,1)S(1)} %collective-permute-done.5.refs_5_.second_ref, bf16[512,1536]{1,0:T(8,128)(2,1)S(1)} %copy-done, ...), custom_call_target="tpu_custom_call", output_to_operand_aliasing={{}: (3, {})} | custom-call | flops 4294967296 | bytes 1572864 | tf_op jit(solution)/shard_map/keyvals/pallas_call | solution.py:79
  28.4 1.0 %collective-permute-done.8.refs_2_ = bf16[64,512]{1,0:T(8,128)(2,1)S(1)} collective-permute-done((bf16[64,512]{1,0:T(8,128)(2,1)S(1)}, bf16[64,512]{1,0:T(8,128)(2,1)S(1)}, u32[]{:S(2)}, u32[]{:S(2)}) %collective-permute-start.8) | collective-permute-done | bytes 65568 | tf_op jit(solution)/shard_map/ppermute | solution.py:24
  29.4 0.5 %collective-permute-start.17 = (bf16[256,512]{1,0:T(8,128)(2,1)S(1)}, bf16[256,512]{1,0:T(8,128)(2,1)S(1)}, u32[]{:S(2)}, u32[]{:S(2)}) collective-permute-start(bf16[256,512]{1,0:T(8,128)(2,1)S(1)} %collective-permute-done.10.first_ref), channel_id=1, source_target_pairs={{0,1},{1,0},{2,3},{3,2},{4,5},{5,4},{6,7},{7,6},{8,9},{9,8},{10,11... | collective-permute-start | bytes 786440 | tf_op jit(solution)/shard_map/ppermute | solution.py:24
  29.9 0.7 %choose_pieces.1.refs_0_ = bf16[64,512]{1,0:T(8,128)(2,1)S(1)} custom-call(s32[4]{0:T(128)S(1)} %copy-done.9, bf16[64,512]{1,0:T(8,128)(2,1)S(1)} %pick_pieces.1.refs_0_, bf16[64,512]{1,0:T(8,128)(2,1)S(1)} %collective-permute-done.7.refs_1_, bf16[64,512]{1,0:T(8,128)(2,1)S(1)} %collective-permute-done.8.refs_2_, ...), custom_call_target="tpu_custom_call" | custom-call | tf_op jit(solution)/shard_map/choose_pieces/pallas_call | solution.py:150
  30.6 1.6 %collective-permute-start.12 = (bf16[64,512]{1,0:T(8,128)(2,1)S(1)}, bf16[64,512]{1,0:T(8,128)(2,1)S(1)}, u32[]{:S(2)}, u32[]{:S(2)}) collective-permute-start(bf16[64,512]{1,0:T(8,128)(2,1)S(1)} %choose_pieces.1.refs_0_), channel_id=1, source_target_pairs={{0,2},{1,3},{2,0},{3,1},{4,6},{5,7},{6,4},{7,5},{8,10},{9,11},{10,... | collective-permute-start | bytes 196616 | tf_op jit(solution)/shard_map/ppermute | solution.py:24
  32.2 2.1 %collective-permute-start.13 = (bf16[64,512]{1,0:T(8,128)(2,1)S(1)}, bf16[64,512]{1,0:T(8,128)(2,1)S(1)}, u32[]{:S(2)}, u32[]{:S(2)}) collective-permute-start(bf16[64,512]{1,0:T(8,128)(2,1)S(1)} %choose_pieces.1.refs_0_), channel_id=1, source_target_pairs={{0,4},{1,5},{2,6},{3,7},{4,0},{5,1},{6,2},{7,3},{8,12},{9,13},{10,... | collective-permute-start | bytes 196616 | tf_op jit(solution)/shard_map/ppermute | solution.py:24
  34.3 0.6 %collective-permute-start.14 = (bf16[64,512]{1,0:T(8,128)(2,1)S(1)}, bf16[64,512]{1,0:T(8,128)(2,1)S(1)}, u32[]{:S(2)}, u32[]{:S(2)}) collective-permute-start(bf16[64,512]{1,0:T(8,128)(2,1)S(1)} %choose_pieces.1.refs_0_), channel_id=1, source_target_pairs={{0,6},{1,7},{2,4},{3,5},{4,2},{5,3},{6,0},{7,1},{8,14},{9,15},{10,... | collective-permute-start | bytes 196616 | tf_op jit(solution)/shard_map/ppermute | solution.py:24
  34.9 0.9 %keyvals.9.refs_0_ = bf16[3584,1024]{1,0:T(8,128)(2,1)S(1)} custom-call(bf16[256,512]{1,0:T(8,128)(2,1)S(1)} %collective-permute-done.11.first_ref, bf16[256,512]{1,0:T(8,128)(2,1)S(1)} %collective-permute-done.18.second_ref, bf16[512,1536]{1,0:T(8,128)(2,1)S(1)} %copy-done, bf16[3584,1024]{1,0:T(8,128)(2,1)S(1)} %keyvals.8.refs_0_), custom_call_target="tpu_custom_call", output_to_operand_aliasing={{}: (3, {})} | custom-call | flops 4294967296 | bytes 1572864 | tf_op jit(solution)/shard_map/keyvals/pallas_call | solution.py:79
  35.8 0.9 %keyvals.10.refs_0_ = bf16[3584,1024]{1,0:T(8,128)(2,1)S(1)} custom-call(bf16[256,512]{1,0:T(8,128)(2,1)S(1)} %collective-permute-done.10.first_ref, bf16[256,512]{1,0:T(8,128)(2,1)S(1)} %collective-permute-done.17.second_ref, bf16[512,1536]{1,0:T(8,128)(2,1)S(1)} %copy-done, bf16[3584,1024]{1,0:T(8,128)(2,1)S(1)} %keyvals.9.refs_0_), custom_call_target="tpu_custom_call", output_to_operand_aliasing={{}: (3, {})} | custom-call | flops 4294967296 | bytes 1572864 | tf_op jit(solution)/shard_map/keyvals/pallas_call | solution.py:79
  36.7 0.0 copy-start.1
  36.8 0.0 copy-start.2
  36.8 0.0 copy-start.4
  36.8 0.0 copy-start.5
  36.8 0.0 copy-start.6
  36.8 0.0 copy-start.7
  36.8 0.0 copy-start.8
  36.8 0.9 %keyvals.11.refs_8_ = bf16[3584,1024]{1,0:T(8,128)(2,1)S(1)} custom-call(bf16[256,512]{1,0:T(8,128)(2,1)S(1)} %collective-permute-done.15.first_ref, bf16[256,512]{1,0:T(8,128)(2,1)S(1)} %collective-permute-done.16.second_ref, bf16[512,1536]{1,0:T(8,128)(2,1)S(1)} %copy-done, bf16[3584,1024]{1,0:T(8,128)(2,1)S(1)} %keyvals.10.refs_0_), custom_call_target="tpu_custom_call", output_to_operand_aliasing={{}: (3, {})} | custom-call | flops 4294967296 | bytes 1572864 | tf_op jit(solution)/shard_map/keyvals/pallas_call | solution.py:79
  37.8 1.7 %collective-permute-done.14.refs_6_ = bf16[64,512]{1,0:T(8,128)(2,1)S(1)} collective-permute-done((bf16[64,512]{1,0:T(8,128)(2,1)S(1)}, bf16[64,512]{1,0:T(8,128)(2,1)S(1)}, u32[]{:S(2)}, u32[]{:S(2)}) %collective-permute-start.14) | collective-permute-done | bytes 65568 | tf_op jit(solution)/shard_map/ppermute | solution.py:24
  39.5 0.5 %collective-permute-start.20 = (bf16[64,512]{1,0:T(8,128)(2,1)S(1)}, bf16[64,512]{1,0:T(8,128)(2,1)S(1)}, u32[]{:S(2)}, u32[]{:S(2)}) collective-permute-start(bf16[64,512]{1,0:T(8,128)(2,1)S(1)} %collective-permute-done.12.refs_2_), channel_id=1, source_target_pairs={{0,1},{1,0},{2,3},{3,2},{4,5},{5,4},{6,7},{7,6},{8,9},{9,8},{10,11... | collective-permute-start | bytes 196616 | tf_op jit(solution)/shard_map/ppermute | solution.py:24
  40.0 0.0 collective-permute-start.21
  40.0 0.5 %collective-permute-start.22 = (bf16[64,512]{1,0:T(8,128)(2,1)S(1)}, bf16[64,512]{1,0:T(8,128)(2,1)S(1)}, u32[]{:S(2)}, u32[]{:S(2)}) collective-permute-start(bf16[64,512]{1,0:T(8,128)(2,1)S(1)} %collective-permute-done.14.refs_6_), channel_id=1, source_target_pairs={{0,1},{1,0},{2,3},{3,2},{4,5},{5,4},{6,7},{7,6},{8,9},{9,8},{10,11... | collective-permute-start | bytes 196616 | tf_op jit(solution)/shard_map/ppermute | solution.py:24
  40.5 0.2 collective-permute-done.19.refs_1_
  40.7 0.2 collective-permute-done.20.refs_3_
  40.9 0.4 collective-permute-done.21.refs_5_
  41.2 0.2 collective-permute-done.22.refs_7_
  41.4 5.7 %finish.1 = (bf16[256,512]{1,0:T(8,128)(2,1)}, bf16[3584,1024]{1,0:T(8,128)(2,1)S(1)}) custom-call(s32[8,8]{1,0:T(8,128)S(1)} %copy-done.8, bf16[256,512]{1,0:T(8,128)(2,1)S(1)} %copy-done.4, bf16[256,512]{1,0:T(8,128)(2,1)S(1)} %get-tuple-element.29.query_ref, s32[8,8,128,128]{3,2,1,0:T(8,128)S(1)} %copy-done.2, ...), custom_call_target="tpu_custom_call", output_to_operand_aliasing={{1}: (16, {})} | custom-call | tf_op jit(solution)/shard_map/finish/pallas_call | solution.py:230
  (28 shorter events, 0.1 us)
Async XLA Ops:
  0.0 5.4 %collective-permute-start.2 = (bf16[256,512]{1,0:T(8,128)(2,1)}, bf16[256,512]{1,0:T(8,128)(2,1)S(1)}, u32[]{:S(2)}, u32[]{:S(2)}) collective-permute-start(bf16[256,512]{1,0:T(8,128)(2,1)} %tokens_ref.1), channel_id=1, source_target_pairs={{0,1},{1,0},{2,3},{3,2},{4,5},{5,4},{6,7},{7,6},{8,9},{9,8},{10,11... | collective-permute-start | bytes 786440 | tf_op jit(solution)/shard_map/ppermute | solution.py:24
  0.5 12.4 %collective-permute-start = (bf16[256,512]{1,0:T(8,128)(2,1)}, bf16[256,512]{1,0:T(8,128)(2,1)S(1)}, u32[]{:S(2)}, u32[]{:S(2)}) collective-permute-start(bf16[256,512]{1,0:T(8,128)(2,1)} %tokens_ref.1), channel_id=1, source_target_pairs={{0,4},{1,5},{2,6},{3,7},{4,0},{5,1},{6,2},{7,3},{8,12},{9,13},{10,... | collective-permute-start | bytes 786440 | tf_op jit(solution)/shard_map/ppermute | solution.py:24
  2.9 10.1 %collective-permute-start.3 = (bf16[256,512]{1,0:T(8,128)(2,1)}, bf16[256,512]{1,0:T(8,128)(2,1)S(1)}, u32[]{:S(2)}, u32[]{:S(2)}) collective-permute-start(bf16[256,512]{1,0:T(8,128)(2,1)} %tokens_ref.1), channel_id=1, source_target_pairs={{0,2},{1,3},{2,0},{3,1},{4,6},{5,7},{6,4},{7,5},{8,10},{9,11},{10,... | collective-permute-start | bytes 786440 | tf_op jit(solution)/shard_map/ppermute | solution.py:24
  5.3 13.2 %copy-start.9 = (s32[4]{0:T(128)S(1)}, s32[4]{0:T(128)}, u32[]{:S(2)}) copy-start(s32[4]{0:T(128)} %hubs_ref.3) | copy-start | bytes 52
  5.3 7.5 %collective-permute-start.1 = (bf16[64,512]{1,0:T(8,128)(2,1)S(1)}, bf16[64,512]{1,0:T(8,128)(2,1)S(1)}, u32[]{:S(2)}, u32[]{:S(2)}) collective-permute-start(bf16[64,512]{1,0:T(8,128)(2,1)S(1)} %bitcast.3), channel_id=1, source_target_pairs={{0,6},{1,7},{2,4},{3,5},{4,2},{5,3},{6,0},{7,1},{8,14},{9,15},{10,... | collective-permute-start | bytes 196616 | tf_op jit(solution)/shard_map/ppermute | solution.py:24
  5.4 1.4 %copy-start = (bf16[512,1536]{1,0:T(8,128)(2,1)S(1)}, bf16[512,1536]{1,0:T(8,128)(2,1)}, u32[]{:S(2)}) copy-start(bf16[512,1536]{1,0:T(8,128)(2,1)} %w_qkv_ref.1) | copy-start | bytes 4718596
  6.8 0.9 %copy-start.3 = (bf16[256,512]{1,0:T(8,128)(2,1)S(1)}, bf16[256,512]{1,0:T(8,128)(2,1)}, u32[]{:S(2)}) copy-start(bf16[256,512]{1,0:T(8,128)(2,1)} %tokens_ref.1) | copy-start | bytes 786436
  13.0 5.6 %collective-permute-start.4 = (bf16[256,512]{1,0:T(8,128)(2,1)S(1)}, bf16[256,512]{1,0:T(8,128)(2,1)S(1)}, u32[]{:S(2)}, u32[]{:S(2)}) collective-permute-start(bf16[256,512]{1,0:T(8,128)(2,1)S(1)} %collective-permute-done.3.refs_2_.first_ref), channel_id=1, source_target_pairs={{0,1},{1,0},{2,3},{3,2},{4,5},{5,4},{6,7},{7,6},{8,9},{9,8},{10,11... | collective-permute-start | bytes 786440 | tf_op jit(solution)/shard_map/ppermute | solution.py:24
  13.0 5.6 %collective-permute-start.5 = (bf16[256,512]{1,0:T(8,128)(2,1)S(1)}, bf16[256,512]{1,0:T(8,128)(2,1)S(1)}, u32[]{:S(2)}, u32[]{:S(2)}) collective-permute-start(bf16[256,512]{1,0:T(8,128)(2,1)S(1)} %collective-permute-done.refs_4_.first_ref), channel_id=1, source_target_pairs={{0,1},{1,0},{2,3},{3,2},{4,5},{5,4},{6,7},{7,6},{8,9},{9,8},{10,11... | collective-permute-start | bytes 786440 | tf_op jit(solution)/shard_map/ppermute | solution.py:24
  13.5 5.1 %collective-permute-start.6 = (bf16[64,512]{1,0:T(8,128)(2,1)S(1)}, bf16[64,512]{1,0:T(8,128)(2,1)S(1)}, u32[]{:S(2)}, u32[]{:S(2)}) collective-permute-start(bf16[64,512]{1,0:T(8,128)(2,1)S(1)} %collective-permute-done.1.refs_6_), channel_id=1, source_target_pairs={{0,1},{1,0},{2,3},{3,2},{4,5},{5,4},{6,7},{7,6},{8,9},{9,8},{10,11... | collective-permute-start | bytes 196616 | tf_op jit(solution)/shard_map/ppermute | solution.py:24
  13.5 14.9 %collective-permute-start.11 = (bf16[256,512]{1,0:T(8,128)(2,1)S(1)}, bf16[256,512]{1,0:T(8,128)(2,1)S(1)}, u32[]{:S(2)}, u32[]{:S(2)}) collective-permute-start(bf16[256,512]{1,0:T(8,128)(2,1)S(1)} %collective-permute-done.3.refs_2_.first_ref), channel_id=1, source_target_pairs={{0,4},{1,5},{2,6},{3,7},{4,0},{5,1},{6,2},{7,3},{8,12},{9,13},{10,... | collective-permute-start | bytes 786440 | tf_op jit(solution)/shard_map/ppermute | solution.py:24
  14.8 11.9 %collective-permute-start.10 = (bf16[256,512]{1,0:T(8,128)(2,1)S(1)}, bf16[256,512]{1,0:T(8,128)(2,1)S(1)}, u32[]{:S(2)}, u32[]{:S(2)}) collective-permute-start(bf16[256,512]{1,0:T(8,128)(2,1)S(1)} %get-tuple-element.33), channel_id=1, source_target_pairs={{0,28},{1,29},{2,30},{3,31},{4,8},{5,9},{6,10},{7,11},{8,4},{9,5},... | collective-permute-start | bytes 786440 | tf_op jit(solution)/shard_map/ppermute | solution.py:24
  19.5 8.9 %collective-permute-start.7 = (bf16[64,512]{1,0:T(8,128)(2,1)S(1)}, bf16[64,512]{1,0:T(8,128)(2,1)S(1)}, u32[]{:S(2)}, u32[]{:S(2)}) collective-permute-start(bf16[64,512]{1,0:T(8,128)(2,1)S(1)} %pick_pieces.1.refs_0_), channel_id=1, source_target_pairs={{0,8},{1,9},{2,10},{3,11},{4,28},{5,29},{6,30},{7,31},{8,16},{9,17... | collective-permute-start | bytes 196616 | tf_op jit(solution)/shard_map/ppermute | solution.py:24
  19.5 9.9 %collective-permute-start.8 = (bf16[64,512]{1,0:T(8,128)(2,1)S(1)}, bf16[64,512]{1,0:T(8,128)(2,1)S(1)}, u32[]{:S(2)}, u32[]{:S(2)}) collective-permute-start(bf16[64,512]{1,0:T(8,128)(2,1)S(1)} %pick_pieces.1.refs_0_), channel_id=1, source_target_pairs={{0,16},{1,17},{2,18},{3,19},{4,20},{5,21},{6,22},{7,23},{8,24},{9,... | collective-permute-start | bytes 196616 | tf_op jit(solution)/shard_map/ppermute | solution.py:24
  20.5 8.9 %collective-permute-start.9 = (bf16[64,512]{1,0:T(8,128)(2,1)S(1)}, bf16[64,512]{1,0:T(8,128)(2,1)S(1)}, u32[]{:S(2)}, u32[]{:S(2)}) collective-permute-start(bf16[64,512]{1,0:T(8,128)(2,1)S(1)} %pick_pieces.1.refs_0_), channel_id=1, source_target_pairs={{0,24},{1,25},{2,26},{3,27},{4,12},{5,13},{6,14},{7,15},{8,0},{9,1... | collective-permute-start | bytes 196616 | tf_op jit(solution)/shard_map/ppermute | solution.py:24
  26.7 7.6 %collective-permute-start.15 = (bf16[256,512]{1,0:T(8,128)(2,1)S(1)}, bf16[256,512]{1,0:T(8,128)(2,1)S(1)}, u32[]{:S(2)}, u32[]{:S(2)}) collective-permute-start(bf16[256,512]{1,0:T(8,128)(2,1)S(1)} %collective-permute-done.10.first_ref), channel_id=1, source_target_pairs={{0,2},{1,3},{2,0},{3,1},{4,6},{5,7},{6,4},{7,5},{8,10},{9,11},{10,... | collective-permute-start | bytes 786440 | tf_op jit(solution)/shard_map/ppermute | solution.py:24
  29.4 5.5 %collective-permute-start.18 = (bf16[256,512]{1,0:T(8,128)(2,1)S(1)}, bf16[256,512]{1,0:T(8,128)(2,1)S(1)}, u32[]{:S(2)}, u32[]{:S(2)}) collective-permute-start(bf16[256,512]{1,0:T(8,128)(2,1)S(1)} %collective-permute-done.11.first_ref), channel_id=1, source_target_pairs={{0,1},{1,0},{2,3},{3,2},{4,5},{5,4},{6,7},{7,6},{8,9},{9,8},{10,11... | collective-permute-start | bytes 786440 | tf_op jit(solution)/shard_map/ppermute | solution.py:24
  29.4 6.4 %collective-permute-start.17 = (bf16[256,512]{1,0:T(8,128)(2,1)S(1)}, bf16[256,512]{1,0:T(8,128)(2,1)S(1)}, u32[]{:S(2)}, u32[]{:S(2)}) collective-permute-start(bf16[256,512]{1,0:T(8,128)(2,1)S(1)} %collective-permute-done.10.first_ref), channel_id=1, source_target_pairs={{0,1},{1,0},{2,3},{3,2},{4,5},{5,4},{6,7},{7,6},{8,9},{9,8},{10,11... | collective-permute-start | bytes 786440 | tf_op jit(solution)/shard_map/ppermute | solution.py:24
  30.6 7.1 %collective-permute-start.12 = (bf16[64,512]{1,0:T(8,128)(2,1)S(1)}, bf16[64,512]{1,0:T(8,128)(2,1)S(1)}, u32[]{:S(2)}, u32[]{:S(2)}) collective-permute-start(bf16[64,512]{1,0:T(8,128)(2,1)S(1)} %choose_pieces.1.refs_0_), channel_id=1, source_target_pairs={{0,2},{1,3},{2,0},{3,1},{4,6},{5,7},{6,4},{7,5},{8,10},{9,11},{10,... | collective-permute-start | bytes 196616 | tf_op jit(solution)/shard_map/ppermute | solution.py:24
  32.2 5.5 %collective-permute-start.13 = (bf16[64,512]{1,0:T(8,128)(2,1)S(1)}, bf16[64,512]{1,0:T(8,128)(2,1)S(1)}, u32[]{:S(2)}, u32[]{:S(2)}) collective-permute-start(bf16[64,512]{1,0:T(8,128)(2,1)S(1)} %choose_pieces.1.refs_0_), channel_id=1, source_target_pairs={{0,4},{1,5},{2,6},{3,7},{4,0},{5,1},{6,2},{7,3},{8,12},{9,13},{10,... | collective-permute-start | bytes 196616 | tf_op jit(solution)/shard_map/ppermute | solution.py:24
  34.3 5.2 %collective-permute-start.14 = (bf16[64,512]{1,0:T(8,128)(2,1)S(1)}, bf16[64,512]{1,0:T(8,128)(2,1)S(1)}, u32[]{:S(2)}, u32[]{:S(2)}) collective-permute-start(bf16[64,512]{1,0:T(8,128)(2,1)S(1)} %choose_pieces.1.refs_0_), channel_id=1, source_target_pairs={{0,6},{1,7},{2,4},{3,5},{4,2},{5,3},{6,0},{7,1},{8,14},{9,15},{10,... | collective-permute-start | bytes 196616 | tf_op jit(solution)/shard_map/ppermute | solution.py:24
  34.9 2.0 %collective-permute-start.16 = (bf16[256,512]{1,0:T(8,128)(2,1)S(1)}, bf16[256,512]{1,0:T(8,128)(2,1)S(1)}, u32[]{:S(2)}, u32[]{:S(2)}) collective-permute-start(bf16[256,512]{1,0:T(8,128)(2,1)S(1)} %collective-permute-done.15.first_ref), channel_id=1, source_target_pairs={{0,1},{1,0},{2,3},{3,2},{4,5},{5,4},{6,7},{7,6},{8,9},{9,8},{10,11... | collective-permute-start | bytes 786440 | tf_op jit(solution)/shard_map/ppermute | solution.py:24
  36.7 4.7 %copy-start.1 = (bf16[512,1536]{1,0:T(8,128)(2,1)S(1)}, bf16[512,1536]{1,0:T(8,128)(2,1)}, u32[]{:S(2)}) copy-start(bf16[512,1536]{1,0:T(8,128)(2,1)} %w_qkv_ref.1) | copy-start | bytes 4718596
  36.8 4.6 %copy-start.2 = (s32[8,8,128,128]{3,2,1,0:T(8,128)S(1)}, s32[8,8,128,128]{3,2,1,0:T(8,128)}, u32[]{:S(2)}) copy-start(s32[8,8,128,128]{3,2,1,0:T(8,128)} %mask_ref.1) | copy-start | bytes 12582916
  36.8 4.6 %copy-start.4 = (bf16[256,512]{1,0:T(8,128)(2,1)S(1)}, bf16[256,512]{1,0:T(8,128)(2,1)}, u32[]{:S(2)}) copy-start(bf16[256,512]{1,0:T(8,128)(2,1)} %tokens_ref.1) | copy-start | bytes 786436
  36.8 4.6 %copy-start.5 = (bf16[512,1024]{1,0:T(8,128)(2,1)S(1)}, bf16[512,1024]{1,0:T(8,128)(2,1)}, u32[]{:S(2)}) copy-start(bf16[512,1024]{1,0:T(8,128)(2,1)} %w_up_ref.1) | copy-start | bytes 3145732
  36.8 4.6 %copy-start.6 = (bf16[1024,512]{1,0:T(8,128)(2,1)S(1)}, bf16[1024,512]{1,0:T(8,128)(2,1)}, u32[]{:S(2)}) copy-start(bf16[1024,512]{1,0:T(8,128)(2,1)} %w_down_ref.1) | copy-start | bytes 3145732
  36.8 4.6 %copy-start.7 = (bf16[512,512]{1,0:T(8,128)(2,1)S(1)}, bf16[512,512]{1,0:T(8,128)(2,1)}, u32[]{:S(2)}) copy-start(bf16[512,512]{1,0:T(8,128)(2,1)} %w_out_ref.1) | copy-start | bytes 1572868
  36.8 4.6 %copy-start.8 = (s32[8,8]{1,0:T(8,128)S(1)}, s32[8,8]{1,0:T(8,128)}, u32[]{:S(2)}) copy-start(s32[8,8]{1,0:T(8,128)} %cols_ref.1) | copy-start | bytes 772
  39.5 1.3 %collective-permute-start.19 = (bf16[64,512]{1,0:T(8,128)(2,1)S(1)}, bf16[64,512]{1,0:T(8,128)(2,1)S(1)}, u32[]{:S(2)}, u32[]{:S(2)}) collective-permute-start(bf16[64,512]{1,0:T(8,128)(2,1)S(1)} %choose_pieces.1.refs_0_), channel_id=1, source_target_pairs={{0,1},{1,0},{2,3},{3,2},{4,5},{5,4},{6,7},{7,6},{8,9},{9,8},{10,11... | collective-permute-start | bytes 196616 | tf_op jit(solution)/shard_map/ppermute | solution.py:24
  39.5 1.4 %collective-permute-start.20 = (bf16[64,512]{1,0:T(8,128)(2,1)S(1)}, bf16[64,512]{1,0:T(8,128)(2,1)S(1)}, u32[]{:S(2)}, u32[]{:S(2)}) collective-permute-start(bf16[64,512]{1,0:T(8,128)(2,1)S(1)} %collective-permute-done.12.refs_2_), channel_id=1, source_target_pairs={{0,1},{1,0},{2,3},{3,2},{4,5},{5,4},{6,7},{7,6},{8,9},{9,8},{10,11... | collective-permute-start | bytes 196616 | tf_op jit(solution)/shard_map/ppermute | solution.py:24
  40.0 1.3 %collective-permute-start.21 = (bf16[64,512]{1,0:T(8,128)(2,1)S(1)}, bf16[64,512]{1,0:T(8,128)(2,1)S(1)}, u32[]{:S(2)}, u32[]{:S(2)}) collective-permute-start(bf16[64,512]{1,0:T(8,128)(2,1)S(1)} %collective-permute-done.13.refs_4_), channel_id=1, source_target_pairs={{0,1},{1,0},{2,3},{3,2},{4,5},{5,4},{6,7},{7,6},{8,9},{9,8},{10,11... | collective-permute-start | bytes 196616 | tf_op jit(solution)/shard_map/ppermute | solution.py:24
  40.0 1.4 %collective-permute-start.22 = (bf16[64,512]{1,0:T(8,128)(2,1)S(1)}, bf16[64,512]{1,0:T(8,128)(2,1)S(1)}, u32[]{:S(2)}, u32[]{:S(2)}) collective-permute-start(bf16[64,512]{1,0:T(8,128)(2,1)S(1)} %collective-permute-done.14.refs_6_), channel_id=1, source_target_pairs={{0,1},{1,0},{2,3},{3,2},{4,5},{5,4},{6,7},{7,6},{8,9},{9,8},{10,11... | collective-permute-start | bytes 196616 | tf_op jit(solution)/shard_map/ppermute | solution.py:24

commit v4 on v3

--- a/solution.py
+++ b/solution.py
@@ -58,28 +58,37 @@
         out_ref[...] = project(normed, w_ref, slice(0, heads * head_dim))
 
 
-def keyval_kernel(heads, head_dim, at, first_ref, second_ref, w_ref, *refs):
+def keyval_kernel(heads, head_dim, at, whence, first_ref, second_ref, w_ref, *refs):
     node_dev = first_ref.shape[0]
-    pool_ref = refs[-1] if at else refs[-3]
+    pool_ref = refs[-1] if at else refs[-4]
+    if not at:
+        hubs_ref, codes_ref = refs[0], refs[-1]
+        here, head_here = place()
+        for j in range(hubs_ref.shape[0]):
+            for i, code in enumerate(whence):
+                number = code(hubs_ref[j], here, head_here).astype(jnp.float32)
+                codes_ref[i, j * PIECE : (j + 1) * PIECE, :] = jnp.full((PIECE, 128), number)
     for k, ref in enumerate((first_ref, second_ref)):
         normed = layer_norm(ref[...].astype(jnp.float32))
         rows = slice((at + k) * node_dev, (at + k + 1) * node_dev)
         keyval_into(pool_ref, rows, normed, w_ref, heads, head_dim)
         if not at and not k:
-            query_into(refs[-2], normed, w_ref, heads, head_dim)
-            refs[-1][...] = ref[...]
-
-
-def keyvals(pool, at, first, second, w_qkv, heads, head_dim, blocks, after=()):
+            query_into(refs[-3], normed, w_ref, heads, head_dim)
+            refs[-2][...] = ref[...]
+
+
+def keyvals(pool, at, first, second, w_qkv, heads, head_dim, blocks, after=(), hub_blocks=None, whence=()):
     node_dev, width = first.shape
     out_shape = [jax.ShapeDtypeStruct((blocks * TB, 2 * width), jnp.bfloat16)]
     if not at:
         out_shape += [jax.ShapeDtypeStruct((node_dev, width), jnp.bfloat16)] * 2
-    operands = [first, second, w_qkv, *after] + ([pool] if at else [])
+        shape = (len(whence), hub_blocks.shape[0] * PIECE, 128)
+        out_shape.append(jax.ShapeDtypeStruct(shape, jnp.float32))
+    operands = [first, second, w_qkv, *after] + ([pool] if at else [hub_blocks])
     result = pl.pallas_call(
-        functools.partial(keyval_kernel, heads, head_dim, at),
+        functools.partial(keyval_kernel, heads, head_dim, at, whence),
         out_shape=out_shape,
-        in_specs=[VMEM] * 3 + [ANY] * len(after) + [VMEM] * bool(at),
+        in_specs=[VMEM] * 3 + [ANY] * len(after) + [VMEM if at else pl.BlockSpec(memory_space=pltpu.SMEM)],
         out_specs=[VMEM] * len(out_shape),
         input_output_aliases={len(operands) - 1: 0} if at else {},
         compiler_params=pltpu.CompilerParams(vmem_limit_bytes=8 << 20),
@@ -91,77 +100,71 @@
     return result if not at else result[0]
 
 
+def later(value, *first):
+    return lax.optimization_barrier((value, *first))[0]
+
+
 def place():
     return lax.axis_index("nodes"), lax.axis_index("heads")
 
 
-def copy_chosen(code, sources, out_ref, out_rows):
-    for k, (ref, row) in enumerate(sources):
-        @pl.when(code == k)
-        def _():
-            rows = pl.ds(pl.multiple_of(row, PIECE), PIECE)
-            out_ref[out_rows, :] = ref[rows, :]
-
-
-def pick_kernel(hub_count, per_group, local, heads, hubs_ref, *refs):
+def chosen(code_ref, at, rows, candidates):
+    width = candidates[0].shape[1]
+    code = jnp.concatenate([code_ref[at, rows, :]] * (width // 128), axis=1)
+    result = candidates[0].astype(jnp.float32)
+    for k, value in enumerate(candidates[1:], 1):
+        result = jnp.where(code == k, value.astype(jnp.float32), result)
+    return result.astype(jnp.bfloat16)
+
+
+def pick_kernel(hub_count, local, code_ref, *refs):
     *sources, piece_ref = refs
     here, head_here = place()
     piece = here % 2 * 4 + head_here % 4
+    candidates = []
+    for k, ref in enumerate(sources):
+        for slot in range(local):
+            row = slot * TB + piece * PIECE if k < 6 else (slot * 2 + head_here % 2) * PIECE
+            candidates.append(ref[pl.ds(pl.multiple_of(row, PIECE), PIECE), :])
     for j in range(hub_count):
-        owner_n = hubs_ref[j] // per_group
-        owner_h = hubs_ref[j] % per_group // local
-        slot = hubs_ref[j] % local
-        far = (owner_n // 2 != here // 2) | (owner_h // 4 != head_here // 4)
-        offset = (owner_n + here) % 2 * 4 + ((owner_h % 4) ^ (head_here % 4))
-        code = jnp.where(far, -1, offset)
-        whole = slot * TB + piece * PIECE
-        strip = slot * 2 * PIECE + head_here % 2 * PIECE
         rows = slice(j * PIECE, (j + 1) * PIECE)
-        copy_chosen(code, [(ref, whole if k < 6 else strip) for k, ref in enumerate(sources)], piece_ref, rows)
-
-        @pl.when(far)
-        def _():
-            piece_ref[rows, :] = jnp.zeros((PIECE, piece_ref.shape[1]), piece_ref.dtype)
-
-
-def pick_pieces(hub_blocks, sources, per_group, heads):
+        piece_ref[rows, :] = chosen(code_ref, 0, rows, candidates)
+
+
+def pick_pieces(codes, sources):
     node_dev, width = sources[0].shape
-    hub_count = hub_blocks.shape[0]
+    rows = codes.shape[1]
     return pl.pallas_call(
-        functools.partial(pick_kernel, hub_count, per_group, node_dev // TB, heads),
-        out_shape=jax.ShapeDtypeStruct((hub_count * PIECE, width), jnp.bfloat16),
-        in_specs=[pl.BlockSpec(memory_space=pltpu.SMEM)] + [VMEM] * 8,
+        functools.partial(pick_kernel, rows // PIECE, node_dev // TB),
+        out_shape=jax.ShapeDtypeStruct((rows, width), jnp.bfloat16),
+        in_specs=[VMEM] * (1 + len(sources)),
         out_specs=VMEM,
         compiler_params=pltpu.CompilerParams(vmem_limit_bytes=4 << 20),
         name="pick_pieces",
-    )(hub_blocks, *sources)
-
-
-def choose_kernel(hub_count, from_where, hubs_ref, *refs):
+    )(codes, *sources)
+
+
+def choose_kernel(at, code_ref, *refs):
     *sources, piece_ref = refs
-    here, head_here = place()
-    for j in range(hub_count):
-        code = from_where(hubs_ref[j], here, head_here)
-        rows = slice(j * PIECE, (j + 1) * PIECE)
-        copy_chosen(code, [(ref, j * PIECE) for ref in sources], piece_ref, rows)
-
-
-def choose_pieces(hub_blocks, sources, from_where):
+    piece_ref[...] = chosen(code_ref, at, slice(None), [ref[...] for ref in sources])
+
+
+def choose_pieces(codes, at, sources):
     return pl.pallas_call(
-        functools.partial(choose_kernel, hub_blocks.shape[0], from_where),
+        functools.partial(choose_kernel, at),
         out_shape=jax.ShapeDtypeStruct(sources[0].shape, jnp.bfloat16),
-        in_specs=[pl.BlockSpec(memory_space=pltpu.SMEM)] + [VMEM] * len(sources),
+        in_specs=[VMEM] * (1 + len(sources)),
         out_specs=VMEM,
         compiler_params=pltpu.CompilerParams(vmem_limit_bytes=4 << 20),
         name="choose_pieces",
-    )(hub_blocks, *sources)
+    )(codes, *sources)
 
 
 def finish_kernel(
     heads, head_dim, hub_count, hub_base, cols_ref,
     tokens_ref, query_ref, mask_ref, w_qkv_ref, w_out_ref, w_up_ref, w_down_ref, *refs
 ):
-    around, (_, out_ref, pool_ref, hub_rows, mask, attn, sem) = refs[:PIECES], refs[PIECES:]
+    around, (_, out_ref, pool_ref, hub_rows, mask, attn, sem) = refs[:2], refs[2:]
     node_dev, width = tokens_ref.shape
     local = node_dev // TB
     per_group, tiles = cols_ref.shape
@@ -169,11 +172,11 @@
     load = pltpu.make_async_copy(mask_ref.at[pl.ds(head_here * local, local)], mask, sem)
     load.start()
     mine = here % 2 * 4 + head_here % 4
-    for k, ref in enumerate(around):
+    for k in range(PIECES):
         for j in range(hub_count):
-            row = ref.shape[0] - (hub_count - j) * PIECE
+            row = (k // 2 * hub_count + j) * PIECE
             rows = pl.ds(pl.multiple_of(j * TB + (mine ^ k) * PIECE, PIECE), PIECE)
-            hub_rows[rows, :] = ref[row : row + PIECE, :]
+            hub_rows[rows, :] = around[k % 2][row : row + PIECE, :]
     hub_normed = layer_norm(hub_rows[...].astype(jnp.float32))
     hub_place = pool_ref.shape[0] // TB - hub_count
     keyval_into(pool_ref, slice(hub_place * TB, None), hub_normed, w_qkv_ref, heads, head_dim)
@@ -233,9 +236,9 @@
         in_specs=[pl.BlockSpec(memory_space=pltpu.SMEM)]
         + [VMEM] * 2
         + [pl.BlockSpec(memory_space=pltpu.HBM)]
-        + [VMEM] * (5 + PIECES),
+        + [VMEM] * 7,
         out_specs=[VMEM, VMEM],
-        input_output_aliases={8 + PIECES: 1},
+        input_output_aliases={10: 1},
         scratch_shapes=[
             pltpu.VMEM((hub_count * TB, width), bf16),
             pltpu.VMEM((node_dev // TB,) + mask.shape[1:], jnp.int32),
@@ -281,6 +284,38 @@
         keyvals, w_qkv=weights, heads=heads, head_dim=head_dim, blocks=3 * per_group + hub_count
     )
 
+    ring = areas == 4 and in_row == 1
+    steps = [1]
+    while steps[-1] * 4 < areas:
+        steps.append(steps[-1] * 4)
+
+    def reach(step):
+        return [s * step for s in (1, 2, 3) if s * step < areas]
+
+    def area_of(n, h):
+        return n // 2 * in_row + h // 4
+
+    def to_area(n, h, shift):
+        at = area_of(n, h) ^ shift
+        return at // in_row * 2 + n % 2, at % in_row * 4 + h % 4
+
+    def owner(block):
+        return block // per_group, block % per_group // local
+
+    def picked_from(block, here, head_here):
+        n, h = owner(block)
+        offset = (n + here) % 2 * 4 + ((h % 4) ^ (head_here % 4))
+        return offset * local + block % local
+
+    def ring_from(block, here, head_here):
+        ahead = area_of(here, head_here) + 4 - area_of(*owner(block))
+        return jnp.where(here % 2 == 0, ahead, 8 - ahead) % 4
+
+    def area_from(step):
+        return lambda block, here, head_here: (area_of(*owner(block)) ^ area_of(here, head_here)) // step % 4
+
+    whence = (picked_from, ring_from) if ring else (picked_from, *map(area_from, steps))
+
     other = range(2, heads, 2)
     sides = [side(tokens, o) for o in other]
     paired = pair(tokens)
@@ -289,15 +324,16 @@
     strip = lax.dynamic_slice_in_dim(tokens.reshape(local, TB, width), strip_at, 2 * PIECE, 1)
     strip = across(strip.reshape(local * 2 * PIECE, width))
     token_core = core(tokens)
-    pool, query, again = keyval(None, 0, tokens, token_core)
-    far = go(again, where=lambda n, h: (n - 1 + 2 * (n & 1), h))
-    paired, strip, pool, query, *sides = lax.optimization_barrier((paired, strip, pool, query, *sides))
+    pool, query, again, codes = keyval(None, 0, tokens, token_core, hub_blocks=hub_blocks, whence=whence)
+    paired, strip, pool, query, codes, *sides = lax.optimization_barrier((paired, strip, pool, query, codes, *sides))
+
+    far = along(paired)
 
     paired_core, strip_core = core(paired), core(strip)
     sides_core = [core(v) for v in sides]
-    paired_sides = [pair(v) for v in sides]
-    sources = [tokens, token_core, sides[0], sides_core[0], paired, paired_core, strip, strip_core]
-    piece = pick_pieces(hub_blocks, sources, per_group, heads)
+    paired_sides = [side(paired, o) for o in other]
+    sources = [again, token_core, sides[0], sides_core[0], paired, paired_core, strip, strip_core]
+    piece = pick_pieces(codes, sources)
 
     for k, (value, other_value) in enumerate(zip(sides, sides_core)):
         pool = keyval(pool, 2 + 2 * k, value, other_value, after=(piece,))
@@ -306,37 +342,14 @@
     far_core = core(far)
     pool = keyval(pool, heads, paired, paired_core)
 
-    def owner_area(block):
-        return block // per_group // 2 * in_row + block % per_group // local // 4
-
-    def area_of(here, head_here):
-        return here // 2 * in_row + head_here // 4
-
-    if areas == 4 and in_row == 1:
+    if ring:
         got = [piece, along(piece), along(piece, 2), along(piece, -1)]
         got, pool, paired_sides = lax.optimization_barrier((got, pool, paired_sides))
-
-        def from_where(block, here, head_here):
-            ahead = area_of(here, head_here) + 4 - owner_area(block)
-            return jnp.where(here % 2 == 0, ahead, 8 - ahead) % 4
-
-        piece = choose_pieces(hub_blocks, got, from_where)
+        piece = choose_pieces(codes, 1, got)
     else:
-
-        def to_area(n, h, shift):
-            at = (n // 2 * in_row + h // 4) ^ shift
-            return at // in_row * 2 + n % 2, at % in_row * 4 + h % 4
-
-        step = 1
-        while step < areas:
-            reach = [s * step for s in (1, 2, 3) if s * step < areas]
-            got = [go(piece, where=lambda n, h, s=s: to_area(n, h, s)) for s in reach]
-
-            def from_where(block, here, head_here, step=step):
-                return (owner_area(block) ^ area_of(here, head_here)) // step % 4
-
-            piece = choose_pieces(hub_blocks, [piece, *got], from_where)
-            step *= 4
+        for i, step in enumerate(steps):
+            got = [go(piece, where=lambda n, h, s=s: to_area(n, h, s)) for s in reach(step)]
+            piece = choose_pieces(codes, 1 + i, [piece, *got])
 
     around = [piece, side(piece), pair(piece), across(piece)]
     paired_sides_core = [core(v) for v in paired_sides]
@@ -347,7 +360,8 @@
         pool = keyval(pool, 2 * heads + 2 * k, value, other_value)
     around, pool = lax.optimization_barrier((around, pool))
 
-    around = [v for value in around for v in (value, core(value))]
+    around = jnp.concatenate(around, axis=0)
+    around = [around, core(around)]
     return finish(
         tile_cols, tokens, query, tile_mask, weights, w_out, w_up, w_down, around, pool, heads, head_dim, hub_count, per_group * nodes
     )

time: 47.4 us -> 45.4 us (0.958)
  starting transfers between devices: 20.4 us -> 18.6 us
  Pallas kernels: 13.1 us -> 12.2 us
  local copies, waits for them, and re-layouts: 3.28 us -> 3.96 us
    ppermute x23 -> x20, starting transfers between devices: 20.4 us -> 18.6 us  [send(): return lax.ppermute(value, AXES, pairs)]
    pallas_call x8, Pallas kernels: 7.37 us -> 6.47 us  [the longest x6 6.31 us: keyvals(): pl.pallas_call(functools.partial(keyval_kernel, heads, head_dim, at, when...]
    unnamed x20 -> x23, local copies, waits for them, and re-layouts: 2.41 us -> 3.07 us
    ppermute x23 -> x20, waiting for transfers between devices: 10.1 us -> 10.2 us  [send(): return lax.ppermute(value, AXES, pairs)]
  transfers between devices with their start and end apart: 23 -> 20, of which waited for: 9 -> 7; matrix products, arithmetic and copies ran while one was open for 2% -> 2% of each run, Pallas kernels for 16% -> 14%
where the time goes in v4:
time: 45.4 us; the launch traced here: 45.1 us
  starting transfers between devices  18.6 us (41%)
  Pallas kernels  12.2 us (27%)
  waiting for transfers between devices  10.2 us (22%)
  local copies, waits for them, and re-layouts  3.96 us (9%)
    ppermute x20, starting transfers between devices, send(): return lax.ppermute(value, AXES, pairs)  18.6 us
    ppermute x20, waiting for transfers between devices, send(): return lax.ppermute(value, AXES, pairs)  10.2 us
    pallas_call x6, Pallas kernels, keyvals(): pl.pallas_call(functools.partial(keyval_kernel, heads, head_dim, at, when...  6.31 us
    pallas_call x1, Pallas kernels, finish(): pl.pallas_call(functools.partial(finish_kernel, heads, head_dim, hub_coun...  5.72 us
    unnamed x23, local copies, waits for them, and re-layouts  3.07 us
  transfers between devices with their start and end apart: 20, of which 7 were waited for; matrix products, arithmetic and copies ran while one was open for 2% of the time, Pallas kernels for 14%

profile of v4, /device:TPU:0, one launch (start us, length us, event | category | flops | bytes accessed | tf_op | source)
XLA Modules:
  0.0 45.1 jit_solution(5373338247607624094)
XLA Ops:
  0.0 0.5 %collective-permute-start.2 = (bf16[256,512]{1,0:T(8,128)(2,1)}, bf16[256,512]{1,0:T(8,128)(2,1)S(1)}, u32[]{:S(2)}, u32[]{:S(2)}) collective-permute-start(bf16[256,512]{1,0:T(8,128)(2,1)} %tokens_ref.1), channel_id=1, source_target_pairs={{0,1},{1,0},{2,3},{3,2},{4,5},{5,4},{6,7},{7,6},{8,9},{9,8},{10,11... | collective-permute-start | bytes 786440 | tf_op jit(solution)/shard_map/ppermute | solution.py:24
  0.5 2.5 %collective-permute-start = (bf16[256,512]{1,0:T(8,128)(2,1)}, bf16[256,512]{1,0:T(8,128)(2,1)S(1)}, u32[]{:S(2)}, u32[]{:S(2)}) collective-permute-start(bf16[256,512]{1,0:T(8,128)(2,1)} %tokens_ref.1), channel_id=1, source_target_pairs={{0,4},{1,5},{2,6},{3,7},{4,0},{5,1},{6,2},{7,3},{8,12},{9,13},{10,... | collective-permute-start | bytes 786440 | tf_op jit(solution)/shard_map/ppermute | solution.py:24
  2.9 1.5 %collective-permute-start.3 = (bf16[256,512]{1,0:T(8,128)(2,1)}, bf16[256,512]{1,0:T(8,128)(2,1)S(1)}, u32[]{:S(2)}, u32[]{:S(2)}) collective-permute-start(bf16[256,512]{1,0:T(8,128)(2,1)} %tokens_ref.1), channel_id=1, source_target_pairs={{0,2},{1,3},{2,0},{3,1},{4,6},{5,7},{6,4},{7,5},{8,10},{9,11},{10,... | collective-permute-start | bytes 786440 | tf_op jit(solution)/shard_map/ppermute | solution.py:24
  4.5 0.9 %constant_dynamic-slice_fusion = bf16[2,32,512]{2,1,0:T(8,128)(2,1)S(1)} fusion(bf16[2,128,512]{2,1,0:T(8,128)(2,1)} %bitcast.2, s32[]{:T(128)S(6)} %select_n.21), kind=kLoop, calls=%fused_computation.4 | loop fusion | bytes 131076 | tf_op jit(solution)/shard_map/dynamic_slice | solution.py:324
  5.3 0.0 collective-permute-start.1
  5.4 0.0 collective-permute-done.2.second_ref.refs_1_
  5.4 1.4 %copy-done = bf16[512,1536]{1,0:T(8,128)(2,1)S(1)} copy-done((bf16[512,1536]{1,0:T(8,128)(2,1)S(1)}, bf16[512,1536]{1,0:T(8,128)(2,1)}, u32[]{:S(2)}) %copy-start) | copy-done | bytes 1572888
  6.8 0.9 %copy-done.6 = bf16[256,512]{1,0:T(8,128)(2,1)S(1)} copy-done((bf16[256,512]{1,0:T(8,128)(2,1)S(1)}, bf16[256,512]{1,0:T(8,128)(2,1)}, u32[]{:S(2)}) %copy-start.6) | copy-done | bytes 262168
  7.8 0.7 %copy-done.9 = s32[4]{0:T(128)S(1)} copy-done((s32[4]{0:T(128)S(1)}, s32[4]{0:T(128)}, u32[]{:S(2)}) %copy-start.9) | copy-done | bytes 40
  8.4 1.7 %keyvals.6 = (bf16[3584,1024]{1,0:T(8,128)(2,1)S(1)}, bf16[256,512]{1,0:T(8,128)(2,1)S(1)}, bf16[256,512]{1,0:T(8,128)(2,1)S(1)}, f32[2,64,128]{2,1,0:T(8,128)S(1)}) custom-call(bf16[256,512]{1,0:T(8,128)(2,1)S(1)} %copy-done.6, bf16[256,512]{1,0:T(8,128)(2,1)S(1)} %collective-permute-done.2.second_ref.refs_1_, bf16[512,1536]{1,0:T(8,128)(2,1)S(1)} %copy-done, ...), custom_call_target="tpu_custom_call" | custom-call | flops 4294967296 | bytes 1572864 | tf_op jit(solution)/shard_map/keyvals/pallas_call | solution.py:88
  10.1 2.7 %collective-permute-done.1.refs_6_ = bf16[64,512]{1,0:T(8,128)(2,1)S(1)} collective-permute-done((bf16[64,512]{1,0:T(8,128)(2,1)S(1)}, bf16[64,512]{1,0:T(8,128)(2,1)S(1)}, u32[]{:S(2)}, u32[]{:S(2)}) %collective-permute-start.1) | collective-permute-done | bytes 65568 | tf_op jit(solution)/shard_map/ppermute | solution.py:24
  12.8 0.0 collective-permute-done.refs_4_.first_ref
  12.9 0.1 collective-permute-done.3.refs_2_.first_ref
  13.0 0.0 collective-permute-start.4
  13.0 0.5 %collective-permute-start.5 = (bf16[256,512]{1,0:T(8,128)(2,1)S(1)}, bf16[256,512]{1,0:T(8,128)(2,1)S(1)}, u32[]{:S(2)}, u32[]{:S(2)}) collective-permute-start(bf16[256,512]{1,0:T(8,128)(2,1)S(1)} %collective-permute-done.refs_4_.first_ref), channel_id=1, source_target_pairs={{0,1},{1,0},{2,3},{3,2},{4,5},{5,4},{6,7},{7,6},{8,9},{9,8},{10,11... | collective-permute-start | bytes 786440 | tf_op jit(solution)/shard_map/ppermute | solution.py:24
  13.5 0.0 collective-permute-start.6
  13.5 1.6 %collective-permute-start.10 = (bf16[256,512]{1,0:T(8,128)(2,1)S(1)}, bf16[256,512]{1,0:T(8,128)(2,1)S(1)}, u32[]{:S(2)}, u32[]{:S(2)}) collective-permute-start(bf16[256,512]{1,0:T(8,128)(2,1)S(1)} %collective-permute-done.refs_4_.first_ref), channel_id=1, source_target_pairs={{0,8},{1,9},{2,10},{3,11},{4,28},{5,29},{6,30},{7,31},{8,16},{9,17... | collective-permute-start | bytes 786440 | tf_op jit(solution)/shard_map/ppermute | solution.py:24
  15.1 1.5 %collective-permute-start.11 = (bf16[256,512]{1,0:T(8,128)(2,1)S(1)}, bf16[256,512]{1,0:T(8,128)(2,1)S(1)}, u32[]{:S(2)}, u32[]{:S(2)}) collective-permute-start(bf16[256,512]{1,0:T(8,128)(2,1)S(1)} %collective-permute-done.refs_4_.first_ref), channel_id=1, source_target_pairs={{0,2},{1,3},{2,0},{3,1},{4,6},{5,7},{6,4},{7,5},{8,10},{9,11},{10,... | collective-permute-start | bytes 786440 | tf_op jit(solution)/shard_map/ppermute | solution.py:24
  16.6 0.1 pick_pieces.1.refs_0_
  16.7 1.6 %collective-permute-start.7 = (bf16[64,512]{1,0:T(8,128)(2,1)S(1)}, bf16[64,512]{1,0:T(8,128)(2,1)S(1)}, u32[]{:S(2)}, u32[]{:S(2)}) collective-permute-start(bf16[64,512]{1,0:T(8,128)(2,1)S(1)} %pick_pieces.1.refs_0_), channel_id=1, source_target_pairs={{0,8},{1,9},{2,10},{3,11},{4,28},{5,29},{6,30},{7,31},{8,16},{9,17... | collective-permute-start | bytes 196616 | tf_op jit(solution)/shard_map/ppermute | solution.py:24
  18.4 1.2 %collective-permute-start.8 = (bf16[64,512]{1,0:T(8,128)(2,1)S(1)}, bf16[64,512]{1,0:T(8,128)(2,1)S(1)}, u32[]{:S(2)}, u32[]{:S(2)}) collective-permute-start(bf16[64,512]{1,0:T(8,128)(2,1)S(1)} %pick_pieces.1.refs_0_), channel_id=1, source_target_pairs={{0,16},{1,17},{2,18},{3,19},{4,20},{5,21},{6,22},{7,23},{8,24},{9,... | collective-permute-start | bytes 196616 | tf_op jit(solution)/shard_map/ppermute | solution.py:24
  19.6 2.7 %collective-permute-start.9 = (bf16[64,512]{1,0:T(8,128)(2,1)S(1)}, bf16[64,512]{1,0:T(8,128)(2,1)S(1)}, u32[]{:S(2)}, u32[]{:S(2)}) collective-permute-start(bf16[64,512]{1,0:T(8,128)(2,1)S(1)} %pick_pieces.1.refs_0_), channel_id=1, source_target_pairs={{0,24},{1,25},{2,26},{3,27},{4,12},{5,13},{6,14},{7,15},{8,0},{9,1... | collective-permute-start | bytes 196616 | tf_op jit(solution)/shard_map/ppermute | solution.py:24
  22.3 0.9 %keyvals.7.refs_0_ = bf16[3584,1024]{1,0:T(8,128)(2,1)S(1)} custom-call(bf16[256,512]{1,0:T(8,128)(2,1)S(1)} %collective-permute-done.3.refs_2_.first_ref, bf16[256,512]{1,0:T(8,128)(2,1)S(1)} %collective-permute-done.4.refs_3_.second_ref, bf16[512,1536]{1,0:T(8,128)(2,1)S(1)} %copy-done, ...), custom_call_target="tpu_custom_call", output_to_operand_aliasing={{}: (4, {})} | custom-call | flops 4294967296 | bytes 1572864 | tf_op jit(solution)/shard_map/keyvals/pallas_call | solution.py:88
  23.2 1.4 %collective-permute-done.10.first_ref = bf16[256,512]{1,0:T(8,128)(2,1)S(1)} collective-permute-done((bf16[256,512]{1,0:T(8,128)(2,1)S(1)}, bf16[256,512]{1,0:T(8,128)(2,1)S(1)}, u32[]{:S(2)}, u32[]{:S(2)}) %collective-permute-start.10) | collective-permute-done | bytes 262176 | tf_op jit(solution)/shard_map/ppermute | solution.py:24
  24.6 1.5 %collective-permute-start.15 = (bf16[256,512]{1,0:T(8,128)(2,1)S(1)}, bf16[256,512]{1,0:T(8,128)(2,1)S(1)}, u32[]{:S(2)}, u32[]{:S(2)}) collective-permute-start(bf16[256,512]{1,0:T(8,128)(2,1)S(1)} %collective-permute-done.10.first_ref), channel_id=1, source_target_pairs={{0,2},{1,3},{2,0},{3,1},{4,6},{5,7},{6,4},{7,5},{8,10},{9,11},{10,... | collective-permute-start | bytes 786440 | tf_op jit(solution)/shard_map/ppermute | solution.py:24
  26.1 0.9 %keyvals.8.refs_0_ = bf16[3584,1024]{1,0:T(8,128)(2,1)S(1)} custom-call(bf16[256,512]{1,0:T(8,128)(2,1)S(1)} %collective-permute-done.refs_4_.first_ref, bf16[256,512]{1,0:T(8,128)(2,1)S(1)} %collective-permute-done.5.refs_5_.second_ref, bf16[512,1536]{1,0:T(8,128)(2,1)S(1)} %copy-done, ...), custom_call_target="tpu_custom_call", output_to_operand_aliasing={{}: (3, {})} | custom-call | flops 4294967296 | bytes 1572864 | tf_op jit(solution)/shard_map/keyvals/pallas_call | solution.py:88
  27.1 1.4 %collective-permute-done.8.refs_2_ = bf16[64,512]{1,0:T(8,128)(2,1)S(1)} collective-permute-done((bf16[64,512]{1,0:T(8,128)(2,1)S(1)}, bf16[64,512]{1,0:T(8,128)(2,1)S(1)}, u32[]{:S(2)}, u32[]{:S(2)}) %collective-permute-start.8) | collective-permute-done | bytes 65568 | tf_op jit(solution)/shard_map/ppermute | solution.py:24
  28.4 0.0 collective-permute-start.18
  28.4 0.5 %collective-permute-start.17 = (bf16[256,512]{1,0:T(8,128)(2,1)S(1)}, bf16[256,512]{1,0:T(8,128)(2,1)S(1)}, u32[]{:S(2)}, u32[]{:S(2)}) collective-permute-start(bf16[256,512]{1,0:T(8,128)(2,1)S(1)} %collective-permute-done.10.first_ref), channel_id=1, source_target_pairs={{0,1},{1,0},{2,3},{3,2},{4,5},{5,4},{6,7},{7,6},{8,9},{9,8},{10,11... | collective-permute-start | bytes 786440 | tf_op jit(solution)/shard_map/ppermute | solution.py:24
  29.0 1.6 %collective-permute-start.12 = (bf16[64,512]{1,0:T(8,128)(2,1)S(1)}, bf16[64,512]{1,0:T(8,128)(2,1)S(1)}, u32[]{:S(2)}, u32[]{:S(2)}) collective-permute-start(bf16[64,512]{1,0:T(8,128)(2,1)S(1)} %choose_pieces.1), channel_id=1, source_target_pairs={{0,2},{1,3},{2,0},{3,1},{4,6},{5,7},{6,4},{7,5},{8,10},{9,11},{10,... | collective-permute-start | bytes 196616 | tf_op jit(solution)/shard_map/ppermute | solution.py:24
  30.6 1.0 %collective-permute-start.13 = (bf16[64,512]{1,0:T(8,128)(2,1)S(1)}, bf16[64,512]{1,0:T(8,128)(2,1)S(1)}, u32[]{:S(2)}, u32[]{:S(2)}) collective-permute-start(bf16[64,512]{1,0:T(8,128)(2,1)S(1)} %choose_pieces.1), channel_id=1, source_target_pairs={{0,4},{1,5},{2,6},{3,7},{4,0},{5,1},{6,2},{7,3},{8,12},{9,13},{10,... | collective-permute-start | bytes 196616 | tf_op jit(solution)/shard_map/ppermute | solution.py:24
  31.5 1.0 %collective-permute-done.15.first_ref = bf16[256,512]{1,0:T(8,128)(2,1)S(1)} collective-permute-done((bf16[256,512]{1,0:T(8,128)(2,1)S(1)}, bf16[256,512]{1,0:T(8,128)(2,1)S(1)}, u32[]{:S(2)}, u32[]{:S(2)}) %collective-permute-start.15) | collective-permute-done | bytes 262176 | tf_op jit(solution)/shard_map/ppermute | solution.py:24
  32.6 0.3 collective-permute-start.14
  32.8 0.9 %keyvals.9.refs_0_ = bf16[3584,1024]{1,0:T(8,128)(2,1)S(1)} custom-call(bf16[256,512]{1,0:T(8,128)(2,1)S(1)} %collective-permute-done.11.first_ref, bf16[256,512]{1,0:T(8,128)(2,1)S(1)} %collective-permute-done.18.second_ref, bf16[512,1536]{1,0:T(8,128)(2,1)S(1)} %copy-done, bf16[3584,1024]{1,0:T(8,128)(2,1)S(1)} %keyvals.8.refs_0_), custom_call_target="tpu_custom_call", output_to_operand_aliasing={{}: (3, {})} | custom-call | flops 4294967296 | bytes 1572864 | tf_op jit(solution)/shard_map/keyvals/pallas_call | solution.py:88
  33.8 0.9 %keyvals.10.refs_0_ = bf16[3584,1024]{1,0:T(8,128)(2,1)S(1)} custom-call(bf16[256,512]{1,0:T(8,128)(2,1)S(1)} %collective-permute-done.10.first_ref, bf16[256,512]{1,0:T(8,128)(2,1)S(1)} %collective-permute-done.17.second_ref, bf16[512,1536]{1,0:T(8,128)(2,1)S(1)} %copy-done, bf16[3584,1024]{1,0:T(8,128)(2,1)S(1)} %keyvals.9.refs_0_), custom_call_target="tpu_custom_call", output_to_operand_aliasing={{}: (3, {})} | custom-call | flops 4294967296 | bytes 1572864 | tf_op jit(solution)/shard_map/keyvals/pallas_call | solution.py:88
  34.7 0.0 copy-start.1
  34.7 0.0 copy-start.2
  34.7 0.0 copy-start.3
  34.7 0.0 copy-start.4
  34.8 0.0 copy-start.5
  34.8 0.0 copy-start.7
  34.8 0.0 copy-start.8
  34.8 0.9 %keyvals.11.refs_2_ = bf16[3584,1024]{1,0:T(8,128)(2,1)S(1)} custom-call(bf16[256,512]{1,0:T(8,128)(2,1)S(1)} %collective-permute-done.15.first_ref, bf16[256,512]{1,0:T(8,128)(2,1)S(1)} %collective-permute-done.16.second_ref, bf16[512,1536]{1,0:T(8,128)(2,1)S(1)} %copy-done, bf16[3584,1024]{1,0:T(8,128)(2,1)S(1)} %keyvals.10.refs_0_), custom_call_target="tpu_custom_call", output_to_operand_aliasing={{}: (3, {})} | custom-call | flops 4294967296 | bytes 1572864 | tf_op jit(solution)/shard_map/keyvals/pallas_call | solution.py:88
  35.7 0.0 collective-permute-done.13
  35.7 2.0 %collective-permute-done.14 = bf16[64,512]{1,0:T(8,128)(2,1)S(1)} collective-permute-done((bf16[64,512]{1,0:T(8,128)(2,1)S(1)}, bf16[64,512]{1,0:T(8,128)(2,1)S(1)}, u32[]{:S(2)}, u32[]{:S(2)}) %collective-permute-start.14) | collective-permute-done | bytes 65568 | tf_op jit(solution)/shard_map/ppermute | solution.py:24
  37.8 0.1 collective-permute-start.19
  37.8 1.5 %collective-permute-done.19.refs_1_ = bf16[256,512]{1,0:T(8,128)(2,1)S(1)} collective-permute-done((bf16[256,512]{1,0:T(8,128)(2,1)S(1)}, bf16[256,512]{1,0:T(8,128)(2,1)S(1)}, u32[]{:S(2)}, u32[]{:S(2)}) %collective-permute-start.19) | collective-permute-done | bytes 262176 | tf_op jit(solution)/shard_map/ppermute | solution.py:24
  39.4 5.7 %finish.1 = (bf16[256,512]{1,0:T(8,128)(2,1)}, bf16[3584,1024]{1,0:T(8,128)(2,1)S(1)}) custom-call(s32[8,8]{1,0:T(8,128)S(1)} %copy-done.8, bf16[256,512]{1,0:T(8,128)(2,1)S(1)} %copy-done.7, bf16[256,512]{1,0:T(8,128)(2,1)S(1)} %get-tuple-element.32.query_ref, s32[8,8,128,128]{3,2,1,0:T(8,128)S(1)} %copy-done.2, ...), custom_call_target="tpu_custom_call", output_to_operand_aliasing={{1}: (10, {})} | custom-call | tf_op jit(solution)/shard_map/finish/pallas_call | solution.py:233
  (26 shorter events, 0.1 us)
Async XLA Ops:
  0.0 5.4 %collective-permute-start.2 = (bf16[256,512]{1,0:T(8,128)(2,1)}, bf16[256,512]{1,0:T(8,128)(2,1)S(1)}, u32[]{:S(2)}, u32[]{:S(2)}) collective-permute-start(bf16[256,512]{1,0:T(8,128)(2,1)} %tokens_ref.1), channel_id=1, source_target_pairs={{0,1},{1,0},{2,3},{3,2},{4,5},{5,4},{6,7},{7,6},{8,9},{9,8},{10,11... | collective-permute-start | bytes 786440 | tf_op jit(solution)/shard_map/ppermute | solution.py:24
  0.5 12.4 %collective-permute-start = (bf16[256,512]{1,0:T(8,128)(2,1)}, bf16[256,512]{1,0:T(8,128)(2,1)S(1)}, u32[]{:S(2)}, u32[]{:S(2)}) collective-permute-start(bf16[256,512]{1,0:T(8,128)(2,1)} %tokens_ref.1), channel_id=1, source_target_pairs={{0,4},{1,5},{2,6},{3,7},{4,0},{5,1},{6,2},{7,3},{8,12},{9,13},{10,... | collective-permute-start | bytes 786440 | tf_op jit(solution)/shard_map/ppermute | solution.py:24
  2.9 10.1 %collective-permute-start.3 = (bf16[256,512]{1,0:T(8,128)(2,1)}, bf16[256,512]{1,0:T(8,128)(2,1)S(1)}, u32[]{:S(2)}, u32[]{:S(2)}) collective-permute-start(bf16[256,512]{1,0:T(8,128)(2,1)} %tokens_ref.1), channel_id=1, source_target_pairs={{0,2},{1,3},{2,0},{3,1},{4,6},{5,7},{6,4},{7,5},{8,10},{9,11},{10,... | collective-permute-start | bytes 786440 | tf_op jit(solution)/shard_map/ppermute | solution.py:24
  5.3 7.5 %collective-permute-start.1 = (bf16[64,512]{1,0:T(8,128)(2,1)S(1)}, bf16[64,512]{1,0:T(8,128)(2,1)S(1)}, u32[]{:S(2)}, u32[]{:S(2)}) collective-permute-start(bf16[64,512]{1,0:T(8,128)(2,1)S(1)} %bitcast.3), channel_id=1, source_target_pairs={{0,6},{1,7},{2,4},{3,5},{4,2},{5,3},{6,0},{7,1},{8,14},{9,15},{10,... | collective-permute-start | bytes 196616 | tf_op jit(solution)/shard_map/ppermute | solution.py:24
  5.4 1.4 %copy-start = (bf16[512,1536]{1,0:T(8,128)(2,1)S(1)}, bf16[512,1536]{1,0:T(8,128)(2,1)}, u32[]{:S(2)}) copy-start(bf16[512,1536]{1,0:T(8,128)(2,1)} %w_qkv_ref.1) | copy-start | bytes 4718596
  6.8 0.9 %copy-start.6 = (bf16[256,512]{1,0:T(8,128)(2,1)S(1)}, bf16[256,512]{1,0:T(8,128)(2,1)}, u32[]{:S(2)}) copy-start(bf16[256,512]{1,0:T(8,128)(2,1)} %tokens_ref.1) | copy-start | bytes 786436
  7.7 0.7 %copy-start.9 = (s32[4]{0:T(128)S(1)}, s32[4]{0:T(128)}, u32[]{:S(2)}) copy-start(s32[4]{0:T(128)} %refs_0_.1) | copy-start | bytes 52
  13.0 3.6 %collective-permute-start.4 = (bf16[256,512]{1,0:T(8,128)(2,1)S(1)}, bf16[256,512]{1,0:T(8,128)(2,1)S(1)}, u32[]{:S(2)}, u32[]{:S(2)}) collective-permute-start(bf16[256,512]{1,0:T(8,128)(2,1)S(1)} %collective-permute-done.3.refs_2_.first_ref), channel_id=1, source_target_pairs={{0,1},{1,0},{2,3},{3,2},{4,5},{5,4},{6,7},{7,6},{8,9},{9,8},{10,11... | collective-permute-start | bytes 786440 | tf_op jit(solution)/shard_map/ppermute | solution.py:24
  13.0 3.6 %collective-permute-start.5 = (bf16[256,512]{1,0:T(8,128)(2,1)S(1)}, bf16[256,512]{1,0:T(8,128)(2,1)S(1)}, u32[]{:S(2)}, u32[]{:S(2)}) collective-permute-start(bf16[256,512]{1,0:T(8,128)(2,1)S(1)} %collective-permute-done.refs_4_.first_ref), channel_id=1, source_target_pairs={{0,1},{1,0},{2,3},{3,2},{4,5},{5,4},{6,7},{7,6},{8,9},{9,8},{10,11... | collective-permute-start | bytes 786440 | tf_op jit(solution)/shard_map/ppermute | solution.py:24
  13.5 3.1 %collective-permute-start.6 = (bf16[64,512]{1,0:T(8,128)(2,1)S(1)}, bf16[64,512]{1,0:T(8,128)(2,1)S(1)}, u32[]{:S(2)}, u32[]{:S(2)}) collective-permute-start(bf16[64,512]{1,0:T(8,128)(2,1)S(1)} %collective-permute-done.1.refs_6_), channel_id=1, source_target_pairs={{0,1},{1,0},{2,3},{3,2},{4,5},{5,4},{6,7},{7,6},{8,9},{9,8},{10,11... | collective-permute-start | bytes 196616 | tf_op jit(solution)/shard_map/ppermute | solution.py:24
  13.5 11.1 %collective-permute-start.10 = (bf16[256,512]{1,0:T(8,128)(2,1)S(1)}, bf16[256,512]{1,0:T(8,128)(2,1)S(1)}, u32[]{:S(2)}, u32[]{:S(2)}) collective-permute-start(bf16[256,512]{1,0:T(8,128)(2,1)S(1)} %collective-permute-done.refs_4_.first_ref), channel_id=1, source_target_pairs={{0,8},{1,9},{2,10},{3,11},{4,28},{5,29},{6,30},{7,31},{8,16},{9,17... | collective-permute-start | bytes 786440 | tf_op jit(solution)/shard_map/ppermute | solution.py:24
  15.1 12.0 %collective-permute-start.11 = (bf16[256,512]{1,0:T(8,128)(2,1)S(1)}, bf16[256,512]{1,0:T(8,128)(2,1)S(1)}, u32[]{:S(2)}, u32[]{:S(2)}) collective-permute-start(bf16[256,512]{1,0:T(8,128)(2,1)S(1)} %collective-permute-done.refs_4_.first_ref), channel_id=1, source_target_pairs={{0,2},{1,3},{2,0},{3,1},{4,6},{5,7},{6,4},{7,5},{8,10},{9,11},{10,... | collective-permute-start | bytes 786440 | tf_op jit(solution)/shard_map/ppermute | solution.py:24
  16.7 10.3 %collective-permute-start.7 = (bf16[64,512]{1,0:T(8,128)(2,1)S(1)}, bf16[64,512]{1,0:T(8,128)(2,1)S(1)}, u32[]{:S(2)}, u32[]{:S(2)}) collective-permute-start(bf16[64,512]{1,0:T(8,128)(2,1)S(1)} %pick_pieces.1.refs_0_), channel_id=1, source_target_pairs={{0,8},{1,9},{2,10},{3,11},{4,28},{5,29},{6,30},{7,31},{8,16},{9,17... | collective-permute-start | bytes 196616 | tf_op jit(solution)/shard_map/ppermute | solution.py:24
  18.4 10.1 %collective-permute-start.8 = (bf16[64,512]{1,0:T(8,128)(2,1)S(1)}, bf16[64,512]{1,0:T(8,128)(2,1)S(1)}, u32[]{:S(2)}, u32[]{:S(2)}) collective-permute-start(bf16[64,512]{1,0:T(8,128)(2,1)S(1)} %pick_pieces.1.refs_0_), channel_id=1, source_target_pairs={{0,16},{1,17},{2,18},{3,19},{4,20},{5,21},{6,22},{7,23},{8,24},{9,... | collective-permute-start | bytes 196616 | tf_op jit(solution)/shard_map/ppermute | solution.py:24
  19.6 8.8 %collective-permute-start.9 = (bf16[64,512]{1,0:T(8,128)(2,1)S(1)}, bf16[64,512]{1,0:T(8,128)(2,1)S(1)}, u32[]{:S(2)}, u32[]{:S(2)}) collective-permute-start(bf16[64,512]{1,0:T(8,128)(2,1)S(1)} %pick_pieces.1.refs_0_), channel_id=1, source_target_pairs={{0,24},{1,25},{2,26},{3,27},{4,12},{5,13},{6,14},{7,15},{8,0},{9,1... | collective-permute-start | bytes 196616 | tf_op jit(solution)/shard_map/ppermute | solution.py:24
  24.6 8.0 %collective-permute-start.15 = (bf16[256,512]{1,0:T(8,128)(2,1)S(1)}, bf16[256,512]{1,0:T(8,128)(2,1)S(1)}, u32[]{:S(2)}, u32[]{:S(2)}) collective-permute-start(bf16[256,512]{1,0:T(8,128)(2,1)S(1)} %collective-permute-done.10.first_ref), channel_id=1, source_target_pairs={{0,2},{1,3},{2,0},{3,1},{4,6},{5,7},{6,4},{7,5},{8,10},{9,11},{10,... | collective-permute-start | bytes 786440 | tf_op jit(solution)/shard_map/ppermute | solution.py:24
  28.4 4.4 %collective-permute-start.18 = (bf16[256,512]{1,0:T(8,128)(2,1)S(1)}, bf16[256,512]{1,0:T(8,128)(2,1)S(1)}, u32[]{:S(2)}, u32[]{:S(2)}) collective-permute-start(bf16[256,512]{1,0:T(8,128)(2,1)S(1)} %collective-permute-done.11.first_ref), channel_id=1, source_target_pairs={{0,1},{1,0},{2,3},{3,2},{4,5},{5,4},{6,7},{7,6},{8,9},{9,8},{10,11... | collective-permute-start | bytes 786440 | tf_op jit(solution)/shard_map/ppermute | solution.py:24
  28.4 5.3 %collective-permute-start.17 = (bf16[256,512]{1,0:T(8,128)(2,1)S(1)}, bf16[256,512]{1,0:T(8,128)(2,1)S(1)}, u32[]{:S(2)}, u32[]{:S(2)}) collective-permute-start(bf16[256,512]{1,0:T(8,128)(2,1)S(1)} %collective-permute-done.10.first_ref), channel_id=1, source_target_pairs={{0,1},{1,0},{2,3},{3,2},{4,5},{5,4},{6,7},{7,6},{8,9},{9,8},{10,11... | collective-permute-start | bytes 786440 | tf_op jit(solution)/shard_map/ppermute | solution.py:24
  29.0 6.7 %collective-permute-start.12 = (bf16[64,512]{1,0:T(8,128)(2,1)S(1)}, bf16[64,512]{1,0:T(8,128)(2,1)S(1)}, u32[]{:S(2)}, u32[]{:S(2)}) collective-permute-start(bf16[64,512]{1,0:T(8,128)(2,1)S(1)} %choose_pieces.1), channel_id=1, source_target_pairs={{0,2},{1,3},{2,0},{3,1},{4,6},{5,7},{6,4},{7,5},{8,10},{9,11},{10,... | collective-permute-start | bytes 196616 | tf_op jit(solution)/shard_map/ppermute | solution.py:24
  30.6 5.2 %collective-permute-start.13 = (bf16[64,512]{1,0:T(8,128)(2,1)S(1)}, bf16[64,512]{1,0:T(8,128)(2,1)S(1)}, u32[]{:S(2)}, u32[]{:S(2)}) collective-permute-start(bf16[64,512]{1,0:T(8,128)(2,1)S(1)} %choose_pieces.1), channel_id=1, source_target_pairs={{0,4},{1,5},{2,6},{3,7},{4,0},{5,1},{6,2},{7,3},{8,12},{9,13},{10,... | collective-permute-start | bytes 196616 | tf_op jit(solution)/shard_map/ppermute | solution.py:24
  32.6 5.2 %collective-permute-start.14 = (bf16[64,512]{1,0:T(8,128)(2,1)S(1)}, bf16[64,512]{1,0:T(8,128)(2,1)S(1)}, u32[]{:S(2)}, u32[]{:S(2)}) collective-permute-start(bf16[64,512]{1,0:T(8,128)(2,1)S(1)} %choose_pieces.1), channel_id=1, source_target_pairs={{0,6},{1,7},{2,4},{3,5},{4,2},{5,3},{6,0},{7,1},{8,14},{9,15},{10,... | collective-permute-start | bytes 196616 | tf_op jit(solution)/shard_map/ppermute | solution.py:24
  32.8 2.0 %collective-permute-start.16 = (bf16[256,512]{1,0:T(8,128)(2,1)S(1)}, bf16[256,512]{1,0:T(8,128)(2,1)S(1)}, u32[]{:S(2)}, u32[]{:S(2)}) collective-permute-start(bf16[256,512]{1,0:T(8,128)(2,1)S(1)} %collective-permute-done.15.first_ref), channel_id=1, source_target_pairs={{0,1},{1,0},{2,3},{3,2},{4,5},{5,4},{6,7},{7,6},{8,9},{9,8},{10,11... | collective-permute-start | bytes 786440 | tf_op jit(solution)/shard_map/ppermute | solution.py:24
  34.7 4.7 %copy-start.1 = (bf16[512,1536]{1,0:T(8,128)(2,1)S(1)}, bf16[512,1536]{1,0:T(8,128)(2,1)}, u32[]{:S(2)}) copy-start(bf16[512,1536]{1,0:T(8,128)(2,1)} %w_qkv_ref.1) | copy-start | bytes 4718596
  34.7 4.7 %copy-start.2 = (s32[8,8,128,128]{3,2,1,0:T(8,128)S(1)}, s32[8,8,128,128]{3,2,1,0:T(8,128)}, u32[]{:S(2)}) copy-start(s32[8,8,128,128]{3,2,1,0:T(8,128)} %mask_ref.1) | copy-start | bytes 12582916
  34.7 4.6 %copy-start.3 = (bf16[512,1024]{1,0:T(8,128)(2,1)S(1)}, bf16[512,1024]{1,0:T(8,128)(2,1)}, u32[]{:S(2)}) copy-start(bf16[512,1024]{1,0:T(8,128)(2,1)} %w_up_ref.1) | copy-start | bytes 3145732
  34.7 4.6 %copy-start.4 = (bf16[1024,512]{1,0:T(8,128)(2,1)S(1)}, bf16[1024,512]{1,0:T(8,128)(2,1)}, u32[]{:S(2)}) copy-start(bf16[1024,512]{1,0:T(8,128)(2,1)} %w_down_ref.1) | copy-start | bytes 3145732
  34.8 4.6 %copy-start.5 = (bf16[512,512]{1,0:T(8,128)(2,1)S(1)}, bf16[512,512]{1,0:T(8,128)(2,1)}, u32[]{:S(2)}) copy-start(bf16[512,512]{1,0:T(8,128)(2,1)} %w_out_ref.1) | copy-start | bytes 1572868
  34.8 4.6 %copy-start.7 = (bf16[256,512]{1,0:T(8,128)(2,1)S(1)}, bf16[256,512]{1,0:T(8,128)(2,1)}, u32[]{:S(2)}) copy-start(bf16[256,512]{1,0:T(8,128)(2,1)} %tokens_ref.1) | copy-start | bytes 786436
  34.8 4.6 %copy-start.8 = (s32[8,8]{1,0:T(8,128)S(1)}, s32[8,8]{1,0:T(8,128)}, u32[]{:S(2)}) copy-start(s32[8,8]{1,0:T(8,128)} %cols_ref.1) | copy-start | bytes 772
  37.8 1.6 %collective-permute-start.19 = (bf16[256,512]{1,0:T(8,128)(2,1)S(1)}, bf16[256,512]{1,0:T(8,128)(2,1)S(1)}, u32[]{:S(2)}, u32[]{:S(2)}) collective-permute-start(bf16[256,512]{1,0:T(8,128)(2,1)S(1)} %constant_dynamic-update-slice_fusion.refs_0_), channel_id=1, source_target_pairs={{0,1},{1,0},{2,3},{3,2},{4,5},{5,4},{6,7},{7,6},{8,9},{9,8},{10,11... | collective-permute-start | bytes 786440 | tf_op jit(solution)/shard_map/ppermute | solution.py:24

commit v5 on v4

--- a/solution.py
+++ b/solution.py
@@ -118,17 +118,19 @@
 
 
 def pick_kernel(hub_count, local, code_ref, *refs):
-    *sources, piece_ref = refs
+    *sources, mine_ref, theirs_ref = refs
     here, head_here = place()
-    piece = here % 2 * 4 + head_here % 4
-    candidates = []
-    for k, ref in enumerate(sources):
-        for slot in range(local):
-            row = slot * TB + piece * PIECE if k < 6 else (slot * 2 + head_here % 2) * PIECE
-            candidates.append(ref[pl.ds(pl.multiple_of(row, PIECE), PIECE), :])
-    for j in range(hub_count):
-        rows = slice(j * PIECE, (j + 1) * PIECE)
-        piece_ref[rows, :] = chosen(code_ref, 0, rows, candidates)
+    lane = head_here % 2
+    for out_ref, core in ((mine_ref, lane), (theirs_ref, 1 - lane)):
+        piece = here % 2 * 4 + head_here % 4 - lane + core
+        candidates = []
+        for k, ref in enumerate(sources):
+            for slot in range(local):
+                row = slot * TB + piece * PIECE if k < 3 else (slot * 2 + core) * PIECE
+                candidates.append(ref[pl.ds(pl.multiple_of(row, PIECE), PIECE), :])
+        for j in range(hub_count):
+            rows = slice(j * PIECE, (j + 1) * PIECE)
+            out_ref[rows, :] = chosen(code_ref, 0, rows, candidates)
 
 
 def pick_pieces(codes, sources):
@@ -136,9 +138,9 @@
     rows = codes.shape[1]
     return pl.pallas_call(
         functools.partial(pick_kernel, rows // PIECE, node_dev // TB),
-        out_shape=jax.ShapeDtypeStruct((rows, width), jnp.bfloat16),
+        out_shape=[jax.ShapeDtypeStruct((rows, width), jnp.bfloat16)] * 2,
         in_specs=[VMEM] * (1 + len(sources)),
-        out_specs=VMEM,
+        out_specs=[VMEM] * 2,
         compiler_params=pltpu.CompilerParams(vmem_limit_bytes=4 << 20),
         name="pick_pieces",
     )(codes, *sources)
@@ -160,26 +162,48 @@
     )(codes, *sources)
 
 
+def hub_keyval_into(pool_ref, scratch, rows_ref, lane, w_ref, heads, head_dim, hub_count):
+    here, head_here = place()
+    mine = here % 2 * 4 + head_here % 4
+    keyval_into(scratch, slice(None), layer_norm(rows_ref[...].astype(jnp.float32)), w_ref, heads, head_dim)
+    hub_place = pool_ref.shape[0] - hub_count * TB
+    for k in range(PIECES // 2):
+        for j in range(hub_count):
+            row = (k * hub_count + j) * PIECE
+            at = hub_place + j * TB + (mine ^ (2 * k + lane)) * PIECE
+            pool_ref[pl.ds(pl.multiple_of(at, PIECE), PIECE), :] = scratch[row : row + PIECE, :]
+
+
+def hub_half_kernel(heads, head_dim, hub_count, rows_ref, w_ref, _, pool_ref, scratch):
+    hub_keyval_into(pool_ref, scratch, rows_ref, 0, w_ref, heads, head_dim, hub_count)
+
+
+def hub_half(pool, rows, w_qkv, heads, head_dim, hub_count):
+    return pl.pallas_call(
+        functools.partial(hub_half_kernel, heads, head_dim, hub_count),
+        out_shape=jax.ShapeDtypeStruct(pool.shape, pool.dtype),
+        in_specs=[VMEM] * 3,
+        out_specs=VMEM,
+        input_output_aliases={2: 0},
+        scratch_shapes=[pltpu.VMEM((rows.shape[0], pool.shape[1]), pool.dtype)],
+        compiler_params=pltpu.CompilerParams(vmem_limit_bytes=8 << 20),
+        name="hub_half",
+    )(rows, w_qkv, pool)
+
+
 def finish_kernel(
-    heads, head_dim, hub_count, hub_base, cols_ref,
-    tokens_ref, query_ref, mask_ref, w_qkv_ref, w_out_ref, w_up_ref, w_down_ref, *refs
+    heads, head_dim, hub_count, hub_base, plan_ref,
+    tokens_ref, query_ref, mask, w_qkv_ref, w_out_ref, w_up_ref, w_down_ref, *refs
 ):
-    around, (_, out_ref, pool_ref, hub_rows, mask, attn, sem) = refs[:2], refs[2:]
+    around_ref, _, out_ref, pool_ref, hub_keyvals, attn, cols_ref, sem = refs
     node_dev, width = tokens_ref.shape
     local = node_dev // TB
-    per_group, tiles = cols_ref.shape
+    per_group, tiles = plan_ref.shape
     here, head_here = place()
-    load = pltpu.make_async_copy(mask_ref.at[pl.ds(head_here * local, local)], mask, sem)
+    load = pltpu.make_async_copy(plan_ref, cols_ref, sem)
     load.start()
-    mine = here % 2 * 4 + head_here % 4
-    for k in range(PIECES):
-        for j in range(hub_count):
-            row = (k // 2 * hub_count + j) * PIECE
-            rows = pl.ds(pl.multiple_of(j * TB + (mine ^ k) * PIECE, PIECE), PIECE)
-            hub_rows[rows, :] = around[k % 2][row : row + PIECE, :]
-    hub_normed = layer_norm(hub_rows[...].astype(jnp.float32))
+    hub_keyval_into(pool_ref, hub_keyvals, around_ref, 1, w_qkv_ref, heads, head_dim, hub_count)
     hub_place = pool_ref.shape[0] // TB - hub_count
-    keyval_into(pool_ref, slice(hub_place * TB, None), hub_normed, w_qkv_ref, heads, head_dim)
     load.wait()
     group = max(head_dim, 128)
     for r in range(local):
@@ -233,21 +257,18 @@
     return pl.pallas_call(
         functools.partial(finish_kernel, heads, head_dim, hub_count, hub_base),
         out_shape=[jax.ShapeDtypeStruct(tokens.shape, bf16), jax.ShapeDtypeStruct(pool.shape, bf16)],
-        in_specs=[pl.BlockSpec(memory_space=pltpu.SMEM)]
-        + [VMEM] * 2
-        + [pl.BlockSpec(memory_space=pltpu.HBM)]
-        + [VMEM] * 7,
+        in_specs=[ANY] + [VMEM] * 9,
         out_specs=[VMEM, VMEM],
-        input_output_aliases={10: 1},
+        input_output_aliases={9: 1},
         scratch_shapes=[
-            pltpu.VMEM((hub_count * TB, width), bf16),
-            pltpu.VMEM((node_dev // TB,) + mask.shape[1:], jnp.int32),
+            pltpu.VMEM((around.shape[0], 2 * width), bf16),
             pltpu.VMEM((node_dev, width), bf16),
+            pltpu.SMEM(cols.shape, jnp.int32),
             pltpu.SemaphoreType.DMA,
         ],
         compiler_params=pltpu.CompilerParams(vmem_limit_bytes=20 << 20),
         name="finish",
-    )(cols, tokens, query, mask, w_qkv, w_out, w_up, w_down, *around, pool)[0]
+    )(cols, tokens, query, mask, w_qkv, w_out, w_up, w_down, around, pool)[0]
 
 
 def body(tokens, w_qkv, w_out, w_up, w_down, tile_cols, tile_mask, hub_blocks):
@@ -304,8 +325,11 @@
 
     def picked_from(block, here, head_here):
         n, h = owner(block)
-        offset = (n + here) % 2 * 4 + ((h % 4) ^ (head_here % 4))
+        offset = (n + here) % 2 * 2 + (h // 2 + head_here // 2) % 2
         return offset * local + block % local
+
+    def lane_from(block, here, head_here):
+        return (owner(block)[1] + head_here) % 2
 
     def ring_from(block, here, head_here):
         ahead = area_of(here, head_here) + 4 - area_of(*owner(block))
@@ -314,7 +338,7 @@
     def area_from(step):
         return lambda block, here, head_here: (area_of(*owner(block)) ^ area_of(here, head_here)) // step % 4
 
-    whence = (picked_from, ring_from) if ring else (picked_from, *map(area_from, steps))
+    whence = (picked_from, lane_from, *([ring_from] if ring else map(area_from, steps)))
 
     other = range(2, heads, 2)
     sides = [side(tokens, o) for o in other]
@@ -325,45 +349,48 @@
     strip = across(strip.reshape(local * 2 * PIECE, width))
     token_core = core(tokens)
     pool, query, again, codes = keyval(None, 0, tokens, token_core, hub_blocks=hub_blocks, whence=whence)
-    paired, strip, pool, query, codes, *sides = lax.optimization_barrier((paired, strip, pool, query, codes, *sides))
-
     far = along(paired)
-
-    paired_core, strip_core = core(paired), core(strip)
+    edges = lax.dynamic_slice_in_dim(tile_mask, head_here * local, local, 0)
+    paired, strip, pool, query, codes, edges, *sides = lax.optimization_barrier(
+        (paired, strip, pool, query, codes, edges, *sides)
+    )
+
+
+    mine, theirs = pick_pieces(codes, [again, sides[0], paired, strip])
+    paired_core = core(paired)
     sides_core = [core(v) for v in sides]
-    paired_sides = [side(paired, o) for o in other]
-    sources = [again, token_core, sides[0], sides_core[0], paired, paired_core, strip, strip_core]
-    piece = pick_pieces(codes, sources)
-
-    for k, (value, other_value) in enumerate(zip(sides, sides_core)):
-        pool = keyval(pool, 2 + 2 * k, value, other_value, after=(piece,))
+    theirs = later(core(theirs), paired_core, *sides_core)
+    piece = choose_pieces(codes, 1, [mine, theirs])
+    paired_sides = [pair(later(v, theirs)) for v in sides]
+
+    pool = keyval(pool, heads, paired, paired_core, after=(piece,))
     far, pool = lax.optimization_barrier((far, pool))
     far_sides = [side(far, o) for o in other]
-    far_core = core(far)
-    pool = keyval(pool, heads, paired, paired_core)
+    for k, (value, other_value) in enumerate(zip(sides, sides_core)):
+        pool = keyval(pool, 2 + 2 * k, value, other_value, after=(far,))
+    paired_core2 = [core(later(v, far)) for v in paired_sides]
 
     if ring:
         got = [piece, along(piece), along(piece, 2), along(piece, -1)]
         got, pool, paired_sides = lax.optimization_barrier((got, pool, paired_sides))
-        piece = choose_pieces(codes, 1, got)
+        piece = choose_pieces(codes, 2, got)
     else:
         for i, step in enumerate(steps):
             got = [go(piece, where=lambda n, h, s=s: to_area(n, h, s)) for s in reach(step)]
-            piece = choose_pieces(codes, 1 + i, [piece, *got])
+            piece = choose_pieces(codes, 2 + i, [piece, *got])
 
     around = [piece, side(piece), pair(piece), across(piece)]
-    paired_sides_core = [core(v) for v in paired_sides]
-    far_sides_core = [core(v) for v in far_sides]
-    for k, (value, other_value) in enumerate(zip(paired_sides, paired_sides_core)):
+    for k, (value, other_value) in enumerate(zip(paired_sides, paired_core2)):
         pool = keyval(pool, heads + 2 + 2 * k, value, other_value)
-    for k, (value, other_value) in enumerate(zip([far, *far_sides], [far_core, *far_sides_core])):
-        pool = keyval(pool, 2 * heads + 2 * k, value, other_value)
+    for k, value in enumerate([far, *far_sides]):
+        pool = keyval(pool, 2 * heads + 2 * k, value, core(later(value, piece)))
     around, pool = lax.optimization_barrier((around, pool))
 
     around = jnp.concatenate(around, axis=0)
-    around = [around, core(around)]
+    pool = hub_half(pool, around, weights, heads, head_dim, hub_count)
+    around = core(around)
     return finish(
-        tile_cols, tokens, query, tile_mask, weights, w_out, w_up, w_down, around, pool, heads, head_dim, hub_count, per_group * nodes
+        tile_cols, again, query, edges, weights, w_out, w_up, w_down, around, pool, heads, head_dim, hub_count, per_group * nodes
     )
 
 

time: 45.4 us -> 43.3 us (0.954)
  waiting for transfers between devices: 10.2 us -> 7.74 us
  local copies, waits for them, and re-layouts: 3.96 us -> 5.37 us
  starting transfers between devices: 18.6 us -> 17.9 us
  Pallas kernels: 12.2 us -> 11.7 us
    ppermute x20, waiting for transfers between devices: 10.2 us -> 7.74 us  [send(): return lax.ppermute(value, AXES, pairs)]
    dynamic_slice x0 -> x1, local copies, waits for them, and re-layouts: none -> 1.32 us  [body(): edges = lax.dynamic_slice_in_dim(tile_mask, head_here * local, local, 0)]
    pallas_call x1, Pallas kernels: 5.72 us -> 4.58 us  [finish(): pl.pallas_call(functools.partial(finish_kernel, heads, head_dim, hub_coun...]
    ppermute x20, starting transfers between devices: 18.6 us -> 17.9 us  [send(): return lax.ppermute(value, AXES, pairs)]
    pallas_call x0 -> x1, Pallas kernels: none -> 0.65 us  [hub_half(): pl.pallas_call(functools.partial(hub_half_kernel, heads, head_dim, hub_co...]
    unnamed x23 -> x19, local copies, waits for them, and re-layouts: 3.07 us -> 3.17 us
  transfers between devices with their start and end apart: 20 -> 20, of which waited for: 7 -> 7; matrix products, arithmetic and copies ran while one was open for 2% -> 5% of each run, Pallas kernels for 14% -> 17%
where the time goes in v5:
time: 43.3 us; the launch traced here: 43 us
  starting transfers between devices  17.9 us (41%)
  Pallas kernels  11.7 us (27%)
  waiting for transfers between devices  7.74 us (18%)
  local copies, waits for them, and re-layouts  5.37 us (12%)
    ppermute x20, starting transfers between devices, send(): return lax.ppermute(value, AXES, pairs)  17.9 us
    ppermute x20, waiting for transfers between devices, send(): return lax.ppermute(value, AXES, pairs)  7.74 us
    pallas_call x6, Pallas kernels, keyvals(): pl.pallas_call(functools.partial(keyval_kernel, heads, head_dim, at, when...  6.32 us
    pallas_call x1, Pallas kernels, finish(): pl.pallas_call(functools.partial(finish_kernel, heads, head_dim, hub_coun...  4.58 us
    unnamed x19, local copies, waits for them, and re-layouts  3.17 us
    dynamic_slice x1, local copies, waits for them, and re-layouts, body(): edges = lax.dynamic_slice_in_dim(tile_mask, head_here * local, local, 0)  1.32 us
    dynamic_slice x1, local copies, waits for them, and re-layouts, body(): lax.dynamic_slice_in_dim(tokens.reshape(local, TB, width), strip_at, 2 *...  0.88 us
  transfers between devices with their start and end apart: 20, of which 7 were waited for; matrix products, arithmetic and copies ran while one was open for 5% of the time, Pallas kernels for 17%

profile of v5, /device:TPU:0, one launch (start us, length us, event | category | flops | bytes accessed | tf_op | source)
XLA Modules:
  0.0 43.0 jit_solution(3793247311680135424)
XLA Ops:
  0.0 0.5 %collective-permute-start = (bf16[256,512]{1,0:T(8,128)(2,1)}, bf16[256,512]{1,0:T(8,128)(2,1)S(1)}, u32[]{:S(2)}, u32[]{:S(2)}) collective-permute-start(bf16[256,512]{1,0:T(8,128)(2,1)} %first_ref.1), channel_id=1, source_target_pairs={{0,1},{1,0},{2,3},{3,2},{4,5},{5,4},{6,7},{7,6},{8,9},{9,8},{10,11... | collective-permute-start | bytes 786440 | tf_op jit(solution)/shard_map/ppermute | solution.py:24
  0.5 2.5 %collective-permute-start.1 = (bf16[256,512]{1,0:T(8,128)(2,1)}, bf16[256,512]{1,0:T(8,128)(2,1)S(1)}, u32[]{:S(2)}, u32[]{:S(2)}) collective-permute-start(bf16[256,512]{1,0:T(8,128)(2,1)} %first_ref.1), channel_id=1, source_target_pairs={{0,4},{1,5},{2,6},{3,7},{4,0},{5,1},{6,2},{7,3},{8,12},{9,13},{10,... | collective-permute-start | bytes 786440 | tf_op jit(solution)/shard_map/ppermute | solution.py:24
  2.9 1.5 %collective-permute-start.3 = (bf16[256,512]{1,0:T(8,128)(2,1)}, bf16[256,512]{1,0:T(8,128)(2,1)S(1)}, u32[]{:S(2)}, u32[]{:S(2)}) collective-permute-start(bf16[256,512]{1,0:T(8,128)(2,1)} %first_ref.1), channel_id=1, source_target_pairs={{0,2},{1,3},{2,0},{3,1},{4,6},{5,7},{6,4},{7,5},{8,10},{9,11},{10,... | collective-permute-start | bytes 786440 | tf_op jit(solution)/shard_map/ppermute | solution.py:24
  4.5 0.9 %constant_dynamic-slice_fusion.1 = bf16[2,32,512]{2,1,0:T(8,128)(2,1)S(1)} fusion(bf16[2,128,512]{2,1,0:T(8,128)(2,1)} %bitcast.2, s32[]{:T(128)S(6)} %select_n.24), kind=kLoop, calls=%fused_computation.5 | loop fusion | bytes 131076 | tf_op jit(solution)/shard_map/dynamic_slice | solution.py:348
  5.3 0.0 collective-permute-start.2
  5.4 1.3 %constant_dynamic-slice_fusion.mask = s32[2,8,128,128]{3,2,1,0:T(8,128)S(1)} fusion(s32[8,8,128,128]{3,2,1,0:T(8,128)} %param.14, s32[]{:T(128)S(6)} %select_n.25), kind=kLoop, calls=%fused_computation.4 | loop fusion | bytes 2097156 | tf_op jit(solution)/shard_map/dynamic_slice | solution.py:353
  6.7 0.0 collective-permute-done.second_ref
  6.7 0.0 copy-start
  6.7 1.4 %copy-done = bf16[512,1536]{1,0:T(8,128)(2,1)S(1)} copy-done((bf16[512,1536]{1,0:T(8,128)(2,1)S(1)}, bf16[512,1536]{1,0:T(8,128)(2,1)}, u32[]{:S(2)}) %copy-start) | copy-done | bytes 1572888
  8.1 0.9 %copy-done.5 = bf16[256,512]{1,0:T(8,128)(2,1)S(1)} copy-done((bf16[256,512]{1,0:T(8,128)(2,1)S(1)}, bf16[256,512]{1,0:T(8,128)(2,1)}, u32[]{:S(2)}) %copy-start.5) | copy-done | bytes 262168
  9.1 0.7 %copy-done.7 = s32[4]{0:T(128)S(1)} copy-done((s32[4]{0:T(128)S(1)}, s32[4]{0:T(128)}, u32[]{:S(2)}) %copy-start.7) | copy-done | bytes 40
  9.7 1.7 %keyvals.6 = (bf16[3584,1024]{1,0:T(8,128)(2,1)S(1)}, bf16[256,512]{1,0:T(8,128)(2,1)S(1)}, bf16[256,512]{1,0:T(8,128)(2,1)S(1)}, f32[3,64,128]{2,1,0:T(8,128)S(1)}) custom-call(bf16[256,512]{1,0:T(8,128)(2,1)S(1)} %copy-done.5, bf16[256,512]{1,0:T(8,128)(2,1)S(1)} %collective-permute-done.second_ref, bf16[512,1536]{1,0:T(8,128)(2,1)S(1)} %copy-done, ...), custom_call_target="tpu_custom_call" | custom-call | flops 4294967296 | bytes 1572864 | tf_op jit(solution)/shard_map/keyvals/pallas_call | solution.py:88
  11.5 1.4 %collective-permute-done.2.refs_3_ = bf16[64,512]{1,0:T(8,128)(2,1)S(1)} collective-permute-done((bf16[64,512]{1,0:T(8,128)(2,1)S(1)}, bf16[64,512]{1,0:T(8,128)(2,1)S(1)}, u32[]{:S(2)}, u32[]{:S(2)}) %collective-permute-start.2) | collective-permute-done | bytes 65568 | tf_op jit(solution)/shard_map/ppermute | solution.py:24
  12.8 0.0 collective-permute-done.1.refs_2_.first_ref
  12.9 0.1 collective-permute-done.3.refs_1_.first_ref
  13.0 0.5 %collective-permute-start.6 = (bf16[256,512]{1,0:T(8,128)(2,1)S(1)}, bf16[256,512]{1,0:T(8,128)(2,1)S(1)}, u32[]{:S(2)}, u32[]{:S(2)}) collective-permute-start(bf16[256,512]{1,0:T(8,128)(2,1)S(1)} %collective-permute-done.3.refs_1_.first_ref), channel_id=1, source_target_pairs={{0,1},{1,0},{2,3},{3,2},{4,5},{5,4},{6,7},{7,6},{8,9},{9,8},{10,11... | collective-permute-start | bytes 786440 | tf_op jit(solution)/shard_map/ppermute | solution.py:24
  13.5 0.1 pick_pieces.1
  13.6 0.1 collective-permute-start.4
  13.7 1.6 %collective-permute-start.10 = (bf16[256,512]{1,0:T(8,128)(2,1)S(1)}, bf16[256,512]{1,0:T(8,128)(2,1)S(1)}, u32[]{:S(2)}, u32[]{:S(2)}) collective-permute-start(bf16[256,512]{1,0:T(8,128)(2,1)S(1)} %collective-permute-done.1.refs_2_.first_ref), channel_id=1, source_target_pairs={{0,8},{1,9},{2,10},{3,11},{4,28},{5,29},{6,30},{7,31},{8,16},{9,17... | collective-permute-start | bytes 786440 | tf_op jit(solution)/shard_map/ppermute | solution.py:24
  15.4 1.6 %collective-permute-start.7 = (bf16[64,512]{1,0:T(8,128)(2,1)S(1)}, bf16[64,512]{1,0:T(8,128)(2,1)S(1)}, u32[]{:S(2)}, u32[]{:S(2)}) collective-permute-start(bf16[64,512]{1,0:T(8,128)(2,1)S(1)} %choose_pieces.2.refs_0_), channel_id=1, source_target_pairs={{0,8},{1,9},{2,10},{3,11},{4,28},{5,29},{6,30},{7,31},{8,16},{9,17... | collective-permute-start | bytes 196616 | tf_op jit(solution)/shard_map/ppermute | solution.py:24
  17.0 2.2 %collective-permute-start.8 = (bf16[64,512]{1,0:T(8,128)(2,1)S(1)}, bf16[64,512]{1,0:T(8,128)(2,1)S(1)}, u32[]{:S(2)}, u32[]{:S(2)}) collective-permute-start(bf16[64,512]{1,0:T(8,128)(2,1)S(1)} %choose_pieces.2.refs_0_), channel_id=1, source_target_pairs={{0,16},{1,17},{2,18},{3,19},{4,20},{5,21},{6,22},{7,23},{8,24},{9,... | collective-permute-start | bytes 196616 | tf_op jit(solution)/shard_map/ppermute | solution.py:24
  19.3 1.7 %collective-permute-start.9 = (bf16[64,512]{1,0:T(8,128)(2,1)S(1)}, bf16[64,512]{1,0:T(8,128)(2,1)S(1)}, u32[]{:S(2)}, u32[]{:S(2)}) collective-permute-start(bf16[64,512]{1,0:T(8,128)(2,1)S(1)} %choose_pieces.2.refs_0_), channel_id=1, source_target_pairs={{0,24},{1,25},{2,26},{3,27},{4,12},{5,13},{6,14},{7,15},{8,0},{9,1... | collective-permute-start | bytes 196616 | tf_op jit(solution)/shard_map/ppermute | solution.py:24
  20.9 0.0 collective-permute-start.11
  20.9 0.9 %keyvals.7.refs_1_ = bf16[3584,1024]{1,0:T(8,128)(2,1)S(1)} custom-call(bf16[256,512]{1,0:T(8,128)(2,1)S(1)} %collective-permute-done.1.refs_2_.first_ref, bf16[256,512]{1,0:T(8,128)(2,1)S(1)} %collective-permute-done.5.second_ref, bf16[512,1536]{1,0:T(8,128)(2,1)S(1)} %copy-done, ...), custom_call_target="tpu_custom_call", output_to_operand_aliasing={{}: (4, {})} | custom-call | flops 4294967296 | bytes 1572864 | tf_op jit(solution)/shard_map/keyvals/pallas_call | solution.py:88
  21.9 3.0 %collective-permute-done.10.refs_0_.first_ref = bf16[256,512]{1,0:T(8,128)(2,1)S(1)} collective-permute-done((bf16[256,512]{1,0:T(8,128)(2,1)S(1)}, bf16[256,512]{1,0:T(8,128)(2,1)S(1)}, u32[]{:S(2)}, u32[]{:S(2)}) %collective-permute-start.10) | collective-permute-done | bytes 262176 | tf_op jit(solution)/shard_map/ppermute | solution.py:24
  24.9 1.5 %collective-permute-start.15 = (bf16[256,512]{1,0:T(8,128)(2,1)S(1)}, bf16[256,512]{1,0:T(8,128)(2,1)S(1)}, u32[]{:S(2)}, u32[]{:S(2)}) collective-permute-start(bf16[256,512]{1,0:T(8,128)(2,1)S(1)} %collective-permute-done.10.refs_0_.first_ref), channel_id=1, source_target_pairs={{0,2},{1,3},{2,0},{3,1},{4,6},{5,7},{6,4},{7,5},{8,10},{9,11},{10,... | collective-permute-start | bytes 786440 | tf_op jit(solution)/shard_map/ppermute | solution.py:24
  26.4 2.1 %collective-permute-done.11.first_ref = bf16[256,512]{1,0:T(8,128)(2,1)S(1)} collective-permute-done((bf16[256,512]{1,0:T(8,128)(2,1)S(1)}, bf16[256,512]{1,0:T(8,128)(2,1)S(1)}, u32[]{:S(2)}, u32[]{:S(2)}) %collective-permute-start.11) | collective-permute-done | bytes 262176 | tf_op jit(solution)/shard_map/ppermute | solution.py:24
  28.5 0.9 %keyvals.8.refs_0_ = bf16[3584,1024]{1,0:T(8,128)(2,1)S(1)} custom-call(bf16[256,512]{1,0:T(8,128)(2,1)S(1)} %collective-permute-done.3.refs_1_.first_ref, bf16[256,512]{1,0:T(8,128)(2,1)S(1)} %collective-permute-done.6.second_ref, bf16[512,1536]{1,0:T(8,128)(2,1)S(1)} %copy-done, ...), custom_call_target="tpu_custom_call", output_to_operand_aliasing={{}: (4, {})} | custom-call | flops 4294967296 | bytes 1572864 | tf_op jit(solution)/shard_map/keyvals/pallas_call | solution.py:88
  29.5 1.6 %collective-permute-start.12 = (bf16[64,512]{1,0:T(8,128)(2,1)S(1)}, bf16[64,512]{1,0:T(8,128)(2,1)S(1)}, u32[]{:S(2)}, u32[]{:S(2)}) collective-permute-start(bf16[64,512]{1,0:T(8,128)(2,1)S(1)} %choose_pieces.3), channel_id=1, source_target_pairs={{0,2},{1,3},{2,0},{3,1},{4,6},{5,7},{6,4},{7,5},{8,10},{9,11},{10,... | collective-permute-start | bytes 196616 | tf_op jit(solution)/shard_map/ppermute | solution.py:24
  31.1 0.3 collective-permute-start.13
  31.3 1.7 %collective-permute-start.14 = (bf16[64,512]{1,0:T(8,128)(2,1)S(1)}, bf16[64,512]{1,0:T(8,128)(2,1)S(1)}, u32[]{:S(2)}, u32[]{:S(2)}) collective-permute-start(bf16[64,512]{1,0:T(8,128)(2,1)S(1)} %choose_pieces.3), channel_id=1, source_target_pairs={{0,6},{1,7},{2,4},{3,5},{4,2},{5,3},{6,0},{7,1},{8,14},{9,15},{10,... | collective-permute-start | bytes 196616 | tf_op jit(solution)/shard_map/ppermute | solution.py:24
  33.0 0.5 %collective-permute-start.16 = (bf16[256,512]{1,0:T(8,128)(2,1)S(1)}, bf16[256,512]{1,0:T(8,128)(2,1)S(1)}, u32[]{:S(2)}, u32[]{:S(2)}) collective-permute-start(bf16[256,512]{1,0:T(8,128)(2,1)S(1)} %collective-permute-done.15.first_ref), channel_id=1, source_target_pairs={{0,1},{1,0},{2,3},{3,2},{4,5},{5,4},{6,7},{7,6},{8,9},{9,8},{10,11... | collective-permute-start | bytes 786440 | tf_op jit(solution)/shard_map/ppermute | solution.py:24
  33.6 0.9 %keyvals.9.refs_0_ = bf16[3584,1024]{1,0:T(8,128)(2,1)S(1)} custom-call(bf16[256,512]{1,0:T(8,128)(2,1)S(1)} %collective-permute-done.11.first_ref, bf16[256,512]{1,0:T(8,128)(2,1)S(1)} %collective-permute-done.18.second_ref, bf16[512,1536]{1,0:T(8,128)(2,1)S(1)} %copy-done, bf16[3584,1024]{1,0:T(8,128)(2,1)S(1)} %keyvals.8.refs_0_), custom_call_target="tpu_custom_call", output_to_operand_aliasing={{}: (3, {})} | custom-call | flops 4294967296 | bytes 1572864 | tf_op jit(solution)/shard_map/keyvals/pallas_call | solution.py:88
  34.5 0.1 collective-permute-done.17.second_ref
  34.6 0.9 %keyvals.10.refs_0_ = bf16[3584,1024]{1,0:T(8,128)(2,1)S(1)} custom-call(bf16[256,512]{1,0:T(8,128)(2,1)S(1)} %collective-permute-done.10.refs_0_.first_ref, bf16[256,512]{1,0:T(8,128)(2,1)S(1)} %collective-permute-done.17.second_ref, bf16[512,1536]{1,0:T(8,128)(2,1)S(1)} %copy-done, ...), custom_call_target="tpu_custom_call", output_to_operand_aliasing={{}: (3, {})} | custom-call | flops 4294967296 | bytes 1572864 | tf_op jit(solution)/shard_map/keyvals/pallas_call | solution.py:88
  35.5 0.0 copy-start.1
  35.5 0.9 %keyvals.11._ = bf16[3584,1024]{1,0:T(8,128)(2,1)S(1)} custom-call(bf16[256,512]{1,0:T(8,128)(2,1)S(1)} %collective-permute-done.15.first_ref, bf16[256,512]{1,0:T(8,128)(2,1)S(1)} %collective-permute-done.16.second_ref, bf16[512,1536]{1,0:T(8,128)(2,1)S(1)} %copy-done, bf16[3584,1024]{1,0:T(8,128)(2,1)S(1)} %keyvals.10.refs_0_), custom_call_target="tpu_custom_call", output_to_operand_aliasing={{}: (3, {})} | custom-call | flops 4294967296 | bytes 1572864 | tf_op jit(solution)/shard_map/keyvals/pallas_call | solution.py:88
  36.5 0.2 collective-permute-done.14
  36.7 0.0 copy-start.2
  36.7 0.0 copy-start.3
  36.7 0.0 copy-start.4
  36.8 0.0 copy-start.6
  36.8 0.1 collective-permute-start.19
  36.8 0.1 copy-done.1
  36.9 0.7 %hub_half.1.refs_1_ = bf16[3584,1024]{1,0:T(8,128)(2,1)S(1)} custom-call(bf16[256,512]{1,0:T(8,128)(2,1)S(1)} %constant_dynamic-update-slice_fusion.rows_ref, bf16[512,1536]{1,0:T(8,128)(2,1)S(1)} %copy-done.1, bf16[3584,1024]{1,0:T(8,128)(2,1)S(1)} %keyvals.11._), custom_call_target="tpu_custom_call", output_to_operand_aliasing={{}: (2, {})} | custom-call | tf_op jit(solution)/shard_map/hub_half/pallas_call | solution.py:182
  37.6 0.8 %collective-permute-done.19.refs_0_ = bf16[256,512]{1,0:T(8,128)(2,1)S(1)} collective-permute-done((bf16[256,512]{1,0:T(8,128)(2,1)S(1)}, bf16[256,512]{1,0:T(8,128)(2,1)S(1)}, u32[]{:S(2)}, u32[]{:S(2)}) %collective-permute-start.19) | collective-permute-done | bytes 262176 | tf_op jit(solution)/shard_map/ppermute | solution.py:24
  38.4 0.1 copy-done.4
  38.4 4.6 %finish.1 = (bf16[256,512]{1,0:T(8,128)(2,1)}, bf16[3584,1024]{1,0:T(8,128)(2,1)S(1)}) custom-call(s32[8,8]{1,0:T(8,128)S(1)} %copy-done.6, bf16[256,512]{1,0:T(8,128)(2,1)S(1)} %get-tuple-element.37.refs_0_.tokens_ref, bf16[256,512]{1,0:T(8,128)(2,1)S(1)} %get-tuple-element.41.query_ref, ...), custom_call_target="tpu_custom_call", output_to_operand_aliasing={{1}: (9, {})} | custom-call | tf_op jit(solution)/shard_map/finish/pallas_call | solution.py:257
  (25 shorter events, 0.1 us)
Async XLA Ops:
  0.0 6.7 %collective-permute-start = (bf16[256,512]{1,0:T(8,128)(2,1)}, bf16[256,512]{1,0:T(8,128)(2,1)S(1)}, u32[]{:S(2)}, u32[]{:S(2)}) collective-permute-start(bf16[256,512]{1,0:T(8,128)(2,1)} %first_ref.1), channel_id=1, source_target_pairs={{0,1},{1,0},{2,3},{3,2},{4,5},{5,4},{6,7},{7,6},{8,9},{9,8},{10,11... | collective-permute-start | bytes 786440 | tf_op jit(solution)/shard_map/ppermute | solution.py:24
  0.5 12.4 %collective-permute-start.1 = (bf16[256,512]{1,0:T(8,128)(2,1)}, bf16[256,512]{1,0:T(8,128)(2,1)S(1)}, u32[]{:S(2)}, u32[]{:S(2)}) collective-permute-start(bf16[256,512]{1,0:T(8,128)(2,1)} %first_ref.1), channel_id=1, source_target_pairs={{0,4},{1,5},{2,6},{3,7},{4,0},{5,1},{6,2},{7,3},{8,12},{9,13},{10,... | collective-permute-start | bytes 786440 | tf_op jit(solution)/shard_map/ppermute | solution.py:24
  2.9 10.1 %collective-permute-start.3 = (bf16[256,512]{1,0:T(8,128)(2,1)}, bf16[256,512]{1,0:T(8,128)(2,1)S(1)}, u32[]{:S(2)}, u32[]{:S(2)}) collective-permute-start(bf16[256,512]{1,0:T(8,128)(2,1)} %first_ref.1), channel_id=1, source_target_pairs={{0,2},{1,3},{2,0},{3,1},{4,6},{5,7},{6,4},{7,5},{8,10},{9,11},{10,... | collective-permute-start | bytes 786440 | tf_op jit(solution)/shard_map/ppermute | solution.py:24
  5.3 7.5 %collective-permute-start.2 = (bf16[64,512]{1,0:T(8,128)(2,1)S(1)}, bf16[64,512]{1,0:T(8,128)(2,1)S(1)}, u32[]{:S(2)}, u32[]{:S(2)}) collective-permute-start(bf16[64,512]{1,0:T(8,128)(2,1)S(1)} %bitcast.3), channel_id=1, source_target_pairs={{0,6},{1,7},{2,4},{3,5},{4,2},{5,3},{6,0},{7,1},{8,14},{9,15},{10,... | collective-permute-start | bytes 196616 | tf_op jit(solution)/shard_map/ppermute | solution.py:24
  6.7 1.4 %copy-start = (bf16[512,1536]{1,0:T(8,128)(2,1)S(1)}, bf16[512,1536]{1,0:T(8,128)(2,1)}, u32[]{:S(2)}) copy-start(bf16[512,1536]{1,0:T(8,128)(2,1)} %w_qkv_ref.1) | copy-start | bytes 4718596
  8.1 0.9 %copy-start.5 = (bf16[256,512]{1,0:T(8,128)(2,1)S(1)}, bf16[256,512]{1,0:T(8,128)(2,1)}, u32[]{:S(2)}) copy-start(bf16[256,512]{1,0:T(8,128)(2,1)} %first_ref.1) | copy-start | bytes 786436
  9.1 0.7 %copy-start.7 = (s32[4]{0:T(128)S(1)}, s32[4]{0:T(128)}, u32[]{:S(2)}) copy-start(s32[4]{0:T(128)} %refs_0_.1) | copy-start | bytes 52
  13.0 2.3 %collective-permute-start.5 = (bf16[256,512]{1,0:T(8,128)(2,1)S(1)}, bf16[256,512]{1,0:T(8,128)(2,1)S(1)}, u32[]{:S(2)}, u32[]{:S(2)}) collective-permute-start(bf16[256,512]{1,0:T(8,128)(2,1)S(1)} %collective-permute-done.1.refs_2_.first_ref), channel_id=1, source_target_pairs={{0,1},{1,0},{2,3},{3,2},{4,5},{5,4},{6,7},{7,6},{8,9},{9,8},{10,11... | collective-permute-start | bytes 786440 | tf_op jit(solution)/shard_map/ppermute | solution.py:24
  13.0 2.3 %collective-permute-start.6 = (bf16[256,512]{1,0:T(8,128)(2,1)S(1)}, bf16[256,512]{1,0:T(8,128)(2,1)S(1)}, u32[]{:S(2)}, u32[]{:S(2)}) collective-permute-start(bf16[256,512]{1,0:T(8,128)(2,1)S(1)} %collective-permute-done.3.refs_1_.first_ref), channel_id=1, source_target_pairs={{0,1},{1,0},{2,3},{3,2},{4,5},{5,4},{6,7},{7,6},{8,9},{9,8},{10,11... | collective-permute-start | bytes 786440 | tf_op jit(solution)/shard_map/ppermute | solution.py:24
  13.6 1.7 %collective-permute-start.4 = (bf16[64,512]{1,0:T(8,128)(2,1)S(1)}, bf16[64,512]{1,0:T(8,128)(2,1)S(1)}, u32[]{:S(2)}, u32[]{:S(2)}) collective-permute-start(bf16[64,512]{1,0:T(8,128)(2,1)S(1)} %get-tuple-element.48), channel_id=1, source_target_pairs={{0,1},{1,0},{2,3},{3,2},{4,5},{5,4},{6,7},{7,6},{8,9},{9,8},{10,11... | collective-permute-start | bytes 196616 | tf_op jit(solution)/shard_map/ppermute | solution.py:24
  13.7 11.1 %collective-permute-start.10 = (bf16[256,512]{1,0:T(8,128)(2,1)S(1)}, bf16[256,512]{1,0:T(8,128)(2,1)S(1)}, u32[]{:S(2)}, u32[]{:S(2)}) collective-permute-start(bf16[256,512]{1,0:T(8,128)(2,1)S(1)} %collective-permute-done.1.refs_2_.first_ref), channel_id=1, source_target_pairs={{0,8},{1,9},{2,10},{3,11},{4,28},{5,29},{6,30},{7,31},{8,16},{9,17... | collective-permute-start | bytes 786440 | tf_op jit(solution)/shard_map/ppermute | solution.py:24
  15.4 14.0 %collective-permute-start.7 = (bf16[64,512]{1,0:T(8,128)(2,1)S(1)}, bf16[64,512]{1,0:T(8,128)(2,1)S(1)}, u32[]{:S(2)}, u32[]{:S(2)}) collective-permute-start(bf16[64,512]{1,0:T(8,128)(2,1)S(1)} %choose_pieces.2.refs_0_), channel_id=1, source_target_pairs={{0,8},{1,9},{2,10},{3,11},{4,28},{5,29},{6,30},{7,31},{8,16},{9,17... | collective-permute-start | bytes 196616 | tf_op jit(solution)/shard_map/ppermute | solution.py:24
  17.0 12.4 %collective-permute-start.8 = (bf16[64,512]{1,0:T(8,128)(2,1)S(1)}, bf16[64,512]{1,0:T(8,128)(2,1)S(1)}, u32[]{:S(2)}, u32[]{:S(2)}) collective-permute-start(bf16[64,512]{1,0:T(8,128)(2,1)S(1)} %choose_pieces.2.refs_0_), channel_id=1, source_target_pairs={{0,16},{1,17},{2,18},{3,19},{4,20},{5,21},{6,22},{7,23},{8,24},{9,... | collective-permute-start | bytes 196616 | tf_op jit(solution)/shard_map/ppermute | solution.py:24
  19.3 10.2 %collective-permute-start.9 = (bf16[64,512]{1,0:T(8,128)(2,1)S(1)}, bf16[64,512]{1,0:T(8,128)(2,1)S(1)}, u32[]{:S(2)}, u32[]{:S(2)}) collective-permute-start(bf16[64,512]{1,0:T(8,128)(2,1)S(1)} %choose_pieces.2.refs_0_), channel_id=1, source_target_pairs={{0,24},{1,25},{2,26},{3,27},{4,12},{5,13},{6,14},{7,15},{8,0},{9,1... | collective-permute-start | bytes 196616 | tf_op jit(solution)/shard_map/ppermute | solution.py:24
  20.9 7.5 %collective-permute-start.11 = (bf16[256,512]{1,0:T(8,128)(2,1)S(1)}, bf16[256,512]{1,0:T(8,128)(2,1)S(1)}, u32[]{:S(2)}, u32[]{:S(2)}) collective-permute-start(bf16[256,512]{1,0:T(8,128)(2,1)S(1)} %collective-permute-done.3.refs_1_.first_ref), channel_id=1, source_target_pairs={{0,4},{1,5},{2,6},{3,7},{4,0},{5,1},{6,2},{7,3},{8,12},{9,13},{10,... | collective-permute-start | bytes 786440 | tf_op jit(solution)/shard_map/ppermute | solution.py:24
  24.9 8.2 %collective-permute-start.15 = (bf16[256,512]{1,0:T(8,128)(2,1)S(1)}, bf16[256,512]{1,0:T(8,128)(2,1)S(1)}, u32[]{:S(2)}, u32[]{:S(2)}) collective-permute-start(bf16[256,512]{1,0:T(8,128)(2,1)S(1)} %collective-permute-done.10.refs_0_.first_ref), channel_id=1, source_target_pairs={{0,2},{1,3},{2,0},{3,1},{4,6},{5,7},{6,4},{7,5},{8,10},{9,11},{10,... | collective-permute-start | bytes 786440 | tf_op jit(solution)/shard_map/ppermute | solution.py:24
  28.5 4.6 %collective-permute-start.18 = (bf16[256,512]{1,0:T(8,128)(2,1)S(1)}, bf16[256,512]{1,0:T(8,128)(2,1)S(1)}, u32[]{:S(2)}, u32[]{:S(2)}) collective-permute-start(bf16[256,512]{1,0:T(8,128)(2,1)S(1)} %collective-permute-done.11.first_ref), channel_id=1, source_target_pairs={{0,1},{1,0},{2,3},{3,2},{4,5},{5,4},{6,7},{7,6},{8,9},{9,8},{10,11... | collective-permute-start | bytes 786440 | tf_op jit(solution)/shard_map/ppermute | solution.py:24
  29.5 7.0 %collective-permute-start.12 = (bf16[64,512]{1,0:T(8,128)(2,1)S(1)}, bf16[64,512]{1,0:T(8,128)(2,1)S(1)}, u32[]{:S(2)}, u32[]{:S(2)}) collective-permute-start(bf16[64,512]{1,0:T(8,128)(2,1)S(1)} %choose_pieces.3), channel_id=1, source_target_pairs={{0,2},{1,3},{2,0},{3,1},{4,6},{5,7},{6,4},{7,5},{8,10},{9,11},{10,... | collective-permute-start | bytes 196616 | tf_op jit(solution)/shard_map/ppermute | solution.py:24
  31.1 5.4 %collective-permute-start.13 = (bf16[64,512]{1,0:T(8,128)(2,1)S(1)}, bf16[64,512]{1,0:T(8,128)(2,1)S(1)}, u32[]{:S(2)}, u32[]{:S(2)}) collective-permute-start(bf16[64,512]{1,0:T(8,128)(2,1)S(1)} %choose_pieces.3), channel_id=1, source_target_pairs={{0,4},{1,5},{2,6},{3,7},{4,0},{5,1},{6,2},{7,3},{8,12},{9,13},{10,... | collective-permute-start | bytes 196616 | tf_op jit(solution)/shard_map/ppermute | solution.py:24
  31.3 5.3 %collective-permute-start.14 = (bf16[64,512]{1,0:T(8,128)(2,1)S(1)}, bf16[64,512]{1,0:T(8,128)(2,1)S(1)}, u32[]{:S(2)}, u32[]{:S(2)}) collective-permute-start(bf16[64,512]{1,0:T(8,128)(2,1)S(1)} %choose_pieces.3), channel_id=1, source_target_pairs={{0,6},{1,7},{2,4},{3,5},{4,2},{5,3},{6,0},{7,1},{8,14},{9,15},{10,... | collective-permute-start | bytes 196616 | tf_op jit(solution)/shard_map/ppermute | solution.py:24
  33.0 1.5 %collective-permute-start.17 = (bf16[256,512]{1,0:T(8,128)(2,1)S(1)}, bf16[256,512]{1,0:T(8,128)(2,1)S(1)}, u32[]{:S(2)}, u32[]{:S(2)}) collective-permute-start(bf16[256,512]{1,0:T(8,128)(2,1)S(1)} %collective-permute-done.10.refs_0_.first_ref), channel_id=1, source_target_pairs={{0,1},{1,0},{2,3},{3,2},{4,5},{5,4},{6,7},{7,6},{8,9},{9,8},{10,11... | collective-permute-start | bytes 786440 | tf_op jit(solution)/shard_map/ppermute | solution.py:24
  33.0 2.5 %collective-permute-start.16 = (bf16[256,512]{1,0:T(8,128)(2,1)S(1)}, bf16[256,512]{1,0:T(8,128)(2,1)S(1)}, u32[]{:S(2)}, u32[]{:S(2)}) collective-permute-start(bf16[256,512]{1,0:T(8,128)(2,1)S(1)} %collective-permute-done.15.first_ref), channel_id=1, source_target_pairs={{0,1},{1,0},{2,3},{3,2},{4,5},{5,4},{6,7},{7,6},{8,9},{9,8},{10,11... | collective-permute-start | bytes 786440 | tf_op jit(solution)/shard_map/ppermute | solution.py:24
  35.5 1.4 %copy-start.1 = (bf16[512,1536]{1,0:T(8,128)(2,1)S(1)}, bf16[512,1536]{1,0:T(8,128)(2,1)}, u32[]{:S(2)}) copy-start(bf16[512,1536]{1,0:T(8,128)(2,1)} %w_qkv_ref.1) | copy-start | bytes 4718596
  36.7 1.7 %copy-start.2 = (bf16[512,1024]{1,0:T(8,128)(2,1)S(1)}, bf16[512,1024]{1,0:T(8,128)(2,1)}, u32[]{:S(2)}) copy-start(bf16[512,1024]{1,0:T(8,128)(2,1)} %w_up_ref.1) | copy-start | bytes 3145732
  36.7 1.6 %copy-start.3 = (bf16[1024,512]{1,0:T(8,128)(2,1)S(1)}, bf16[1024,512]{1,0:T(8,128)(2,1)}, u32[]{:S(2)}) copy-start(bf16[1024,512]{1,0:T(8,128)(2,1)} %w_down_ref.1) | copy-start | bytes 3145732
  36.7 1.7 %copy-start.4 = (bf16[512,512]{1,0:T(8,128)(2,1)S(1)}, bf16[512,512]{1,0:T(8,128)(2,1)}, u32[]{:S(2)}) copy-start(bf16[512,512]{1,0:T(8,128)(2,1)} %w_out_ref.1) | copy-start | bytes 1572868
  36.8 1.7 %copy-start.6 = (s32[8,8]{1,0:T(8,128)S(1)}, s32[8,8]{1,0:T(8,128)}, u32[]{:S(2)}) copy-start(s32[8,8]{1,0:T(8,128)} %plan_ref.1) | copy-start | bytes 772
  36.8 1.6 %collective-permute-start.19 = (bf16[256,512]{1,0:T(8,128)(2,1)S(1)}, bf16[256,512]{1,0:T(8,128)(2,1)S(1)}, u32[]{:S(2)}, u32[]{:S(2)}) collective-permute-start(bf16[256,512]{1,0:T(8,128)(2,1)S(1)} %constant_dynamic-update-slice_fusion.rows_ref), channel_id=1, source_target_pairs={{0,1},{1,0},{2,3},{3,2},{4,5},{5,4},{6,7},{7,6},{8,9},{9,8},{10,11... | collective-permute-start | bytes 786440 | tf_op jit(solution)/shard_map/ppermute | solution.py:24

commit v6 on v5

--- a/solution.py
+++ b/solution.py
@@ -216,7 +216,7 @@
             index = region * per_group + ((block // local) ^ head_here) * local + block % local
             index = jnp.where(col < hub_base, index, hub_place + col - hub_base)
             places.append(pl.ds(pl.multiple_of(index * TB, TB), TB))
-        edges = jnp.concatenate([mask[r, t].astype(jnp.float32) for t in range(tiles)], axis=1)
+        edges = jnp.concatenate([mask[r, t] for t in range(tiles)], axis=1)
         for g in range(width // group):
             cols = slice(g * group, (g + 1) * group)
             beyond = slice(width + g * group, width + (g + 1) * group)
@@ -350,7 +350,7 @@
     token_core = core(tokens)
     pool, query, again, codes = keyval(None, 0, tokens, token_core, hub_blocks=hub_blocks, whence=whence)
     far = along(paired)
-    edges = lax.dynamic_slice_in_dim(tile_mask, head_here * local, local, 0)
+    edges = lax.dynamic_slice_in_dim(tile_mask, head_here * local, local, 0).astype(jnp.float32)
     paired, strip, pool, query, codes, edges, *sides = lax.optimization_barrier(
         (paired, strip, pool, query, codes, edges, *sides)
     )

time: 43.3 us -> 43.3 us (level)
  local copies, waits for them, and re-layouts: 5.37 us -> 4.05 us
  other arithmetic: 0 us -> 1.31 us
    dynamic_slice x1 -> x0, local copies, waits for them, and re-layouts: 1.32 us -> none  [body(): edges = lax.dynamic_slice_in_dim(tile_mask, head_here * local, local, 0)]
    convert_element_type x0 -> x1, other arithmetic: none -> 1.31 us  [body(): lax.dynamic_slice_in_dim(tile_mask, head_here * local, local, 0)]
where the time goes in v6:
time: 43.3 us; the launch traced here: 43 us
  starting transfers between devices  17.9 us (41%)
  Pallas kernels  11.7 us (27%)
  waiting for transfers between devices  7.75 us (18%)
  local copies, waits for them, and re-layouts  4.05 us (9%)
  other arithmetic  1.31 us (3%)
    ppermute x20, starting transfers between devices, send(): return lax.ppermute(value, AXES, pairs)  17.9 us
    ppermute x20, waiting for transfers between devices, send(): return lax.ppermute(value, AXES, pairs)  7.75 us
    pallas_call x6, Pallas kernels, keyvals(): pl.pallas_call(functools.partial(keyval_kernel, heads, head_dim, at, when...  6.31 us
    pallas_call x1, Pallas kernels, finish(): pl.pallas_call(functools.partial(finish_kernel, heads, head_dim, hub_coun...  4.58 us
    unnamed x19, local copies, waits for them, and re-layouts  3.17 us
    convert_element_type x1, other arithmetic, body(): lax.dynamic_slice_in_dim(tile_mask, head_here * local, local, 0)  1.31 us
    dynamic_slice x1, local copies, waits for them, and re-layouts, body(): lax.dynamic_slice_in_dim(tokens.reshape(local, TB, width), strip_at, 2 *...  0.88 us
  transfers between devices with their start and end apart: 20, of which 7 were waited for; matrix products, arithmetic and copies ran while one was open for 5% of the time, Pallas kernels for 17%

profile of v6, /device:TPU:0, one launch (start us, length us, event | category | flops | bytes accessed | tf_op | source)
XLA Modules:
  0.0 43.0 jit_solution(1932024534290133156)
XLA Ops:
  0.0 0.5 %collective-permute-start = (bf16[256,512]{1,0:T(8,128)(2,1)}, bf16[256,512]{1,0:T(8,128)(2,1)S(1)}, u32[]{:S(2)}, u32[]{:S(2)}) collective-permute-start(bf16[256,512]{1,0:T(8,128)(2,1)} %first_ref.1), channel_id=1, source_target_pairs={{0,1},{1,0},{2,3},{3,2},{4,5},{5,4},{6,7},{7,6},{8,9},{9,8},{10,11... | collective-permute-start | bytes 786440 | tf_op jit(solution)/shard_map/ppermute | solution.py:24
  0.5 2.5 %collective-permute-start.1 = (bf16[256,512]{1,0:T(8,128)(2,1)}, bf16[256,512]{1,0:T(8,128)(2,1)S(1)}, u32[]{:S(2)}, u32[]{:S(2)}) collective-permute-start(bf16[256,512]{1,0:T(8,128)(2,1)} %first_ref.1), channel_id=1, source_target_pairs={{0,4},{1,5},{2,6},{3,7},{4,0},{5,1},{6,2},{7,3},{8,12},{9,13},{10,... | collective-permute-start | bytes 786440 | tf_op jit(solution)/shard_map/ppermute | solution.py:24
  2.9 1.5 %collective-permute-start.3 = (bf16[256,512]{1,0:T(8,128)(2,1)}, bf16[256,512]{1,0:T(8,128)(2,1)S(1)}, u32[]{:S(2)}, u32[]{:S(2)}) collective-permute-start(bf16[256,512]{1,0:T(8,128)(2,1)} %first_ref.1), channel_id=1, source_target_pairs={{0,2},{1,3},{2,0},{3,1},{4,6},{5,7},{6,4},{7,5},{8,10},{9,11},{10,... | collective-permute-start | bytes 786440 | tf_op jit(solution)/shard_map/ppermute | solution.py:24
  4.5 0.9 %constant_dynamic-slice_fusion = bf16[2,32,512]{2,1,0:T(8,128)(2,1)S(1)} fusion(bf16[2,128,512]{2,1,0:T(8,128)(2,1)} %bitcast.2, s32[]{:T(128)S(6)} %select_n.24), kind=kLoop, calls=%fused_computation.5 | loop fusion | bytes 131076 | tf_op jit(solution)/shard_map/dynamic_slice | solution.py:348
  5.3 0.0 collective-permute-start.2
  5.4 1.3 %dynamic-slice_convert_fusion.mask = f32[2,8,128,128]{3,2,1,0:T(8,128)S(1)} fusion(s32[8,8,128,128]{3,2,1,0:T(8,128)} %param.14, s32[]{:T(128)S(6)} %select_n.25), kind=kLoop, calls=%fused_computation | loop fusion | flops 262144 | bytes 2097156 | tf_op jit(solution)/shard_map/convert_element_type | solution.py:353
  6.7 0.0 copy-start
  6.7 1.4 %copy-done = bf16[512,1536]{1,0:T(8,128)(2,1)S(1)} copy-done((bf16[512,1536]{1,0:T(8,128)(2,1)S(1)}, bf16[512,1536]{1,0:T(8,128)(2,1)}, u32[]{:S(2)}) %copy-start) | copy-done | bytes 1572888
  8.1 0.9 %copy-done.5 = bf16[256,512]{1,0:T(8,128)(2,1)S(1)} copy-done((bf16[256,512]{1,0:T(8,128)(2,1)S(1)}, bf16[256,512]{1,0:T(8,128)(2,1)}, u32[]{:S(2)}) %copy-start.5) | copy-done | bytes 262168
  9.1 0.7 %copy-done.7 = s32[4]{0:T(128)S(1)} copy-done((s32[4]{0:T(128)S(1)}, s32[4]{0:T(128)}, u32[]{:S(2)}) %copy-start.7) | copy-done | bytes 40
  9.7 1.7 %keyvals.6 = (bf16[3584,1024]{1,0:T(8,128)(2,1)S(1)}, bf16[256,512]{1,0:T(8,128)(2,1)S(1)}, bf16[256,512]{1,0:T(8,128)(2,1)S(1)}, f32[3,64,128]{2,1,0:T(8,128)S(1)}) custom-call(bf16[256,512]{1,0:T(8,128)(2,1)S(1)} %copy-done.5, bf16[256,512]{1,0:T(8,128)(2,1)S(1)} %collective-permute-done.second_ref, bf16[512,1536]{1,0:T(8,128)(2,1)S(1)} %copy-done, ...), custom_call_target="tpu_custom_call" | custom-call | flops 4294967296 | bytes 1572864 | tf_op jit(solution)/shard_map/keyvals/pallas_call | solution.py:88
  11.5 1.4 %collective-permute-done.2.refs_3_ = bf16[64,512]{1,0:T(8,128)(2,1)S(1)} collective-permute-done((bf16[64,512]{1,0:T(8,128)(2,1)S(1)}, bf16[64,512]{1,0:T(8,128)(2,1)S(1)}, u32[]{:S(2)}, u32[]{:S(2)}) %collective-permute-start.2) | collective-permute-done | bytes 65568 | tf_op jit(solution)/shard_map/ppermute | solution.py:24
  12.8 0.0 collective-permute-done.1.refs_2_.first_ref
  12.9 0.1 collective-permute-done.3.refs_1_.first_ref
  13.0 0.0 collective-permute-start.5
  13.0 0.5 %collective-permute-start.6 = (bf16[256,512]{1,0:T(8,128)(2,1)S(1)}, bf16[256,512]{1,0:T(8,128)(2,1)S(1)}, u32[]{:S(2)}, u32[]{:S(2)}) collective-permute-start(bf16[256,512]{1,0:T(8,128)(2,1)S(1)} %collective-permute-done.3.refs_1_.first_ref), channel_id=1, source_target_pairs={{0,1},{1,0},{2,3},{3,2},{4,5},{5,4},{6,7},{7,6},{8,9},{9,8},{10,11... | collective-permute-start | bytes 786440 | tf_op jit(solution)/shard_map/ppermute | solution.py:24
  13.5 0.1 pick_pieces.1
  13.6 0.1 collective-permute-start.4
  13.7 1.6 %collective-permute-start.10 = (bf16[256,512]{1,0:T(8,128)(2,1)S(1)}, bf16[256,512]{1,0:T(8,128)(2,1)S(1)}, u32[]{:S(2)}, u32[]{:S(2)}) collective-permute-start(bf16[256,512]{1,0:T(8,128)(2,1)S(1)} %collective-permute-done.1.refs_2_.first_ref), channel_id=1, source_target_pairs={{0,8},{1,9},{2,10},{3,11},{4,28},{5,29},{6,30},{7,31},{8,16},{9,17... | collective-permute-start | bytes 786440 | tf_op jit(solution)/shard_map/ppermute | solution.py:24
  15.4 1.6 %collective-permute-start.7 = (bf16[64,512]{1,0:T(8,128)(2,1)S(1)}, bf16[64,512]{1,0:T(8,128)(2,1)S(1)}, u32[]{:S(2)}, u32[]{:S(2)}) collective-permute-start(bf16[64,512]{1,0:T(8,128)(2,1)S(1)} %choose_pieces.2.refs_0_), channel_id=1, source_target_pairs={{0,8},{1,9},{2,10},{3,11},{4,28},{5,29},{6,30},{7,31},{8,16},{9,17... | collective-permute-start | bytes 196616 | tf_op jit(solution)/shard_map/ppermute | solution.py:24
  17.0 2.2 %collective-permute-start.8 = (bf16[64,512]{1,0:T(8,128)(2,1)S(1)}, bf16[64,512]{1,0:T(8,128)(2,1)S(1)}, u32[]{:S(2)}, u32[]{:S(2)}) collective-permute-start(bf16[64,512]{1,0:T(8,128)(2,1)S(1)} %choose_pieces.2.refs_0_), channel_id=1, source_target_pairs={{0,16},{1,17},{2,18},{3,19},{4,20},{5,21},{6,22},{7,23},{8,24},{9,... | collective-permute-start | bytes 196616 | tf_op jit(solution)/shard_map/ppermute | solution.py:24
  19.3 1.7 %collective-permute-start.9 = (bf16[64,512]{1,0:T(8,128)(2,1)S(1)}, bf16[64,512]{1,0:T(8,128)(2,1)S(1)}, u32[]{:S(2)}, u32[]{:S(2)}) collective-permute-start(bf16[64,512]{1,0:T(8,128)(2,1)S(1)} %choose_pieces.2.refs_0_), channel_id=1, source_target_pairs={{0,24},{1,25},{2,26},{3,27},{4,12},{5,13},{6,14},{7,15},{8,0},{9,1... | collective-permute-start | bytes 196616 | tf_op jit(solution)/shard_map/ppermute | solution.py:24
  20.9 0.0 collective-permute-start.11
  20.9 0.9 %keyvals.7.refs_1_ = bf16[3584,1024]{1,0:T(8,128)(2,1)S(1)} custom-call(bf16[256,512]{1,0:T(8,128)(2,1)S(1)} %collective-permute-done.1.refs_2_.first_ref, bf16[256,512]{1,0:T(8,128)(2,1)S(1)} %collective-permute-done.5.second_ref, bf16[512,1536]{1,0:T(8,128)(2,1)S(1)} %copy-done, ...), custom_call_target="tpu_custom_call", output_to_operand_aliasing={{}: (4, {})} | custom-call | flops 4294967296 | bytes 1572864 | tf_op jit(solution)/shard_map/keyvals/pallas_call | solution.py:88
  21.9 3.0 %collective-permute-done.10.refs_0_.first_ref = bf16[256,512]{1,0:T(8,128)(2,1)S(1)} collective-permute-done((bf16[256,512]{1,0:T(8,128)(2,1)S(1)}, bf16[256,512]{1,0:T(8,128)(2,1)S(1)}, u32[]{:S(2)}, u32[]{:S(2)}) %collective-permute-start.10) | collective-permute-done | bytes 262176 | tf_op jit(solution)/shard_map/ppermute | solution.py:24
  24.9 1.5 %collective-permute-start.15 = (bf16[256,512]{1,0:T(8,128)(2,1)S(1)}, bf16[256,512]{1,0:T(8,128)(2,1)S(1)}, u32[]{:S(2)}, u32[]{:S(2)}) collective-permute-start(bf16[256,512]{1,0:T(8,128)(2,1)S(1)} %collective-permute-done.10.refs_0_.first_ref), channel_id=1, source_target_pairs={{0,2},{1,3},{2,0},{3,1},{4,6},{5,7},{6,4},{7,5},{8,10},{9,11},{10,... | collective-permute-start | bytes 786440 | tf_op jit(solution)/shard_map/ppermute | solution.py:24
  26.4 2.1 %collective-permute-done.11.first_ref = bf16[256,512]{1,0:T(8,128)(2,1)S(1)} collective-permute-done((bf16[256,512]{1,0:T(8,128)(2,1)S(1)}, bf16[256,512]{1,0:T(8,128)(2,1)S(1)}, u32[]{:S(2)}, u32[]{:S(2)}) %collective-permute-start.11) | collective-permute-done | bytes 262176 | tf_op jit(solution)/shard_map/ppermute | solution.py:24
  28.5 0.9 %keyvals.8.refs_0_ = bf16[3584,1024]{1,0:T(8,128)(2,1)S(1)} custom-call(bf16[256,512]{1,0:T(8,128)(2,1)S(1)} %collective-permute-done.3.refs_1_.first_ref, bf16[256,512]{1,0:T(8,128)(2,1)S(1)} %collective-permute-done.6.second_ref, bf16[512,1536]{1,0:T(8,128)(2,1)S(1)} %copy-done, ...), custom_call_target="tpu_custom_call", output_to_operand_aliasing={{}: (4, {})} | custom-call | flops 4294967296 | bytes 1572864 | tf_op jit(solution)/shard_map/keyvals/pallas_call | solution.py:88
  29.5 1.6 %collective-permute-start.12 = (bf16[64,512]{1,0:T(8,128)(2,1)S(1)}, bf16[64,512]{1,0:T(8,128)(2,1)S(1)}, u32[]{:S(2)}, u32[]{:S(2)}) collective-permute-start(bf16[64,512]{1,0:T(8,128)(2,1)S(1)} %choose_pieces.3), channel_id=1, source_target_pairs={{0,2},{1,3},{2,0},{3,1},{4,6},{5,7},{6,4},{7,5},{8,10},{9,11},{10,... | collective-permute-start | bytes 196616 | tf_op jit(solution)/shard_map/ppermute | solution.py:24
  31.1 0.3 collective-permute-start.13
  31.3 1.7 %collective-permute-start.14 = (bf16[64,512]{1,0:T(8,128)(2,1)S(1)}, bf16[64,512]{1,0:T(8,128)(2,1)S(1)}, u32[]{:S(2)}, u32[]{:S(2)}) collective-permute-start(bf16[64,512]{1,0:T(8,128)(2,1)S(1)} %choose_pieces.3), channel_id=1, source_target_pairs={{0,6},{1,7},{2,4},{3,5},{4,2},{5,3},{6,0},{7,1},{8,14},{9,15},{10,... | collective-permute-start | bytes 196616 | tf_op jit(solution)/shard_map/ppermute | solution.py:24
  33.0 0.5 %collective-permute-start.16 = (bf16[256,512]{1,0:T(8,128)(2,1)S(1)}, bf16[256,512]{1,0:T(8,128)(2,1)S(1)}, u32[]{:S(2)}, u32[]{:S(2)}) collective-permute-start(bf16[256,512]{1,0:T(8,128)(2,1)S(1)} %collective-permute-done.15.first_ref), channel_id=1, source_target_pairs={{0,1},{1,0},{2,3},{3,2},{4,5},{5,4},{6,7},{7,6},{8,9},{9,8},{10,11... | collective-permute-start | bytes 786440 | tf_op jit(solution)/shard_map/ppermute | solution.py:24
  33.6 0.9 %keyvals.9.refs_0_ = bf16[3584,1024]{1,0:T(8,128)(2,1)S(1)} custom-call(bf16[256,512]{1,0:T(8,128)(2,1)S(1)} %collective-permute-done.11.first_ref, bf16[256,512]{1,0:T(8,128)(2,1)S(1)} %collective-permute-done.18.second_ref, bf16[512,1536]{1,0:T(8,128)(2,1)S(1)} %copy-done, bf16[3584,1024]{1,0:T(8,128)(2,1)S(1)} %keyvals.8.refs_0_), custom_call_target="tpu_custom_call", output_to_operand_aliasing={{}: (3, {})} | custom-call | flops 4294967296 | bytes 1572864 | tf_op jit(solution)/shard_map/keyvals/pallas_call | solution.py:88
  34.5 0.1 collective-permute-done.17.second_ref
  34.6 0.9 %keyvals.10.refs_0_ = bf16[3584,1024]{1,0:T(8,128)(2,1)S(1)} custom-call(bf16[256,512]{1,0:T(8,128)(2,1)S(1)} %collective-permute-done.10.refs_0_.first_ref, bf16[256,512]{1,0:T(8,128)(2,1)S(1)} %collective-permute-done.17.second_ref, bf16[512,1536]{1,0:T(8,128)(2,1)S(1)} %copy-done, ...), custom_call_target="tpu_custom_call", output_to_operand_aliasing={{}: (3, {})} | custom-call | flops 4294967296 | bytes 1572864 | tf_op jit(solution)/shard_map/keyvals/pallas_call | solution.py:88
  35.5 0.0 copy-start.1
  35.5 0.9 %keyvals.11._ = bf16[3584,1024]{1,0:T(8,128)(2,1)S(1)} custom-call(bf16[256,512]{1,0:T(8,128)(2,1)S(1)} %collective-permute-done.15.first_ref, bf16[256,512]{1,0:T(8,128)(2,1)S(1)} %collective-permute-done.16.second_ref, bf16[512,1536]{1,0:T(8,128)(2,1)S(1)} %copy-done, bf16[3584,1024]{1,0:T(8,128)(2,1)S(1)} %keyvals.10.refs_0_), custom_call_target="tpu_custom_call", output_to_operand_aliasing={{}: (3, {})} | custom-call | flops 4294967296 | bytes 1572864 | tf_op jit(solution)/shard_map/keyvals/pallas_call | solution.py:88
  36.5 0.2 collective-permute-done.14
  36.7 0.0 copy-start.2
  36.7 0.0 copy-start.3
  36.7 0.0 copy-start.4
  36.8 0.0 copy-start.6
  36.8 0.1 collective-permute-start.19
  36.8 0.1 copy-done.1
  36.9 0.7 %hub_half.1.refs_1_ = bf16[3584,1024]{1,0:T(8,128)(2,1)S(1)} custom-call(bf16[256,512]{1,0:T(8,128)(2,1)S(1)} %constant_dynamic-update-slice_fusion.rows_ref, bf16[512,1536]{1,0:T(8,128)(2,1)S(1)} %copy-done.1, bf16[3584,1024]{1,0:T(8,128)(2,1)S(1)} %keyvals.11._), custom_call_target="tpu_custom_call", output_to_operand_aliasing={{}: (2, {})} | custom-call | tf_op jit(solution)/shard_map/hub_half/pallas_call | solution.py:182
  37.6 0.8 %collective-permute-done.19.refs_0_ = bf16[256,512]{1,0:T(8,128)(2,1)S(1)} collective-permute-done((bf16[256,512]{1,0:T(8,128)(2,1)S(1)}, bf16[256,512]{1,0:T(8,128)(2,1)S(1)}, u32[]{:S(2)}, u32[]{:S(2)}) %collective-permute-start.19) | collective-permute-done | bytes 262176 | tf_op jit(solution)/shard_map/ppermute | solution.py:24
  38.4 0.1 copy-done.4
  38.4 4.6 %finish.1 = (bf16[256,512]{1,0:T(8,128)(2,1)}, bf16[3584,1024]{1,0:T(8,128)(2,1)S(1)}) custom-call(s32[8,8]{1,0:T(8,128)S(1)} %copy-done.6, bf16[256,512]{1,0:T(8,128)(2,1)S(1)} %get-tuple-element.37.refs_0_.tokens_ref, bf16[256,512]{1,0:T(8,128)(2,1)S(1)} %get-tuple-element.41.query_ref, ...), custom_call_target="tpu_custom_call", output_to_operand_aliasing={{1}: (9, {})} | custom-call | tf_op jit(solution)/shard_map/finish/pallas_call | solution.py:257
  (25 shorter events, 0.1 us)
Async XLA Ops:
  0.0 6.7 %collective-permute-start = (bf16[256,512]{1,0:T(8,128)(2,1)}, bf16[256,512]{1,0:T(8,128)(2,1)S(1)}, u32[]{:S(2)}, u32[]{:S(2)}) collective-permute-start(bf16[256,512]{1,0:T(8,128)(2,1)} %first_ref.1), channel_id=1, source_target_pairs={{0,1},{1,0},{2,3},{3,2},{4,5},{5,4},{6,7},{7,6},{8,9},{9,8},{10,11... | collective-permute-start | bytes 786440 | tf_op jit(solution)/shard_map/ppermute | solution.py:24
  0.5 12.4 %collective-permute-start.1 = (bf16[256,512]{1,0:T(8,128)(2,1)}, bf16[256,512]{1,0:T(8,128)(2,1)S(1)}, u32[]{:S(2)}, u32[]{:S(2)}) collective-permute-start(bf16[256,512]{1,0:T(8,128)(2,1)} %first_ref.1), channel_id=1, source_target_pairs={{0,4},{1,5},{2,6},{3,7},{4,0},{5,1},{6,2},{7,3},{8,12},{9,13},{10,... | collective-permute-start | bytes 786440 | tf_op jit(solution)/shard_map/ppermute | solution.py:24
  2.9 10.1 %collective-permute-start.3 = (bf16[256,512]{1,0:T(8,128)(2,1)}, bf16[256,512]{1,0:T(8,128)(2,1)S(1)}, u32[]{:S(2)}, u32[]{:S(2)}) collective-permute-start(bf16[256,512]{1,0:T(8,128)(2,1)} %first_ref.1), channel_id=1, source_target_pairs={{0,2},{1,3},{2,0},{3,1},{4,6},{5,7},{6,4},{7,5},{8,10},{9,11},{10,... | collective-permute-start | bytes 786440 | tf_op jit(solution)/shard_map/ppermute | solution.py:24
  5.3 7.5 %collective-permute-start.2 = (bf16[64,512]{1,0:T(8,128)(2,1)S(1)}, bf16[64,512]{1,0:T(8,128)(2,1)S(1)}, u32[]{:S(2)}, u32[]{:S(2)}) collective-permute-start(bf16[64,512]{1,0:T(8,128)(2,1)S(1)} %bitcast.3), channel_id=1, source_target_pairs={{0,6},{1,7},{2,4},{3,5},{4,2},{5,3},{6,0},{7,1},{8,14},{9,15},{10,... | collective-permute-start | bytes 196616 | tf_op jit(solution)/shard_map/ppermute | solution.py:24
  6.7 1.4 %copy-start = (bf16[512,1536]{1,0:T(8,128)(2,1)S(1)}, bf16[512,1536]{1,0:T(8,128)(2,1)}, u32[]{:S(2)}) copy-start(bf16[512,1536]{1,0:T(8,128)(2,1)} %w_qkv_ref.1) | copy-start | bytes 4718596
  8.1 0.9 %copy-start.5 = (bf16[256,512]{1,0:T(8,128)(2,1)S(1)}, bf16[256,512]{1,0:T(8,128)(2,1)}, u32[]{:S(2)}) copy-start(bf16[256,512]{1,0:T(8,128)(2,1)} %first_ref.1) | copy-start | bytes 786436
  9.1 0.7 %copy-start.7 = (s32[4]{0:T(128)S(1)}, s32[4]{0:T(128)}, u32[]{:S(2)}) copy-start(s32[4]{0:T(128)} %refs_0_.1) | copy-start | bytes 52
  13.0 2.3 %collective-permute-start.5 = (bf16[256,512]{1,0:T(8,128)(2,1)S(1)}, bf16[256,512]{1,0:T(8,128)(2,1)S(1)}, u32[]{:S(2)}, u32[]{:S(2)}) collective-permute-start(bf16[256,512]{1,0:T(8,128)(2,1)S(1)} %collective-permute-done.1.refs_2_.first_ref), channel_id=1, source_target_pairs={{0,1},{1,0},{2,3},{3,2},{4,5},{5,4},{6,7},{7,6},{8,9},{9,8},{10,11... | collective-permute-start | bytes 786440 | tf_op jit(solution)/shard_map/ppermute | solution.py:24
  13.0 2.3 %collective-permute-start.6 = (bf16[256,512]{1,0:T(8,128)(2,1)S(1)}, bf16[256,512]{1,0:T(8,128)(2,1)S(1)}, u32[]{:S(2)}, u32[]{:S(2)}) collective-permute-start(bf16[256,512]{1,0:T(8,128)(2,1)S(1)} %collective-permute-done.3.refs_1_.first_ref), channel_id=1, source_target_pairs={{0,1},{1,0},{2,3},{3,2},{4,5},{5,4},{6,7},{7,6},{8,9},{9,8},{10,11... | collective-permute-start | bytes 786440 | tf_op jit(solution)/shard_map/ppermute | solution.py:24
  13.6 1.7 %collective-permute-start.4 = (bf16[64,512]{1,0:T(8,128)(2,1)S(1)}, bf16[64,512]{1,0:T(8,128)(2,1)S(1)}, u32[]{:S(2)}, u32[]{:S(2)}) collective-permute-start(bf16[64,512]{1,0:T(8,128)(2,1)S(1)} %get-tuple-element.48), channel_id=1, source_target_pairs={{0,1},{1,0},{2,3},{3,2},{4,5},{5,4},{6,7},{7,6},{8,9},{9,8},{10,11... | collective-permute-start | bytes 196616 | tf_op jit(solution)/shard_map/ppermute | solution.py:24
  13.7 11.1 %collective-permute-start.10 = (bf16[256,512]{1,0:T(8,128)(2,1)S(1)}, bf16[256,512]{1,0:T(8,128)(2,1)S(1)}, u32[]{:S(2)}, u32[]{:S(2)}) collective-permute-start(bf16[256,512]{1,0:T(8,128)(2,1)S(1)} %collective-permute-done.1.refs_2_.first_ref), channel_id=1, source_target_pairs={{0,8},{1,9},{2,10},{3,11},{4,28},{5,29},{6,30},{7,31},{8,16},{9,17... | collective-permute-start | bytes 786440 | tf_op jit(solution)/shard_map/ppermute | solution.py:24
  15.4 14.0 %collective-permute-start.7 = (bf16[64,512]{1,0:T(8,128)(2,1)S(1)}, bf16[64,512]{1,0:T(8,128)(2,1)S(1)}, u32[]{:S(2)}, u32[]{:S(2)}) collective-permute-start(bf16[64,512]{1,0:T(8,128)(2,1)S(1)} %choose_pieces.2.refs_0_), channel_id=1, source_target_pairs={{0,8},{1,9},{2,10},{3,11},{4,28},{5,29},{6,30},{7,31},{8,16},{9,17... | collective-permute-start | bytes 196616 | tf_op jit(solution)/shard_map/ppermute | solution.py:24
  17.0 12.4 %collective-permute-start.8 = (bf16[64,512]{1,0:T(8,128)(2,1)S(1)}, bf16[64,512]{1,0:T(8,128)(2,1)S(1)}, u32[]{:S(2)}, u32[]{:S(2)}) collective-permute-start(bf16[64,512]{1,0:T(8,128)(2,1)S(1)} %choose_pieces.2.refs_0_), channel_id=1, source_target_pairs={{0,16},{1,17},{2,18},{3,19},{4,20},{5,21},{6,22},{7,23},{8,24},{9,... | collective-permute-start | bytes 196616 | tf_op jit(solution)/shard_map/ppermute | solution.py:24
  19.3 10.2 %collective-permute-start.9 = (bf16[64,512]{1,0:T(8,128)(2,1)S(1)}, bf16[64,512]{1,0:T(8,128)(2,1)S(1)}, u32[]{:S(2)}, u32[]{:S(2)}) collective-permute-start(bf16[64,512]{1,0:T(8,128)(2,1)S(1)} %choose_pieces.2.refs_0_), channel_id=1, source_target_pairs={{0,24},{1,25},{2,26},{3,27},{4,12},{5,13},{6,14},{7,15},{8,0},{9,1... | collective-permute-start | bytes 196616 | tf_op jit(solution)/shard_map/ppermute | solution.py:24
  20.9 7.5 %collective-permute-start.11 = (bf16[256,512]{1,0:T(8,128)(2,1)S(1)}, bf16[256,512]{1,0:T(8,128)(2,1)S(1)}, u32[]{:S(2)}, u32[]{:S(2)}) collective-permute-start(bf16[256,512]{1,0:T(8,128)(2,1)S(1)} %collective-permute-done.3.refs_1_.first_ref), channel_id=1, source_target_pairs={{0,4},{1,5},{2,6},{3,7},{4,0},{5,1},{6,2},{7,3},{8,12},{9,13},{10,... | collective-permute-start | bytes 786440 | tf_op jit(solution)/shard_map/ppermute | solution.py:24
  24.9 8.2 %collective-permute-start.15 = (bf16[256,512]{1,0:T(8,128)(2,1)S(1)}, bf16[256,512]{1,0:T(8,128)(2,1)S(1)}, u32[]{:S(2)}, u32[]{:S(2)}) collective-permute-start(bf16[256,512]{1,0:T(8,128)(2,1)S(1)} %collective-permute-done.10.refs_0_.first_ref), channel_id=1, source_target_pairs={{0,2},{1,3},{2,0},{3,1},{4,6},{5,7},{6,4},{7,5},{8,10},{9,11},{10,... | collective-permute-start | bytes 786440 | tf_op jit(solution)/shard_map/ppermute | solution.py:24
  28.5 4.6 %collective-permute-start.18 = (bf16[256,512]{1,0:T(8,128)(2,1)S(1)}, bf16[256,512]{1,0:T(8,128)(2,1)S(1)}, u32[]{:S(2)}, u32[]{:S(2)}) collective-permute-start(bf16[256,512]{1,0:T(8,128)(2,1)S(1)} %collective-permute-done.11.first_ref), channel_id=1, source_target_pairs={{0,1},{1,0},{2,3},{3,2},{4,5},{5,4},{6,7},{7,6},{8,9},{9,8},{10,11... | collective-permute-start | bytes 786440 | tf_op jit(solution)/shard_map/ppermute | solution.py:24
  29.5 7.0 %collective-permute-start.12 = (bf16[64,512]{1,0:T(8,128)(2,1)S(1)}, bf16[64,512]{1,0:T(8,128)(2,1)S(1)}, u32[]{:S(2)}, u32[]{:S(2)}) collective-permute-start(bf16[64,512]{1,0:T(8,128)(2,1)S(1)} %choose_pieces.3), channel_id=1, source_target_pairs={{0,2},{1,3},{2,0},{3,1},{4,6},{5,7},{6,4},{7,5},{8,10},{9,11},{10,... | collective-permute-start | bytes 196616 | tf_op jit(solution)/shard_map/ppermute | solution.py:24
  31.1 5.4 %collective-permute-start.13 = (bf16[64,512]{1,0:T(8,128)(2,1)S(1)}, bf16[64,512]{1,0:T(8,128)(2,1)S(1)}, u32[]{:S(2)}, u32[]{:S(2)}) collective-permute-start(bf16[64,512]{1,0:T(8,128)(2,1)S(1)} %choose_pieces.3), channel_id=1, source_target_pairs={{0,4},{1,5},{2,6},{3,7},{4,0},{5,1},{6,2},{7,3},{8,12},{9,13},{10,... | collective-permute-start | bytes 196616 | tf_op jit(solution)/shard_map/ppermute | solution.py:24
  31.3 5.3 %collective-permute-start.14 = (bf16[64,512]{1,0:T(8,128)(2,1)S(1)}, bf16[64,512]{1,0:T(8,128)(2,1)S(1)}, u32[]{:S(2)}, u32[]{:S(2)}) collective-permute-start(bf16[64,512]{1,0:T(8,128)(2,1)S(1)} %choose_pieces.3), channel_id=1, source_target_pairs={{0,6},{1,7},{2,4},{3,5},{4,2},{5,3},{6,0},{7,1},{8,14},{9,15},{10,... | collective-permute-start | bytes 196616 | tf_op jit(solution)/shard_map/ppermute | solution.py:24
  33.0 1.5 %collective-permute-start.17 = (bf16[256,512]{1,0:T(8,128)(2,1)S(1)}, bf16[256,512]{1,0:T(8,128)(2,1)S(1)}, u32[]{:S(2)}, u32[]{:S(2)}) collective-permute-start(bf16[256,512]{1,0:T(8,128)(2,1)S(1)} %collective-permute-done.10.refs_0_.first_ref), channel_id=1, source_target_pairs={{0,1},{1,0},{2,3},{3,2},{4,5},{5,4},{6,7},{7,6},{8,9},{9,8},{10,11... | collective-permute-start | bytes 786440 | tf_op jit(solution)/shard_map/ppermute | solution.py:24
  33.0 2.5 %collective-permute-start.16 = (bf16[256,512]{1,0:T(8,128)(2,1)S(1)}, bf16[256,512]{1,0:T(8,128)(2,1)S(1)}, u32[]{:S(2)}, u32[]{:S(2)}) collective-permute-start(bf16[256,512]{1,0:T(8,128)(2,1)S(1)} %collective-permute-done.15.first_ref), channel_id=1, source_target_pairs={{0,1},{1,0},{2,3},{3,2},{4,5},{5,4},{6,7},{7,6},{8,9},{9,8},{10,11... | collective-permute-start | bytes 786440 | tf_op jit(solution)/shard_map/ppermute | solution.py:24
  35.5 1.4 %copy-start.1 = (bf16[512,1536]{1,0:T(8,128)(2,1)S(1)}, bf16[512,1536]{1,0:T(8,128)(2,1)}, u32[]{:S(2)}) copy-start(bf16[512,1536]{1,0:T(8,128)(2,1)} %w_qkv_ref.1) | copy-start | bytes 4718596
  36.7 1.7 %copy-start.2 = (bf16[512,1024]{1,0:T(8,128)(2,1)S(1)}, bf16[512,1024]{1,0:T(8,128)(2,1)}, u32[]{:S(2)}) copy-start(bf16[512,1024]{1,0:T(8,128)(2,1)} %w_up_ref.1) | copy-start | bytes 3145732
  36.7 1.6 %copy-start.3 = (bf16[1024,512]{1,0:T(8,128)(2,1)S(1)}, bf16[1024,512]{1,0:T(8,128)(2,1)}, u32[]{:S(2)}) copy-start(bf16[1024,512]{1,0:T(8,128)(2,1)} %w_down_ref.1) | copy-start | bytes 3145732
  36.7 1.7 %copy-start.4 = (bf16[512,512]{1,0:T(8,128)(2,1)S(1)}, bf16[512,512]{1,0:T(8,128)(2,1)}, u32[]{:S(2)}) copy-start(bf16[512,512]{1,0:T(8,128)(2,1)} %w_out_ref.1) | copy-start | bytes 1572868
  36.8 1.7 %copy-start.6 = (s32[8,8]{1,0:T(8,128)S(1)}, s32[8,8]{1,0:T(8,128)}, u32[]{:S(2)}) copy-start(s32[8,8]{1,0:T(8,128)} %plan_ref.1) | copy-start | bytes 772
  36.8 1.6 %collective-permute-start.19 = (bf16[256,512]{1,0:T(8,128)(2,1)S(1)}, bf16[256,512]{1,0:T(8,128)(2,1)S(1)}, u32[]{:S(2)}, u32[]{:S(2)}) collective-permute-start(bf16[256,512]{1,0:T(8,128)(2,1)S(1)} %constant_dynamic-update-slice_fusion.rows_ref), channel_id=1, source_target_pairs={{0,1},{1,0},{2,3},{3,2},{4,5},{5,4},{6,7},{7,6},{8,9},{9,8},{10,11... | collective-permute-start | bytes 786440 | tf_op jit(solution)/shard_map/ppermute | solution.py:24
